TPU v7x, 32 devices: a whole 2x2x4 slice. The times are simulated.
32 devices in a mesh: bulk: 4 (over x, core), valve: 8 (over z, y).
Axes of the slice: x: 2, y: 2, z: 4, core: 2. Of those that a mesh axis runs over, the one named last changes fastest.
Arguments:
- bg_adjoint: float32 [5, 32, 256, 128], P(None, 'bulk', 'valve'), may hold values from -6 to 6
- bg_velocity: float32 [3, 32, 256, 128], P(None, 'bulk', 'valve'), may hold values from -6 to 6
- bg_source: float32 [5, 32, 256, 128], P(None, 'bulk', 'valve'), may hold values from -6 to 6
- bg_iblank: int32 [32, 256, 128], P('bulk', 'valve'), may hold values 0 or 1
- valve_adjoint: float32 [5, 64, 128, 128], P(None, 'valve', 'bulk'), may hold values from -6 to 6
- valve_velocity: float32 [3, 64, 128, 128], P(None, 'valve', 'bulk'), may hold values from -6 to 6
- valve_source: float32 [5, 64, 128, 128], P(None, 'valve', 'bulk'), may hold values from -6 to 6
- flux_mix: float32 [3, 5, 5], replicated, may hold values from -2.5 to 2.5
- rec_cell: int32 [32, 32, 128], P(('bulk', 'valve')), may hold values from 0 to 32767
- donor_base: int32 [32, 32, 128], P(('bulk', 'valve')), may hold values from 0 to 28542, as said below
- donor_weight: float32 [8, 32, 32, 128], P(None, ('bulk', 'valve')), may hold values from 0 to 1, as said below
- slot_count: int32 [32, 32], P(('bulk', 'valve')), may hold values from 0 to 128, as said below
Outputs:
- bg_out: float32 [5, 32, 256, 128], P(None, 'bulk', 'valve')
- valve_out: float32 [5, 64, 128, 128], P(None, 'valve', 'bulk')
Inputs may be any that keep to these rules, and one draw needn't show every extreme that they name: donor_base is a cell of the block whose neighbours at +1 along each of the three dimensions, alone and together, are in the same block; both ends of the range occur in every draw. `donor_weight`: the eight weights of a slot are non-negative and sum to one. `slot_count`: some owner takes 128 live slots from every sender.
All inputs are finite; a program needn't handle non-finite values. No bound on the sum of `bg_iblank` on one device may be relied on, other than what follows from the above.
Results may differ from a plain program's by a relative error of at most 0.0001.
Values sent between devices are 32-bit elements; how exact they have to be, the bound alone decides.
No kernel may reach another device: no remote copies, remote signals or barrier semaphores. Data moves between devices by JAX's collectives and lax.ppermute only.
A program may use at most 128 MiB of HBM per device.

v0:
```python
import functools

import jax
import jax.numpy as jnp
from jax import lax
from jax.experimental import pallas as pl
from jax.experimental.pallas import tpu as pltpu
from jax.sharding import PartitionSpec as P

NVAR = 5
ITERS = 4
CAP = 128
BX = 8
BY = 32
BZ = 128
PLANES = BX * BY
FACE = BY + BX
SEND_ROWS = 16
VMEM_LIMIT = 48 * 1024 * 1024

VMEM = pl.BlockSpec(memory_space=pltpu.VMEM)
SMEM = pl.BlockSpec(memory_space=pltpu.SMEM)


def params():
    return pltpu.CompilerParams(vmem_limit_bytes=VMEM_LIMIT)


def f32(*shape):
    return jax.ShapeDtypeStruct(shape, jnp.float32)


def swap_pairs(count, odd):
    return {i: (i + 1 if i % 2 == odd else i - 1) % count for i in range(count)}


def face_plans(bulk, valve):
    number = lambda b, v: b * valve + v
    plans = []
    for odd in (0, 1):
        swap = swap_pairs(bulk, odd)
        plans.append([(number(b, v), number(swap[b], v)) for b in range(bulk) for v in range(valve)])
    for odd in (0, 1):
        swap = swap_pairs(valve, odd)
        pairs = []
        for b in range(bulk):
            for v in range(valve):
                end = odd and v in (0, valve - 1)
                pairs.append((number(b, v), number(b ^ 1, v) if end else number(b, swap[v])))
        plans.append(pairs)
    return plans


def exchange(faces, plans):
    return [lax.ppermute(face, ("bulk", "valve"), plan) for face, plan in zip(faces, plans)]


def write_faces(info, bg, va, sends):
    for axis in range(2):
        flip = info[axis] % 2
        planes, rows = (bg, va) if axis == 0 else (va, bg)
        for swap in range(2):
            send = sends[2 * axis + swap]
            high = (flip == 0) if swap == 0 else (flip == 1)
            x_at = jnp.where(high, BX - 1, 0)
            for c in range(NVAR):
                send[c, 0:BY, :] = planes[c, x_at]
                for x in range(BX):
                    send[c, BY + x : BY + x + 1, :] = jnp.where(
                        high, rows[c, x, BY - 1 : BY, :], rows[c, x, 0:1, :]
                    )


def fill_padded(info, grid, axis_x, faces, padded):
    axis_y = 1 - axis_x
    for c in range(NVAR):
        for x in range(BX):
            padded[c, x + 1, 8 : 8 + BY, :] = grid[c, x]
    for axis in range(2):
        even, odd = faces[2 * axis], faces[2 * axis + 1]
        flip = info[axis] % 2
        not_first = info[axis] > 0
        not_last = info[axis] < info[2 + axis] - 1
        rows = slice(0, BY) if axis == axis_x else slice(BY, FACE)
        for c in range(NVAR):
            first, second = even[c, rows, :], odd[c, rows, :]
            low = jnp.where(jnp.logical_and(not_first, flip == 0), second, jnp.where(not_first, first, 0.0))
            high = jnp.where(jnp.logical_and(not_last, flip == 0), first, jnp.where(not_last, second, 0.0))
            if axis == axis_x:
                padded[c, 0, 8 : 8 + BY, :] = low
                padded[c, BX + 1, 8 : 8 + BY, :] = high
            else:
                for x in range(BX):
                    padded[c, x + 1, 7:8, :] = low[x : x + 1, :]
                    padded[c, x + 1, 8 + BY : 9 + BY, :] = high[x : x + 1, :]


def sweep(flux, padded, velocity, source, blanking, out):
    rows = 16
    depth = lax.broadcasted_iota(jnp.int32, (rows, BZ), 1)
    first, last = depth == 0, depth == BZ - 1

    def plane(x, carry):
        for part in range(BY // rows):
            y = part * rows
            here = slice(y, y + rows)
            vel = [velocity[d, x, here, :] for d in range(3)]
            speed = 1.0 + (vel[0] * vel[0] + vel[1] * vel[1] + vel[2] * vel[2])
            half = 0.5 * lax.rsqrt(speed)
            acc = [source[i, x, here, :] for i in range(NVAR)]
            for d in range(3):
                slope = half * vel[d]
                mixed = []
                for j in range(NVAR):
                    if d == 0:
                        low = padded[j, x, y + 8 : y + 8 + rows, :]
                        high = padded[j, x + 2, y + 8 : y + 8 + rows, :]
                    elif d == 1:
                        low = padded[j, x + 1, y + 7 : y + 7 + rows, :]
                        high = padded[j, x + 1, y + 9 : y + 9 + rows, :]
                    else:
                        mid = padded[j, x + 1, y + 8 : y + 8 + rows, :]
                        low = jnp.where(first, 0.0, pltpu.roll(mid, 1, 1))
                        high = jnp.where(last, 0.0, pltpu.roll(mid, BZ - 1, 1))
                    acc[j] = acc[j] + (low + high)
                    mixed.append(slope * (high - low))
                for i in range(NVAR):
                    for j in range(NVAR):
                        acc[i] = acc[i] + flux[d, j, i] * mixed[j]
            scale = 1.0 / 12.0
            if blanking is not None:
                scale = blanking[x, here, :].astype(jnp.float32) * scale
            for i in range(NVAR):
                out[i, x, here, :] = scale * acc[i]
        return carry

    lax.fori_loop(0, BX, plane, 0)


def faces_kernel(info, bg, va, *sends):
    write_faces(info, bg, va, sends)


def first_faces(info, bg, va):
    return pl.pallas_call(
        faces_kernel,
        out_shape=[f32(NVAR, FACE, BZ)] * 4,
        in_specs=[SMEM, VMEM, VMEM],
        out_specs=[VMEM] * 4,
        compiler_params=params(),
        name="first_faces",
    )(info, bg, va)


def sweep_kernel(which, want_faces, info, flux, *refs):
    refs = list(refs)
    grids = {}
    for name in which:
        size = 4 if name == "bg" else 3
        grids[name] = refs[:size]
        refs = refs[size:]
    faces, refs = refs[:4], refs[4:]
    outs = {name: refs[k] for k, name in enumerate(which)}
    refs = refs[len(which) :]
    sends = refs[:4] if want_faces else None
    padded = refs[-1]
    for name in which:
        fill_padded(info, grids[name][0], 0 if name == "bg" else 1, faces, padded)
        blanking = grids[name][3] if name == "bg" else None
        sweep(flux, padded, grids[name][1], grids[name][2], blanking, outs[name])
    if want_faces:
        write_faces(info, outs["bg"], outs["va"], sends)


def sweep_call(info, flux, grids, faces, want_faces):
    which = tuple(grids)
    operands = [array for name in which for array in grids[name]]
    outs = [f32(NVAR, BX, BY, BZ)] * len(which) + ([f32(NVAR, FACE, BZ)] * 4 if want_faces else [])
    return pl.pallas_call(
        functools.partial(sweep_kernel, which, want_faces),
        out_shape=outs,
        in_specs=[SMEM, SMEM] + [VMEM] * (len(operands) + 4),
        out_specs=[VMEM] * len(outs),
        scratch_shapes=[pltpu.VMEM((NVAR, BX + 2, BY + 16, BZ), jnp.float32)],
        compiler_params=params(),
        name="sweep_" + "_".join(which),
    )(info, flux, *operands, *faces)


def parts_of(value):
    high = value.astype(jnp.bfloat16)
    return high, (value - high.astype(jnp.float32)).astype(jnp.bfloat16)


def pick_kernel(group, owners, count, valve, cells, base, weight, payload, table):
    for v in range(NVAR):
        across = valve[v].reshape(PLANES, BZ).T
        high, low = parts_of(across)
        table[v * BZ : (v + 1) * BZ, 0:PLANES] = high
        table[v * BZ : (v + 1) * BZ, PLANES : 2 * PLANES] = low
    width = group * CAP
    plane_at = lax.broadcasted_iota(jnp.int32, (PLANES, CAP), 0)
    depth_at = lax.broadcasted_iota(jnp.int32, (BZ, CAP), 0)
    slot_at = lax.broadcasted_iota(jnp.int32, (1, CAP), 1)

    def step(index, carry):
        start = index * group
        hits = []
        for k in range(group):
            plane = cells[pl.ds(start + k, 1), :] // BZ
            hits.append(jnp.where(plane_at == plane, 1.0, 0.0).astype(jnp.bfloat16))
        hit = jnp.concatenate(hits, axis=1)
        both = jnp.concatenate([hit, hit], axis=0)
        rows = jnp.dot(table[...], both, preferred_element_type=jnp.float32)
        for k in range(group):
            owner = start + k
            depth = cells[pl.ds(owner, 1), :] % BZ
            here = depth_at == depth
            live = slot_at < count[0, owner]
            for v in range(NVAR):
                row = rows[v * BZ : (v + 1) * BZ, k * CAP : (k + 1) * CAP]
                value = jnp.sum(jnp.where(here, row, 0.0), axis=0, keepdims=True)
                payload[owner, 8 + v : 9 + v, :] = jnp.where(live, value, 0.0)
            for k8 in range(8):
                payload[owner, k8 : k8 + 1, :] = weight[k8, pl.ds(owner, 1), :]
            payload[owner, 13:14, :] = base[pl.ds(owner, 1), :].astype(jnp.float32)
            payload[owner, 14:16, :] = jnp.zeros((2, CAP), jnp.float32)
        return carry

    lax.fori_loop(0, owners // group, step, 0)


def pick(count, valve, cells, base, weight):
    owners = cells.shape[0]
    group = 4 if owners % 4 == 0 else 1
    return pl.pallas_call(
        functools.partial(pick_kernel, group, owners),
        out_shape=f32(owners, SEND_ROWS, CAP),
        in_specs=[SMEM] + [VMEM] * 4,
        out_specs=VMEM,
        scratch_shapes=[pltpu.VMEM((NVAR * BZ, 2 * PLANES), jnp.bfloat16)],
        compiler_params=params(),
        name="pick",
    )(count, valve, cells, base, weight)


def scatter_kernel(group, senders, arrived, swept, out, total, spread, placed):
    width = group * CAP
    plane_at = lax.broadcasted_iota(jnp.int32, (PLANES, CAP), 0)
    depth_at = lax.broadcasted_iota(jnp.int32, (BZ, CAP), 0)
    total[...] = jnp.zeros_like(total)

    def step(index, carry):
        start = index * group
        for k in range(group):
            sender = start + k
            cols = slice(k * CAP, (k + 1) * CAP)
            lows = slice(width + k * CAP, width + (k + 1) * CAP)
            anchor = arrived[sender, 13:14, :].astype(jnp.int32)
            delta = plane_at - anchor // BZ
            at = [delta == i * BY + j for i in range(2) for j in range(2)]
            for step_z in range(2):
                whole = jnp.zeros((PLANES, CAP), jnp.float32)
                for corner in range(4):
                    row = 2 * corner + step_z
                    whole = jnp.where(at[corner], arrived[sender, row : row + 1, :], whole)
                high, low = parts_of(whole)
                spread[step_z * PLANES : (step_z + 1) * PLANES, cols] = high
                spread[step_z * PLANES : (step_z + 1) * PLANES, lows] = low
            here = depth_at == anchor % BZ
            for v in range(NVAR):
                high, low = parts_of(arrived[sender, 8 + v : 9 + v, :])
                high, low = high.astype(jnp.float32), low.astype(jnp.float32)
                placed[v * BZ : (v + 1) * BZ, cols] = jnp.where(here, high, 0.0).astype(jnp.bfloat16)
                placed[v * BZ : (v + 1) * BZ, lows] = jnp.where(here, low, 0.0).astype(jnp.bfloat16)
        dims = (((1,), (1,)), ((), ()))
        first = lax.dot_general(
            spread[:, :width], placed[:, :width], dims, preferred_element_type=jnp.float32
        )
        second = lax.dot_general(
            spread[:, :width], placed[:, width:], dims, preferred_element_type=jnp.float32
        )
        third = lax.dot_general(
            spread[:, width:], placed[:, :width], dims, preferred_element_type=jnp.float32
        )
        total[...] += first + (second + third)
        return carry

    lax.fori_loop(0, senders // group, step, 0)
    depth = lax.broadcasted_iota(jnp.int32, (PLANES, BZ), 1)
    for v in range(NVAR):
        cols = slice(v * BZ, (v + 1) * BZ)
        upper = jnp.where(depth == 0, 0.0, pltpu.roll(total[PLANES:, cols], 1, 1))
        pushed = total[:PLANES, cols] + upper
        out[v] = swept[v] + pushed.reshape(BX, BY, BZ)


def scatter(arrived, swept):
    senders = arrived.shape[0]
    group = 4 if senders % 4 == 0 else 1
    return pl.pallas_call(
        functools.partial(scatter_kernel, group, senders),
        out_shape=f32(NVAR, BX, BY, BZ),
        in_specs=[VMEM, VMEM],
        out_specs=VMEM,
        scratch_shapes=[
            pltpu.VMEM((2 * PLANES, NVAR * BZ), jnp.float32),
            pltpu.VMEM((2 * PLANES, 2 * group * CAP), jnp.bfloat16),
            pltpu.VMEM((NVAR * BZ, 2 * group * CAP), jnp.bfloat16),
        ],
        compiler_params=params(),
        name="scatter",
    )(arrived, swept)


def body(
    bulk,
    valve,
    bg_adjoint,
    bg_velocity,
    bg_source,
    bg_iblank,
    valve_adjoint,
    valve_velocity,
    valve_source,
    flux_mix,
    rec_cell,
    donor_base,
    donor_weight,
    slot_count,
):
    plans = face_plans(bulk, valve)
    info = jnp.stack(
        [lax.axis_index("bulk"), lax.axis_index("valve"), jnp.int32(bulk), jnp.int32(valve)]
    ).astype(jnp.int32)
    bg, va = bg_adjoint, valve_adjoint
    faces = first_faces(info, bg, va)
    for repeat in range(ITERS - 1):
        arrived = exchange(faces, plans)
        grids = {"bg": (bg, bg_velocity, bg_source, bg_iblank), "va": (va, valve_velocity, valve_source)}
        bg, va, *faces = sweep_call(info, flux_mix, grids, arrived, True)
    arrived = exchange(faces, plans)
    (va,) = sweep_call(info, flux_mix, {"va": (va, valve_velocity, valve_source)}, arrived, False)
    payload = pick(slot_count, va, rec_cell[0], donor_base[0], donor_weight[:, 0])
    received = lax.all_to_all(payload, ("bulk", "valve"), split_axis=0, concat_axis=0, tiled=True)
    (bg,) = sweep_call(info, flux_mix, {"bg": (bg, bg_velocity, bg_source, bg_iblank)}, arrived, False)
    return (scatter(received, bg), va)


def solution(mesh):
    placed = (
        P(None, "bulk", "valve", None),
        P(None, "bulk", "valve", None),
        P(None, "bulk", "valve", None),
        P("bulk", "valve", None),
        P(None, "valve", "bulk", None),
        P(None, "valve", "bulk", None),
        P(None, "valve", "bulk", None),
        P(),
        P(("bulk", "valve"), None, None),
        P(("bulk", "valve"), None, None),
        P(None, ("bulk", "valve"), None, None),
        P(("bulk", "valve"), None),
    )
    return jax.shard_map(
        functools.partial(body, mesh.shape["bulk"], mesh.shape["valve"]),
        mesh=mesh,
        in_specs=placed,
        out_specs=(P(None, "bulk", "valve", None), P(None, "valve", "bulk", None)),
        check_vma=False,
    )
```

profile of v0, /device:TPU:0, one launch (start us, length us, event | category | flops | bytes accessed | tf_op | source)
XLA Modules:
  0.0 95.0 jit_solution(3699476302144672247)
XLA Ops:
  0.7 1.1 %copy-done.6 = f32[5,8,32,128]{3,2,1,0:T(8,128)S(1)} copy-done((f32[5,8,32,128]{3,2,1,0:T(8,128)S(1)}, f32[5,8,32,128]{3,2,1,0:T(8,128)}, u32[]{:S(2)}) %copy-start.6) | copy-done | bytes 655384
  1.8 1.1 %copy-done.7 = f32[5,8,32,128]{3,2,1,0:T(8,128)S(1)} copy-done((f32[5,8,32,128]{3,2,1,0:T(8,128)S(1)}, f32[5,8,32,128]{3,2,1,0:T(8,128)}, u32[]{:S(2)}) %copy-start.7) | copy-done | bytes 655384
  4.0 2.6 %collective-permute-start.1 = (f32[5,40,128]{2,1,0:T(8,128)S(1)}, f32[5,40,128]{2,1,0:T(8,128)S(1)}, u32[]{:S(2)}, u32[]{:S(2)}) collective-permute-start(f32[5,40,128]{2,1,0:T(8,128)S(1)} %get-tuple-element.25), channel_id=1, source_target_pairs={{0,24},{1,25},{2,26},{3,27},{4,28},{5,29},{6,30},{7,31},{8,16},{9,... | collective-permute-start | bytes 307208 | tf_op jit(solution)/shard_map/ppermute | solution.py:55
  6.7 1.5 %collective-permute-start.2 = (f32[5,40,128]{2,1,0:T(8,128)S(1)}, f32[5,40,128]{2,1,0:T(8,128)S(1)}, u32[]{:S(2)}, u32[]{:S(2)}) collective-permute-start(f32[5,40,128]{2,1,0:T(8,128)S(1)} %get-tuple-element.26), channel_id=1, source_target_pairs={{0,1},{1,0},{2,3},{3,2},{4,5},{5,4},{6,7},{7,6},{8,9},{9,8},{10,11... | collective-permute-start | bytes 307208 | tf_op jit(solution)/shard_map/ppermute | solution.py:55
  9.8 2.9 %collective-permute-done.2.refs_9_ = f32[5,40,128]{2,1,0:T(8,128)S(1)} collective-permute-done((f32[5,40,128]{2,1,0:T(8,128)S(1)}, f32[5,40,128]{2,1,0:T(8,128)S(1)}, u32[]{:S(2)}, u32[]{:S(2)}) %collective-permute-start.2) | collective-permute-done | bytes 102432 | tf_op jit(solution)/shard_map/ppermute | solution.py:55
  15.7 3.7 %sweep_bg_va.3 = (f32[5,8,32,128]{3,2,1,0:T(8,128)S(1)}, f32[5,8,32,128]{3,2,1,0:T(8,128)S(1)}, f32[5,40,128]{2,1,0:T(8,128)S(1)}, f32[5,40,128]{2,1,0:T(8,128)S...) custom-call(s32[4]{0:T(128)S(1)} %pad_add_fusion.info, f32[3,5,5]{2,1,0:T(8,128)S(1)} %copy.17.flux, ...), custom_call_target="tpu_custom_call" | custom-call | tf_op jit(solution)/shard_map/sweep_bg_va/pallas_call | solution.py:179
  20.1 2.5 %collective-permute-start.6 = (f32[5,40,128]{2,1,0:T(8,128)S(1)}, f32[5,40,128]{2,1,0:T(8,128)S(1)}, u32[]{:S(2)}, u32[]{:S(2)}) collective-permute-start(f32[5,40,128]{2,1,0:T(8,128)S(1)} %get-tuple-element.32), channel_id=1, source_target_pairs={{0,1},{1,0},{2,3},{3,2},{4,5},{5,4},{6,7},{7,6},{8,9},{9,8},{10,11... | collective-permute-start | bytes 307208 | tf_op jit(solution)/shard_map/ppermute | solution.py:55
  22.6 1.5 %collective-permute-done.5.refs_8_ = f32[5,40,128]{2,1,0:T(8,128)S(1)} collective-permute-done((f32[5,40,128]{2,1,0:T(8,128)S(1)}, f32[5,40,128]{2,1,0:T(8,128)S(1)}, u32[]{:S(2)}, u32[]{:S(2)}) %collective-permute-start.5) | collective-permute-done | bytes 102432 | tf_op jit(solution)/shard_map/ppermute | solution.py:55
  24.1 3.0 %collective-permute-done.6.refs_9_ = f32[5,40,128]{2,1,0:T(8,128)S(1)} collective-permute-done((f32[5,40,128]{2,1,0:T(8,128)S(1)}, f32[5,40,128]{2,1,0:T(8,128)S(1)}, u32[]{:S(2)}, u32[]{:S(2)}) %collective-permute-start.6) | collective-permute-done | bytes 102432 | tf_op jit(solution)/shard_map/ppermute | solution.py:55
  27.1 3.7 %sweep_bg_va.4 = (f32[5,8,32,128]{3,2,1,0:T(8,128)S(1)}, f32[5,8,32,128]{3,2,1,0:T(8,128)S(1)}, f32[5,40,128]{2,1,0:T(8,128)S(1)}, f32[5,40,128]{2,1,0:T(8,128)S...) custom-call(s32[4]{0:T(128)S(1)} %pad_add_fusion.info, f32[3,5,5]{2,1,0:T(8,128)S(1)} %copy.17.flux, ...), custom_call_target="tpu_custom_call" | custom-call | tf_op jit(solution)/shard_map/sweep_bg_va/pallas_call | solution.py:179
  30.9 1.6 %collective-permute-start.9 = (f32[5,40,128]{2,1,0:T(8,128)S(1)}, f32[5,40,128]{2,1,0:T(8,128)S(1)}, u32[]{:S(2)}, u32[]{:S(2)}) collective-permute-start(f32[5,40,128]{2,1,0:T(8,128)S(1)} %get-tuple-element.37), channel_id=1, source_target_pairs={{0,24},{1,25},{2,26},{3,27},{4,28},{5,29},{6,30},{7,31},{8,16},{9,... | collective-permute-start | bytes 307208 | tf_op jit(solution)/shard_map/ppermute | solution.py:55
  32.5 2.5 %collective-permute-start.10 = (f32[5,40,128]{2,1,0:T(8,128)S(1)}, f32[5,40,128]{2,1,0:T(8,128)S(1)}, u32[]{:S(2)}, u32[]{:S(2)}) collective-permute-start(f32[5,40,128]{2,1,0:T(8,128)S(1)} %get-tuple-element.38), channel_id=1, source_target_pairs={{0,1},{1,0},{2,3},{3,2},{4,5},{5,4},{6,7},{7,6},{8,9},{9,8},{10,11... | collective-permute-start | bytes 307208 | tf_op jit(solution)/shard_map/ppermute | solution.py:55
  35.6 4.0 %collective-permute-done.10.refs_9_ = f32[5,40,128]{2,1,0:T(8,128)S(1)} collective-permute-done((f32[5,40,128]{2,1,0:T(8,128)S(1)}, f32[5,40,128]{2,1,0:T(8,128)S(1)}, u32[]{:S(2)}, u32[]{:S(2)}) %collective-permute-start.10) | collective-permute-done | bytes 102432 | tf_op jit(solution)/shard_map/ppermute | solution.py:55
  39.6 3.7 %sweep_bg_va.5 = (f32[5,8,32,128]{3,2,1,0:T(8,128)S(1)}, f32[5,8,32,128]{3,2,1,0:T(8,128)S(1)}, f32[5,40,128]{2,1,0:T(8,128)S(1)}, f32[5,40,128]{2,1,0:T(8,128)S...) custom-call(s32[4]{0:T(128)S(1)} %pad_add_fusion.info, f32[3,5,5]{2,1,0:T(8,128)S(1)} %copy.17.flux, ...), custom_call_target="tpu_custom_call" | custom-call | tf_op jit(solution)/shard_map/sweep_bg_va/pallas_call | solution.py:179
  44.0 2.5 %collective-permute-start.14 = (f32[5,40,128]{2,1,0:T(8,128)S(1)}, f32[5,40,128]{2,1,0:T(8,128)S(1)}, u32[]{:S(2)}, u32[]{:S(2)}) collective-permute-start(f32[5,40,128]{2,1,0:T(8,128)S(1)} %get-tuple-element.43), channel_id=1, source_target_pairs={{0,1},{1,0},{2,3},{3,2},{4,5},{5,4},{6,7},{7,6},{8,9},{9,8},{10,11... | collective-permute-start | bytes 307208 | tf_op jit(solution)/shard_map/ppermute | solution.py:55
  46.5 1.5 %collective-permute-done.13.refs_4_.refs_5_ = f32[5,40,128]{2,1,0:T(8,128)S(1)} collective-permute-done((f32[5,40,128]{2,1,0:T(8,128)S(1)}, f32[5,40,128]{2,1,0:T(8,128)S(1)}, u32[]{:S(2)}, u32[]{:S(2)}) %collective-permute-start.13) | collective-permute-done | bytes 102432 | tf_op jit(solution)/shard_map/ppermute | solution.py:55
  48.1 3.0 %collective-permute-done.14.refs_5_.refs_6_ = f32[5,40,128]{2,1,0:T(8,128)S(1)} collective-permute-done((f32[5,40,128]{2,1,0:T(8,128)S(1)}, f32[5,40,128]{2,1,0:T(8,128)S(1)}, u32[]{:S(2)}, u32[]{:S(2)}) %collective-permute-start.14) | collective-permute-done | bytes 102432 | tf_op jit(solution)/shard_map/ppermute | solution.py:55
  51.1 3.0 %sweep_va.1.valve = f32[5,8,32,128]{3,2,1,0:T(8,128)} custom-call(s32[4]{0:T(128)S(1)} %pad_add_fusion.info, f32[3,5,5]{2,1,0:T(8,128)S(1)} %copy.17.flux, f32[5,8,32,128]{3,2,1,0:T(8,128)S(1)} %get-tuple-element.40.refs_0_, f32[3,8,32,128]{3,2,1,0:T(8,128)S(1)} %copy-done.3, f32[5,8,32,128]{3,2,1,0:T(8,128)S(1)} %copy-done, ...), custom_call_target="tpu_custom_call" | custom-call | tf_op jit(solution)/shard_map/sweep_va/pallas_call | solution.py:179
  54.7 1.1 %copy-done.8 = f32[5,8,32,128]{3,2,1,0:T(8,128)S(1)} copy-done((f32[5,8,32,128]{3,2,1,0:T(8,128)S(1)}, f32[5,8,32,128]{3,2,1,0:T(8,128)}, u32[]{:S(2)}) %copy-start.8) | copy-done | bytes 655384
  55.8 6.1 %pick.1 = f32[32,16,128]{2,1,0:T(8,128)} custom-call(s32[1,32]{1,0:T(1,128)S(1)} %copy-done.14, f32[5,8,32,128]{3,2,1,0:T(8,128)S(1)} %copy-done.8, s32[32,128]{1,0:T(8,128)S(1)} %bitcast.6, s32[32,128]{1,0:T(8,128)S(1)} %bitcast.7, f32[8,32,128]{2,1,0:T(8,128)S(1)} %bitcast.5), custom_call_target="tpu_custom_call" | custom-call | tf_op jit(solution)/shard_map/pick/pallas_call | solution.py:236
  61.9 5.9 %all-to-all-start = ((f32[32,16,128]{2,1,0:T(8,128)}), f32[32,16,128]{2,1,0:T(8,128)S(1)}, u32[]{:S(2)}, u32[]{:S(2)}) async-start(f32[32,16,128]{2,1,0:T(8,128)} %pick.1), calls=%async_computation | async-start | bytes 524288 | tf_op jit(solution)/shard_map/all_to_all | solution.py:345
  67.8 2.2 %sweep_bg.1.swept = f32[5,8,32,128]{3,2,1,0:T(8,128)S(1)} custom-call(s32[4]{0:T(128)S(1)} %pad_add_fusion.info, f32[3,5,5]{2,1,0:T(8,128)S(1)} %copy.17.flux, f32[5,8,32,128]{3,2,1,0:T(8,128)S(1)} %get-tuple-element.45.refs_0_, f32[3,8,32,128]{3,2,1,0:T(8,128)S(1)} %copy-done.5, f32[5,8,32,128]{3,2,1,0:T(8,128)S(1)} %copy-done.1, ...), custom_call_target="tpu_custom_call" | custom-call | tf_op jit(solution)/shard_map/sweep_bg/pallas_call | solution.py:179
  70.1 8.4 %all-to-all-done.arrived = f32[32,16,128]{2,1,0:T(8,128)S(1)} async-done(((f32[32,16,128]{2,1,0:T(8,128)}), f32[32,16,128]{2,1,0:T(8,128)S(1)}, u32[]{:S(2)}, u32[]{:S(2)}) %all-to-all-start) | async-done | bytes 262176 | tf_op jit(solution)/shard_map/all_to_all | solution.py:345
  78.5 16.5 %scatter.1 = f32[5,8,32,128]{3,2,1,0:T(8,128)} custom-call(f32[32,16,128]{2,1,0:T(8,128)S(1)} %all-to-all-done.arrived, f32[5,8,32,128]{3,2,1,0:T(8,128)S(1)} %sweep_bg.1.swept), custom_call_target="tpu_custom_call" | custom-call | tf_op jit(solution)/shard_map/scatter/pallas_call | solution.py:301
  (50 shorter events, 8.5 us)
Async XLA Ops:
  2.9 9.9 %copy-start = (f32[5,8,32,128]{3,2,1,0:T(8,128)S(1)}, f32[5,8,32,128]{3,2,1,0:T(8,128)}, u32[]{:S(2)}) copy-start(f32[5,8,32,128]{3,2,1,0:T(8,128)} %refs_2_.8) | copy-start | bytes 1966084
  2.9 9.9 %copy-start.1 = (f32[5,8,32,128]{3,2,1,0:T(8,128)S(1)}, f32[5,8,32,128]{3,2,1,0:T(8,128)}, u32[]{:S(2)}) copy-start(f32[5,8,32,128]{3,2,1,0:T(8,128)} %refs_2_.9) | copy-start | bytes 1966084
  3.5 5.4 %collective-permute-start = (f32[5,40,128]{2,1,0:T(8,128)S(1)}, f32[5,40,128]{2,1,0:T(8,128)S(1)}, u32[]{:S(2)}, u32[]{:S(2)}) collective-permute-start(f32[5,40,128]{2,1,0:T(8,128)S(1)} %get-tuple-element.24), channel_id=1, source_target_pairs={{0,8},{1,9},{2,10},{3,11},{4,12},{5,13},{6,14},{7,15},{8,0},{9,1},... | collective-permute-start | bytes 307208 | tf_op jit(solution)/shard_map/ppermute | solution.py:55
  4.0 5.8 %collective-permute-start.1 = (f32[5,40,128]{2,1,0:T(8,128)S(1)}, f32[5,40,128]{2,1,0:T(8,128)S(1)}, u32[]{:S(2)}, u32[]{:S(2)}) collective-permute-start(f32[5,40,128]{2,1,0:T(8,128)S(1)} %get-tuple-element.25), channel_id=1, source_target_pairs={{0,24},{1,25},{2,26},{3,27},{4,28},{5,29},{6,30},{7,31},{8,16},{9,... | collective-permute-start | bytes 307208 | tf_op jit(solution)/shard_map/ppermute | solution.py:55
  6.7 6.1 %collective-permute-start.2 = (f32[5,40,128]{2,1,0:T(8,128)S(1)}, f32[5,40,128]{2,1,0:T(8,128)S(1)}, u32[]{:S(2)}, u32[]{:S(2)}) collective-permute-start(f32[5,40,128]{2,1,0:T(8,128)S(1)} %get-tuple-element.26), channel_id=1, source_target_pairs={{0,1},{1,0},{2,3},{3,2},{4,5},{5,4},{6,7},{7,6},{8,9},{9,8},{10,11... | collective-permute-start | bytes 307208 | tf_op jit(solution)/shard_map/ppermute | solution.py:55
  8.2 4.6 %collective-permute-start.3 = (f32[5,40,128]{2,1,0:T(8,128)S(1)}, f32[5,40,128]{2,1,0:T(8,128)S(1)}, u32[]{:S(2)}, u32[]{:S(2)}) collective-permute-start(f32[5,40,128]{2,1,0:T(8,128)S(1)} %get-tuple-element.27), channel_id=1, source_target_pairs={{0,8},{1,2},{2,1},{3,4},{4,3},{5,6},{6,5},{7,15},{8,0},{9,10},{10,... | collective-permute-start | bytes 307208 | tf_op jit(solution)/shard_map/ppermute | solution.py:55
  19.4 3.2 %collective-permute-start.4 = (f32[5,40,128]{2,1,0:T(8,128)S(1)}, f32[5,40,128]{2,1,0:T(8,128)S(1)}, u32[]{:S(2)}, u32[]{:S(2)}) collective-permute-start(f32[5,40,128]{2,1,0:T(8,128)S(1)} %get-tuple-element.30), channel_id=1, source_target_pairs={{0,8},{1,9},{2,10},{3,11},{4,12},{5,13},{6,14},{7,15},{8,0},{9,1},... | collective-permute-start | bytes 307208 | tf_op jit(solution)/shard_map/ppermute | solution.py:55
  19.4 4.7 %collective-permute-start.5 = (f32[5,40,128]{2,1,0:T(8,128)S(1)}, f32[5,40,128]{2,1,0:T(8,128)S(1)}, u32[]{:S(2)}, u32[]{:S(2)}) collective-permute-start(f32[5,40,128]{2,1,0:T(8,128)S(1)} %get-tuple-element.31), channel_id=1, source_target_pairs={{0,24},{1,25},{2,26},{3,27},{4,28},{5,29},{6,30},{7,31},{8,16},{9,... | collective-permute-start | bytes 307208 | tf_op jit(solution)/shard_map/ppermute | solution.py:55
  20.1 7.1 %collective-permute-start.6 = (f32[5,40,128]{2,1,0:T(8,128)S(1)}, f32[5,40,128]{2,1,0:T(8,128)S(1)}, u32[]{:S(2)}, u32[]{:S(2)}) collective-permute-start(f32[5,40,128]{2,1,0:T(8,128)S(1)} %get-tuple-element.32), channel_id=1, source_target_pairs={{0,1},{1,0},{2,3},{3,2},{4,5},{5,4},{6,7},{7,6},{8,9},{9,8},{10,11... | collective-permute-start | bytes 307208 | tf_op jit(solution)/shard_map/ppermute | solution.py:55
  22.6 4.6 %collective-permute-start.7 = (f32[5,40,128]{2,1,0:T(8,128)S(1)}, f32[5,40,128]{2,1,0:T(8,128)S(1)}, u32[]{:S(2)}, u32[]{:S(2)}) collective-permute-start(f32[5,40,128]{2,1,0:T(8,128)S(1)} %get-tuple-element.33), channel_id=1, source_target_pairs={{0,8},{1,2},{2,1},{3,4},{4,3},{5,6},{6,5},{7,15},{8,0},{9,10},{10,... | collective-permute-start | bytes 307208 | tf_op jit(solution)/shard_map/ppermute | solution.py:55
  30.9 4.2 %collective-permute-start.8 = (f32[5,40,128]{2,1,0:T(8,128)S(1)}, f32[5,40,128]{2,1,0:T(8,128)S(1)}, u32[]{:S(2)}, u32[]{:S(2)}) collective-permute-start(f32[5,40,128]{2,1,0:T(8,128)S(1)} %get-tuple-element.36), channel_id=1, source_target_pairs={{0,8},{1,9},{2,10},{3,11},{4,12},{5,13},{6,14},{7,15},{8,0},{9,1},... | collective-permute-start | bytes 307208 | tf_op jit(solution)/shard_map/ppermute | solution.py:55
  30.9 4.7 %collective-permute-start.9 = (f32[5,40,128]{2,1,0:T(8,128)S(1)}, f32[5,40,128]{2,1,0:T(8,128)S(1)}, u32[]{:S(2)}, u32[]{:S(2)}) collective-permute-start(f32[5,40,128]{2,1,0:T(8,128)S(1)} %get-tuple-element.37), channel_id=1, source_target_pairs={{0,24},{1,25},{2,26},{3,27},{4,28},{5,29},{6,30},{7,31},{8,16},{9,... | collective-permute-start | bytes 307208 | tf_op jit(solution)/shard_map/ppermute | solution.py:55
  32.5 7.0 %collective-permute-start.10 = (f32[5,40,128]{2,1,0:T(8,128)S(1)}, f32[5,40,128]{2,1,0:T(8,128)S(1)}, u32[]{:S(2)}, u32[]{:S(2)}) collective-permute-start(f32[5,40,128]{2,1,0:T(8,128)S(1)} %get-tuple-element.38), channel_id=1, source_target_pairs={{0,1},{1,0},{2,3},{3,2},{4,5},{5,4},{6,7},{7,6},{8,9},{9,8},{10,11... | collective-permute-start | bytes 307208 | tf_op jit(solution)/shard_map/ppermute | solution.py:55
  35.0 4.6 %collective-permute-start.11 = (f32[5,40,128]{2,1,0:T(8,128)S(1)}, f32[5,40,128]{2,1,0:T(8,128)S(1)}, u32[]{:S(2)}, u32[]{:S(2)}) collective-permute-start(f32[5,40,128]{2,1,0:T(8,128)S(1)} %get-tuple-element.39), channel_id=1, source_target_pairs={{0,8},{1,2},{2,1},{3,4},{4,3},{5,6},{6,5},{7,15},{8,0},{9,10},{10,... | collective-permute-start | bytes 307208 | tf_op jit(solution)/shard_map/ppermute | solution.py:55
  39.6 11.5 %copy-start.3 = (f32[3,8,32,128]{3,2,1,0:T(8,128)S(1)}, f32[3,8,32,128]{3,2,1,0:T(8,128)}, u32[]{:S(2)}) copy-start(f32[3,8,32,128]{3,2,1,0:T(8,128)} %refs_1_.8) | copy-start | bytes 1179652
  43.3 3.2 %collective-permute-start.12 = (f32[5,40,128]{2,1,0:T(8,128)S(1)}, f32[5,40,128]{2,1,0:T(8,128)S(1)}, u32[]{:S(2)}, u32[]{:S(2)}) collective-permute-start(f32[5,40,128]{2,1,0:T(8,128)S(1)} %get-tuple-element.41), channel_id=1, source_target_pairs={{0,8},{1,9},{2,10},{3,11},{4,12},{5,13},{6,14},{7,15},{8,0},{9,1},... | collective-permute-start | bytes 307208 | tf_op jit(solution)/shard_map/ppermute | solution.py:55
  43.4 4.7 %collective-permute-start.13 = (f32[5,40,128]{2,1,0:T(8,128)S(1)}, f32[5,40,128]{2,1,0:T(8,128)S(1)}, u32[]{:S(2)}, u32[]{:S(2)}) collective-permute-start(f32[5,40,128]{2,1,0:T(8,128)S(1)} %get-tuple-element.42), channel_id=1, source_target_pairs={{0,24},{1,25},{2,26},{3,27},{4,28},{5,29},{6,30},{7,31},{8,16},{9,... | collective-permute-start | bytes 307208 | tf_op jit(solution)/shard_map/ppermute | solution.py:55
  44.0 7.0 %collective-permute-start.14 = (f32[5,40,128]{2,1,0:T(8,128)S(1)}, f32[5,40,128]{2,1,0:T(8,128)S(1)}, u32[]{:S(2)}, u32[]{:S(2)}) collective-permute-start(f32[5,40,128]{2,1,0:T(8,128)S(1)} %get-tuple-element.43), channel_id=1, source_target_pairs={{0,1},{1,0},{2,3},{3,2},{4,5},{5,4},{6,7},{7,6},{8,9},{9,8},{10,11... | collective-permute-start | bytes 307208 | tf_op jit(solution)/shard_map/ppermute | solution.py:55
  46.5 4.6 %collective-permute-start.15 = (f32[5,40,128]{2,1,0:T(8,128)S(1)}, f32[5,40,128]{2,1,0:T(8,128)S(1)}, u32[]{:S(2)}, u32[]{:S(2)}) collective-permute-start(f32[5,40,128]{2,1,0:T(8,128)S(1)} %get-tuple-element.44), channel_id=1, source_target_pairs={{0,8},{1,2},{2,1},{3,4},{4,3},{5,6},{6,5},{7,15},{8,0},{9,10},{10,... | collective-permute-start | bytes 307208 | tf_op jit(solution)/shard_map/ppermute | solution.py:55
  51.1 3.0 %copy-start.11 = (f32[8,1,32,128]{3,2,1,0:T(8,128)S(1)}, f32[8,1,32,128]{3,2,1,0:T(8,128)}, u32[]{:S(2)}) copy-start(f32[8,1,32,128]{3,2,1,0:T(8,128)} %param.22) | copy-start | bytes 393220
  51.1 3.0 %copy-start.12 = (s32[1,32,128]{2,1,0:T(8,128)S(1)}, s32[1,32,128]{2,1,0:T(8,128)}, u32[]{:S(2)}) copy-start(s32[1,32,128]{2,1,0:T(8,128)} %param.20) | copy-start | bytes 49156
  61.9 5.9 %copy-start.5 = (f32[3,8,32,128]{3,2,1,0:T(8,128)S(1)}, f32[3,8,32,128]{3,2,1,0:T(8,128)}, u32[]{:S(2)}) copy-start(f32[3,8,32,128]{3,2,1,0:T(8,128)} %refs_1_.9) | copy-start | bytes 1179652
  61.9 5.9 %copy-start.10 = (s32[8,32,128]{2,1,0:T(8,128)S(1)}, s32[8,32,128]{2,1,0:T(8,128)}, u32[]{:S(2)}) copy-start(s32[8,32,128]{2,1,0:T(8,128)} %refs_3_.7) | copy-start | bytes 393220
  61.9 16.5 %all-to-all-start = ((f32[32,16,128]{2,1,0:T(8,128)}), f32[32,16,128]{2,1,0:T(8,128)S(1)}, u32[]{:S(2)}, u32[]{:S(2)}) async-start(f32[32,16,128]{2,1,0:T(8,128)} %pick.1), calls=%async_computation | async-start | bytes 524288 | tf_op jit(solution)/shard_map/all_to_all | solution.py:345
  (8 other events, 9.8 us)
where the time goes:
time: 95.4 us; the launch traced here: 95 us
  Pallas kernels  39.5 us (41%)
  waiting for transfers between devices  25.9 us (27%)
  starting transfers between devices  21.1 us (22%)
  local copies, waits for them, and re-layouts  7.53 us (8%)
    ppermute x16, waiting for transfers between devices, exchange(): lax.ppermute(face, ('bulk', 'valve'), plan)  17.6 us
    pallas_call x1, Pallas kernels, scatter(): pl.pallas_call(functools.partial(scatter_kernel, group, senders), out_sha...  16.5 us
    pallas_call x5, Pallas kernels, sweep_call(): pl.pallas_call(functools.partial(sweep_kernel, which, want_faces), out_sh...  16.3 us
    ppermute x16, starting transfers between devices, exchange(): lax.ppermute(face, ('bulk', 'valve'), plan)  15.2 us
    all_to_all x1, waiting for transfers between devices, body(): lax.all_to_all(payload, ('bulk', 'valve'), split_axis=0, concat_axis=0, t...  8.38 us
    unnamed x31, local copies, waits for them, and re-layouts  7.53 us
    pallas_call x1, Pallas kernels, pick(): pl.pallas_call(functools.partial(pick_kernel, group, owners), out_shape=f...  6.11 us
    all_to_all x1, starting transfers between devices, body(): lax.all_to_all(payload, ('bulk', 'valve'), split_axis=0, concat_axis=0, t...  5.87 us
  transfers between devices with their start and end apart: 17, of which 9 were waited for; matrix products, arithmetic and copies ran while one was open for 1% of the time, Pallas kernels for 2%

commit v1 on v0

v1 whole, which is shorter than its diff:
```python
import functools

import jax
import jax.numpy as jnp
from jax import lax
from jax.experimental import pallas as pl
from jax.experimental.pallas import tpu as pltpu
from jax.sharding import PartitionSpec as P

NVAR = 5
ITERS = 4
CAP = 128
BX = 8
BY = 32
BZ = 128
PLANES = BX * BY
FACE = BY + BX
SEND_ROWS = 16

VMEM = pl.BlockSpec(memory_space=pltpu.VMEM)
SMEM = pl.BlockSpec(memory_space=pltpu.SMEM)
HBM = pl.BlockSpec(memory_space=pltpu.HBM)


def params(mib):
    return pltpu.CompilerParams(vmem_limit_bytes=mib * 1024 * 1024)


def in_hbm(x):
    return pltpu.with_memory_space_constraint(x, pltpu.HBM)


def f32(*shape):
    return jax.ShapeDtypeStruct(shape, jnp.float32)


def swap_pairs(count, odd):
    return {i: (i + 1 if i % 2 == odd else i - 1) % count for i in range(count)}


def face_plans(bulk, valve):
    number = lambda b, v: b * valve + v
    plans = []
    for odd in (0, 1):
        swap = swap_pairs(bulk, odd)
        plans.append([(number(b, v), number(swap[b], v)) for b in range(bulk) for v in range(valve)])
    for odd in (0, 1):
        swap = swap_pairs(valve, odd)
        pairs = []
        for b in range(bulk):
            for v in range(valve):
                end = odd and v in (0, valve - 1)
                pairs.append((number(b, v), number(b ^ 1, v) if end else number(b, swap[v])))
        plans.append(pairs)
    return plans


def exchange(faces, plans):
    return [lax.ppermute(face, ("bulk", "valve"), plan) for face, plan in zip(faces, plans)]


def low_high(flip, even, odd):
    return jnp.where(flip == 0, odd, even), jnp.where(flip == 0, even, odd)


def own_faces(info, grid, axis_x, messages):
    faces = []
    for c in range(NVAR):
        sides = []
        for axis, rows in ((axis_x, slice(0, BY)), (1 - axis_x, slice(BY, FACE))):
            even, odd = messages[2 * axis], messages[2 * axis + 1]
            sides += low_high(info[axis] % 2, even[c, rows, :], odd[c, rows, :])
        faces.append(sides)
    return faces


def arrived_faces(info, axis_x, messages):
    faces = own_faces(info, None, axis_x, messages)
    for c in range(NVAR):
        for at, axis in ((0, axis_x), (2, 1 - axis_x)):
            faces[c][at] = jnp.where(info[axis] > 0, faces[c][at], 0.0)
            faces[c][at + 1] = jnp.where(info[axis] < info[2 + axis] - 1, faces[c][at + 1], 0.0)
    return faces


def send_faces(info, axis_x, faces, messages):
    for c in range(NVAR):
        for at, axis, rows in ((0, axis_x, slice(0, BY)), (2, 1 - axis_x, slice(BY, FACE))):
            low, high = faces[c][at : at + 2]
            even = info[axis] % 2 == 0
            messages[2 * axis][c, rows, :] = jnp.where(even, high, low)
            messages[2 * axis + 1][c, rows, :] = jnp.where(even, low, high)


def block_face(ref, c, side):
    if side == 0:
        return ref[c, 0:BY, :]
    if side == 1:
        return ref[c, PLANES - BY : PLANES, :]
    return ref[c, pl.ds(0 if side == 2 else BY - 1, BX, stride=BY), :]


def swept_faces(info, flux, axis_x, inner, velocity, blanking, messages):
    halos = arrived_faces(info, axis_x, messages)
    shares = []
    for side in range(4):
        d, sign = side // 2, 2.0 * (side % 2) - 1.0
        vel = [block_face(velocity, k, side) for k in range(3)]
        speed = 1.0 + (vel[0] * vel[0] + vel[1] * vel[1] + vel[2] * vel[2])
        slope = (0.5 * sign) * lax.rsqrt(speed) * vel[d]
        scale = 1.0 / 12.0
        if blanking is not None:
            scale = block_face(blanking, 0, side).astype(jnp.float32) * scale
        mixed = [slope * halos[j][side] for j in range(NVAR)]
        share = []
        for i in range(NVAR):
            total = halos[i][side]
            for j in range(NVAR):
                total = total + flux[d, j, i] * mixed[j]
            share.append(scale * total)
        shares.append(share)
    x_row = lax.broadcasted_iota(jnp.int32, (BY, BZ), 0)
    y_row = lax.broadcasted_iota(jnp.int32, (BX, BZ), 0)
    faces = []
    for c in range(NVAR):
        xs = [block_face(inner, c, side) + shares[side][c] for side in range(2)]
        ys = [block_face(inner, c, side) + shares[side][c] for side in range(2, 4)]
        for k, at in enumerate((0, BX - 1)):
            for m, row in enumerate((0, BY - 1)):
                xs[k] = xs[k] + jnp.where(x_row == row, shares[2 + m][c][at : at + 1, :], 0.0)
                ys[m] = ys[m] + jnp.where(y_row == at, shares[k][c][row : row + 1, :], 0.0)
        faces.append(xs + ys)
    return faces


def loads(pairs, sem):
    copies = []
    for source, target in pairs:
        part = []
        for c in range(source.shape[0]):
            at = sum(map(len, copies)) + c
            part.append(pltpu.make_async_copy(source.at[c], target.at[c], sem.at[at]))
        copies.append(part)
    return copies


def each(copies, act):
    for part in copies:
        for copy in part:
            getattr(copy, act)()


def first_kernel(info, bg, va, *refs):
    messages, bg_here, va_here, sem = refs[:4], refs[4], refs[5], refs[6]
    copies = loads([(bg, bg_here), (va, va_here)], sem)
    each(copies, "start")
    for axis_x, grid in ((0, bg_here), (1, va_here)):
        each(copies[axis_x : axis_x + 1], "wait")
        faces = [[block_face(grid, c, side) for side in range(4)] for c in range(NVAR)]
        send_faces(info, axis_x, faces, messages)


def first_faces(info, bg, va):
    return pl.pallas_call(
        first_kernel,
        out_shape=[f32(NVAR, FACE, BZ)] * 4 + [f32(NVAR, PLANES, BZ)] * 2,
        in_specs=[SMEM, HBM, HBM],
        out_specs=[VMEM] * 6,
        scratch_shapes=[pltpu.SemaphoreType.DMA((2 * NVAR,))],
        compiler_params=params(4),
        name="first_faces",
    )(info, in_hbm(bg), in_hbm(va))


def faces_kernel(info, flux, bg, bg_velocity, blanking, va, va_velocity, *messages):
    arrived, sends = messages[:4], messages[4:]
    faces = swept_faces(info, flux, 0, bg, bg_velocity, blanking, arrived)
    send_faces(info, 0, faces, sends)
    faces = swept_faces(info, flux, 1, va, va_velocity, None, arrived)
    send_faces(info, 1, faces, sends)


def next_faces(info, flux, bg, bg_velocity, blanking, va, va_velocity, arrived):
    return pl.pallas_call(
        faces_kernel,
        out_shape=[f32(NVAR, FACE, BZ)] * 4,
        in_specs=[SMEM, SMEM] + [VMEM] * 9,
        out_specs=[VMEM] * 4,
        compiler_params=params(4),
        name="next_faces",
    )(info, flux, bg, bg_velocity, blanking, va, va_velocity, *arrived)


def fill_padded(faces, grid, padded):
    edge = jnp.zeros((1, BZ), jnp.float32)
    plane = jnp.zeros((BY, BZ), jnp.float32)
    inside = slice(8, 8 + BY)
    for c in range(NVAR):
        padded[c, 0, inside, :] = plane
        padded[c, BX + 1, inside, :] = plane
        for x in range(BX):
            if 0 < x < BX - 1:
                padded[c, x + 1, inside, :] = grid[c, x * BY : (x + 1) * BY, :]
            else:
                padded[c, x + 1, inside, :] = faces[c][0 if x == 0 else 1]
            padded[c, x + 1, 7:8, :] = edge
            padded[c, x + 1, 8:9, :] = faces[c][2][x : x + 1, :]
            padded[c, x + 1, 7 + BY : 8 + BY, :] = faces[c][3][x : x + 1, :]
            padded[c, x + 1, 8 + BY : 9 + BY, :] = edge


def sweep(flux, padded, velocity, source, blanking, out):
    rows = 16
    depth = lax.broadcasted_iota(jnp.int32, (rows, BZ), 1)
    first, last = depth == 0, depth == BZ - 1

    def plane(x, carry):
        for part in range(BY // rows):
            y = part * rows
            here = pl.ds(pl.multiple_of(x * BY + y, rows), rows)
            vel = [velocity[d, here, :] for d in range(3)]
            speed = 1.0 + (vel[0] * vel[0] + vel[1] * vel[1] + vel[2] * vel[2])
            half = 0.5 * lax.rsqrt(speed)
            acc = [source[i, here, :] for i in range(NVAR)]
            for d in range(3):
                slope = half * vel[d]
                mixed = []
                for j in range(NVAR):
                    if d == 0:
                        low = padded[j, x, y + 8 : y + 8 + rows, :]
                        high = padded[j, x + 2, y + 8 : y + 8 + rows, :]
                    elif d == 1:
                        low = padded[j, x + 1, y + 7 : y + 7 + rows, :]
                        high = padded[j, x + 1, y + 9 : y + 9 + rows, :]
                    else:
                        mid = padded[j, x + 1, y + 8 : y + 8 + rows, :]
                        low = jnp.where(first, 0.0, pltpu.roll(mid, 1, 1))
                        high = jnp.where(last, 0.0, pltpu.roll(mid, BZ - 1, 1))
                    acc[j] = acc[j] + (low + high)
                    mixed.append(slope * (high - low))
                for i in range(NVAR):
                    for j in range(NVAR):
                        acc[i] = acc[i] + flux[d, j, i] * mixed[j]
            scale = 1.0 / 12.0
            if blanking is not None:
                scale = blanking[0, here, :].astype(jnp.float32) * scale
            for i in range(NVAR):
                out[i, here, :] = scale * acc[i]
        return carry

    lax.fori_loop(0, BX, plane, 0)


def sweep_kernel(info, flux, *refs):
    bg, bg_velocity, bg_source, blanking, va, va_velocity, va_source = refs[:7]
    messages, (bg_out, va_out, bg_padded, va_padded) = refs[7:11], refs[11:]
    fill_padded(own_faces(info, bg, 0, messages), bg, bg_padded)
    fill_padded(own_faces(info, va, 1, messages), va, va_padded)
    sweep(flux, bg_padded, bg_velocity, bg_source, blanking, bg_out)
    sweep(flux, va_padded, va_velocity, va_source, None, va_out)


def first_sweep_kernel(info, flux, bg, va, *refs):
    fixed, messages, outs = refs[:5], refs[5:9], refs[9:]
    bg_out, va_out, here = outs[0], outs[1], outs[2:7]
    bg_padded, va_padded, sem = outs[7:]
    copies = loads(list(zip(fixed, here)), sem)
    each(copies, "start")
    fill_padded(own_faces(info, bg, 0, messages), bg, bg_padded)
    fill_padded(own_faces(info, va, 1, messages), va, va_padded)
    each(copies[:3], "wait")
    sweep(flux, bg_padded, here[0], here[1], here[2], bg_out)
    each(copies[3:], "wait")
    sweep(flux, va_padded, here[3], here[4], None, va_out)


def sweep_cost():
    cells = BX * BY * BZ
    return pl.CostEstimate(flops=2 * cells * 230, bytes_accessed=4 * cells * 37, transcendentals=2 * cells)


def padded_scratch():
    return [pltpu.VMEM((NVAR, BX + 2, BY + 16, BZ), jnp.float32)] * 2


def first_sweep(info, flux, bg, va, bg_fixed, va_fixed, messages):
    fixed = (*bg_fixed, *va_fixed)
    outs = pl.pallas_call(
        first_sweep_kernel,
        out_shape=[f32(NVAR, PLANES, BZ)] * 2 + [jax.ShapeDtypeStruct(x.shape, x.dtype) for x in fixed],
        in_specs=[SMEM, SMEM] + [VMEM] * 2 + [HBM] * 5 + [VMEM] * 4,
        out_specs=[VMEM] * 7,
        scratch_shapes=padded_scratch() + [pltpu.SemaphoreType.DMA((sum(x.shape[0] for x in fixed),))],
        compiler_params=params(8),
        cost_estimate=sweep_cost(),
        name="first_sweep",
    )(info, flux, bg, va, *map(in_hbm, fixed), *messages)
    return outs[0], outs[1], tuple(outs[2:5]), tuple(outs[5:7])


def sweep_inner(info, flux, bg, va, messages):
    return pl.pallas_call(
        sweep_kernel,
        out_shape=[f32(NVAR, PLANES, BZ)] * 2,
        in_specs=[SMEM, SMEM] + [VMEM] * 11,
        out_specs=[VMEM] * 2,
        scratch_shapes=padded_scratch(),
        compiler_params=params(8),
        cost_estimate=sweep_cost(),
        name="sweep_inner",
    )(info, flux, *bg, *va, *messages)


def add_faces(faces, inner, out):
    for c in range(NVAR):
        out[c, BY : PLANES - BY, :] = inner[c, BY : PLANES - BY, :]
        out[c, 0:BY, :] = faces[c][0]
        out[c, PLANES - BY : PLANES, :] = faces[c][1]
        for side in (2, 3):
            for x in range(1, BX - 1):
                row = x * BY + (0 if side == 2 else BY - 1)
                out[c, row : row + 1, :] = faces[c][side][x : x + 1, :]


def parts_of(value):
    high = value.astype(jnp.bfloat16)
    return high, (value - high.astype(jnp.float32)).astype(jnp.bfloat16)


def pick_kernel(group, info, flux, inner, velocity, *refs):
    arrived, (count, cells, base, weight) = refs[:4], refs[4:8]
    valve, payload, done, table, hits, next_hits, cells_here, base_here, weight_here, sem = refs[8:]
    owners = cells.shape[0]
    loaded = loads([(weight, weight_here)], sem)
    loaded += [[pltpu.make_async_copy(cells, cells_here, sem.at[8])]]
    loaded += [[pltpu.make_async_copy(base, base_here, sem.at[9])]]
    each(loaded, "start")
    add_faces(swept_faces(info, flux, 1, inner, velocity, None, arrived), inner, done)
    stored = [[pltpu.make_async_copy(done, valve, sem.at[10])]]
    each(stored, "start")
    for v in range(NVAR):
        across = done[v].T
        high, low = parts_of(across)
        table[v * BZ : (v + 1) * BZ, 0:PLANES] = high
        table[v * BZ : (v + 1) * BZ, PLANES : 2 * PLANES] = low
    each(loaded, "wait")
    plane_at = lax.broadcasted_iota(jnp.int32, (PLANES, CAP), 0)
    depth_at = lax.broadcasted_iota(jnp.int32, (BZ, CAP), 0)
    slot_at = lax.broadcasted_iota(jnp.int32, (1, CAP), 1)
    steps = owners // group

    def find(index, target):
        for k in range(group):
            plane = lax.shift_right_logical(cells_here[pl.ds(index * group + k, 1), :], 7)
            hit = jnp.where(plane_at == plane, 1.0, 0.0).astype(jnp.bfloat16)
            target[0:PLANES, k * CAP : (k + 1) * CAP] = hit
            target[PLANES:, k * CAP : (k + 1) * CAP] = hit

    def fetch(source):
        return jnp.dot(table[...], source[...], preferred_element_type=jnp.float32)

    def put(index, rows):
        for k in range(group):
            owner = index * group + k
            here = depth_at == jnp.bitwise_and(cells_here[pl.ds(owner, 1), :], BZ - 1)
            live = slot_at < count[0, owner]
            for v in range(NVAR):
                row = rows[v * BZ : (v + 1) * BZ, k * CAP : (k + 1) * CAP]
                value = jnp.sum(jnp.where(here, row, 0.0), axis=0, keepdims=True)
                payload[owner, 8 + v : 9 + v, :] = jnp.where(live, value, 0.0)
            for corner in range(8):
                payload[owner, corner : corner + 1, :] = weight_here[corner, pl.ds(owner, 1), :]
            payload[owner, 13:14, :] = base_here[pl.ds(owner, 1), :].astype(jnp.float32)
            payload[owner, 14:16, :] = jnp.zeros((2, CAP), jnp.float32)

    find(0, hits)

    def step(pair, carry):
        one, two = 2 * pair, 2 * pair + 1
        rows_one = fetch(hits)
        find(two, next_hits)
        rows_two = fetch(next_hits)
        put(one, rows_one)
        find(jnp.minimum(two + 1, steps - 1), hits)
        put(two, rows_two)
        return carry

    lax.fori_loop(0, steps // 2, step, 0)
    each(stored, "wait")


def pick(info, flux, inner, velocity, arrived, count, cells, base, weight):
    owners = cells.shape[0]
    group = 4 if owners % 8 == 0 else 1
    slots = group * CAP
    return pl.pallas_call(
        functools.partial(pick_kernel, group),
        out_shape=[f32(NVAR, PLANES, BZ), f32(owners, SEND_ROWS, CAP)],
        in_specs=[SMEM, SMEM] + [VMEM] * 6 + [SMEM] + [HBM] * 3,
        out_specs=[HBM, VMEM],
        scratch_shapes=[
            pltpu.VMEM((NVAR, PLANES, BZ), jnp.float32),
            pltpu.VMEM((NVAR * BZ, 2 * PLANES), jnp.bfloat16),
            pltpu.VMEM((2 * PLANES, slots), jnp.bfloat16),
            pltpu.VMEM((2 * PLANES, slots), jnp.bfloat16),
            pltpu.VMEM(cells.shape, jnp.int32),
            pltpu.VMEM(base.shape, jnp.int32),
            pltpu.VMEM(weight.shape, jnp.float32),
            pltpu.SemaphoreType.DMA((11,)),
        ],
        compiler_params=params(20),
        name="pick",
    )(info, flux, inner, velocity, *arrived, in_hbm(count), in_hbm(cells), in_hbm(base), in_hbm(weight))


def scatter_kernel(group, info, flux, inner, velocity, blanking, *refs):
    arrived, received = refs[:4], refs[4]
    out, swept, total, spread, placed, next_spread, next_placed, sem = refs[5:]
    width = group * CAP
    steps = received.shape[0] // group
    tile = 16
    plane_at = lax.broadcasted_iota(jnp.int32, (PLANES // tile, tile, CAP), 0) * tile
    plane_at = plane_at + lax.broadcasted_iota(jnp.int32, (PLANES // tile, tile, CAP), 1)
    plane_at = plane_at.astype(jnp.float32).astype(jnp.bfloat16)
    depth_at = plane_at[: BZ // tile]
    zero = jnp.zeros((), jnp.bfloat16)

    def wide(row):
        return jnp.broadcast_to(row, (tile, CAP)).astype(jnp.bfloat16)[None]

    def wide_parts(row):
        high = row.astype(jnp.bfloat16).astype(jnp.float32)
        return wide(high), wide(row - high)

    def build(index, spread, placed):
        for k in range(group):
            sender = index * group + k
            cols = [slice(part * width + k * CAP, part * width + (k + 1) * CAP) for part in range(2)]
            anchor = received[sender, 13:14, :].astype(jnp.int32)
            plane = lax.shift_right_logical(anchor, 7)
            at = [plane_at == wide((plane + (i * BY + j)).astype(jnp.float32)) for i in range(2) for j in range(2)]
            for step_z in range(2):
                rows = slice(step_z * PLANES, (step_z + 1) * PLANES)
                high = low = zero
                for corner in range(4):
                    row = 2 * corner + step_z
                    high_row, low_row = wide_parts(received[sender, row : row + 1, :])
                    high = jnp.where(at[corner], high_row, high)
                    low = jnp.where(at[corner], low_row, low)
                spread[rows, cols[0]] = low.reshape(PLANES, CAP)
                spread[rows, cols[1]] = high.reshape(PLANES, CAP)
            here = depth_at == wide(jnp.bitwise_and(anchor, BZ - 1).astype(jnp.float32))
            for v in range(NVAR):
                rows = slice(v * BZ, (v + 1) * BZ)
                high_row, low_row = wide_parts(received[sender, 8 + v : 9 + v, :])
                placed[rows, cols[0]] = jnp.where(here, high_row, zero).reshape(BZ, CAP)
                placed[rows, cols[1]] = jnp.where(here, low_row, zero).reshape(BZ, CAP)

    def add(spread, placed):
        dims = (((1,), (1,)), ((), ()))
        high = placed[:, :width]
        both = jnp.concatenate([high, high], axis=1)
        product = lax.dot_general(both, spread[...], dims, preferred_element_type=jnp.float32)
        product = product + lax.dot_general(
            placed[:, width:], spread[:, width:], dims, preferred_element_type=jnp.float32
        )
        total[...] += product

    add_faces(swept_faces(info, flux, 0, inner, velocity, blanking, arrived), inner, swept)
    total[...] = jnp.zeros_like(total)
    build(0, spread, placed)

    def step(pair, carry):
        two = 2 * pair + 1
        add(spread, placed)
        build(two, next_spread, next_placed)
        add(next_spread, next_placed)
        build(jnp.minimum(two + 1, steps - 1), spread, placed)
        return carry

    lax.fori_loop(0, steps // 2, step, 0)
    depth = lax.broadcasted_iota(jnp.int32, (BZ, PLANES), 0)
    stored = [[pltpu.make_async_copy(swept.at[v], out.at[v], sem.at[v])] for v in range(NVAR)]
    for v in range(NVAR):
        rows = slice(v * BZ, (v + 1) * BZ)
        upper = jnp.where(depth == 0, 0.0, pltpu.roll(total[rows, PLANES:], 1, 0))
        swept[v] = swept[v] + (total[rows, :PLANES] + upper).T
        each(stored[v : v + 1], "start")
    each(stored, "wait")


def scatter(info, flux, inner, velocity, blanking, arrived, received):
    senders = received.shape[0]
    group = 4 if senders % 8 == 0 else 1
    columns = 2 * group * CAP
    return pl.pallas_call(
        functools.partial(scatter_kernel, group),
        out_shape=f32(NVAR, PLANES, BZ),
        in_specs=[SMEM, SMEM] + [VMEM] * 8,
        out_specs=HBM,
        scratch_shapes=[
            pltpu.VMEM((NVAR, PLANES, BZ), jnp.float32),
            pltpu.VMEM((NVAR * BZ, 2 * PLANES), jnp.float32),
            pltpu.VMEM((2 * PLANES, columns), jnp.bfloat16),
            pltpu.VMEM((NVAR * BZ, columns), jnp.bfloat16),
            pltpu.VMEM((2 * PLANES, columns), jnp.bfloat16),
            pltpu.VMEM((NVAR * BZ, columns), jnp.bfloat16),
            pltpu.SemaphoreType.DMA((NVAR,)),
        ],
        compiler_params=params(32),
        name="scatter",
    )(info, flux, inner, velocity, blanking, *arrived, received)


def body(
    bulk,
    valve,
    bg_adjoint,
    bg_velocity,
    bg_source,
    bg_iblank,
    valve_adjoint,
    valve_velocity,
    valve_source,
    flux_mix,
    rec_cell,
    donor_base,
    donor_weight,
    slot_count,
):
    plans = face_plans(bulk, valve)
    info = jnp.stack(
        [lax.axis_index("bulk"), lax.axis_index("valve"), jnp.int32(bulk), jnp.int32(valve)]
    ).astype(jnp.int32)
    flat = lambda block: block.reshape(-1, PLANES, BZ)
    bg, va = flat(bg_adjoint), flat(valve_adjoint)
    bg_fixed = (flat(bg_velocity), flat(bg_source), flat(bg_iblank))
    va_fixed = (flat(valve_velocity), flat(valve_source))
    *faces, bg, va = first_faces(info, bg, va)
    for repeat in range(ITERS):
        arrived = exchange(faces, plans)
        if repeat == 0:
            bg, va, bg_fixed, va_fixed = first_sweep(info, flux_mix, bg, va, bg_fixed, va_fixed, faces)
        else:
            bg, va = sweep_inner(info, flux_mix, (bg, *bg_fixed), (va, *va_fixed), faces)
        if repeat < ITERS - 1:
            faces = next_faces(info, flux_mix, bg, bg_fixed[0], bg_fixed[2], va, va_fixed[0], arrived)
    va, payload = pick(
        info, flux_mix, va, va_fixed[0], arrived, slot_count, rec_cell[0], donor_base[0], donor_weight[:, 0]
    )
    received = lax.all_to_all(payload, ("bulk", "valve"), split_axis=0, concat_axis=0, tiled=True)
    bg = scatter(info, flux_mix, bg, bg_fixed[0], bg_fixed[2], arrived, received)
    return (bg.reshape(bg_adjoint.shape), va.reshape(valve_adjoint.shape))


def solution(mesh):
    placed = (
        P(None, "bulk", "valve", None),
        P(None, "bulk", "valve", None),
        P(None, "bulk", "valve", None),
        P("bulk", "valve", None),
        P(None, "valve", "bulk", None),
        P(None, "valve", "bulk", None),
        P(None, "valve", "bulk", None),
        P(),
        P(("bulk", "valve"), None, None),
        P(("bulk", "valve"), None, None),
        P(None, ("bulk", "valve"), None, None),
        P(("bulk", "valve"), None),
    )
    return jax.shard_map(
        functools.partial(body, mesh.shape["bulk"], mesh.shape["valve"]),
        mesh=mesh,
        in_specs=placed,
        out_specs=(P(None, "bulk", "valve", None), P(None, "valve", "bulk", None)),
        check_vma=False,
    )
```

time: 95.4 us -> 74.8 us (0.78)
  waiting for transfers between devices: 25.9 us -> 2.18 us
  blocking collectives: 0 us -> 14.7 us
  local copies, waits for them, and re-layouts: 7.53 us -> 0.01 us
  starting transfers between devices: 21.1 us -> 16.5 us
    ppermute x16, waiting for transfers between devices: 17.6 us -> 2.18 us  [exchange(): lax.ppermute(face, ('bulk', 'valve'), plan)]
    all_to_all x0 -> x1, blocking collectives: none -> 14.7 us  [body(): lax.all_to_all(payload, ('bulk', 'valve'), split_axis=0, concat_axis=0, t...]
    all_to_all x1 -> x0, waiting for transfers between devices: 8.38 us -> none  [body(): lax.all_to_all(payload, ('bulk', 'valve'), split_axis=0, concat_axis=0, t...]
    unnamed x31 -> x3, local copies, waits for them, and re-layouts: 7.53 us -> 0.01 us
    all_to_all x1 -> x0, starting transfers between devices: 5.87 us -> none  [body(): lax.all_to_all(payload, ('bulk', 'valve'), split_axis=0, concat_axis=0, t...]
    ppermute x16, starting transfers between devices: 15.2 us -> 16.5 us  [exchange(): lax.ppermute(face, ('bulk', 'valve'), plan)]
    pallas_call x8 -> x10, Pallas kernels: 39.5 us -> 40.2 us  [the longest x1 12.5 us: scatter(): pl.pallas_call(functools.partial(scatter_kernel, group), out_shape=f32(NV...]
  transfers between devices with their start and end apart: 17 -> 16, of which waited for: 9 -> 3; matrix products, arithmetic and copies ran while one was open for 1% -> 0% of each run, Pallas kernels for 2% -> 22%
where the time goes in v1:
time: 74.8 us; the launch traced here: 74.4 us
  Pallas kernels  40.2 us (54%)
  starting transfers between devices  16.5 us (22%)
  blocking collectives  14.7 us (20%)
  waiting for transfers between devices  2.18 us (3%)
  between operations  0.78 us (1%)
    ppermute x16, starting transfers between devices, exchange(): lax.ppermute(face, ('bulk', 'valve'), plan)  16.5 us
    all_to_all x1, blocking collectives, body(): lax.all_to_all(payload, ('bulk', 'valve'), split_axis=0, concat_axis=0, t...  14.7 us
    pallas_call x1, Pallas kernels, scatter(): pl.pallas_call(functools.partial(scatter_kernel, group), out_shape=f32(NV...  12.5 us
    pallas_call x3, Pallas kernels, sweep_inner(): pl.pallas_call(sweep_kernel, out_shape=[f32(NVAR, PLANES, BZ)] * 2, in_sp...  11 us
    pallas_call x1, Pallas kernels, pick(): pl.pallas_call(functools.partial(pick_kernel, group), out_shape=[f32(NVAR...  6.32 us
    pallas_call x1, Pallas kernels, first_sweep(): pl.pallas_call(first_sweep_kernel, out_shape=[f32(NVAR, PLANES, BZ)] * 2...  5 us
    pallas_call x3, Pallas kernels, next_faces(): pl.pallas_call(faces_kernel, out_shape=[f32(NVAR, FACE, BZ)] * 4, in_spec...  3.32 us
    ppermute x16, waiting for transfers between devices, exchange(): lax.ppermute(face, ('bulk', 'valve'), plan)  2.18 us
  transfers between devices with their start and end apart: 16, of which 3 were waited for; matrix products, arithmetic and copies ran while one was open for 0% of the time, Pallas kernels for 22%

profile of v1, /device:TPU:0, one launch (start us, length us, event | category | flops | bytes accessed | tf_op | source)
XLA Modules:
  0.0 74.4 jit_solution(4687436498187487066)
XLA Ops:
  0.7 2.0 %first_faces.1 = (f32[5,40,128]{2,1,0:T(8,128)S(1)}, f32[5,40,128]{2,1,0:T(8,128)S(1)}, f32[5,40,128]{2,1,0:T(8,128)S(1)}, f32[5,40,128]{2,1,0:T(8,128)S(1)}, f3...) custom-call(s32[4]{0:T(128)S(1)} %pad_add_fusion.info, f32[5,256,128]{2,1,0:T(8,128)} %bitcast.16, ...), custom_call_target="tpu_custom_call" | custom-call | tf_op jit(solution)/shard_map/first_faces/pallas_call | solution.py:164
  2.7 0.5 collective-permute-start
  3.3 2.6 %collective-permute-start.1 = (f32[5,40,128]{2,1,0:T(8,128)S(1)}, f32[5,40,128]{2,1,0:T(8,128)S(1)}, u32[]{:S(2)}, u32[]{:S(2)}) collective-permute-start(f32[5,40,128]{2,1,0:T(8,128)S(1)} %get-tuple-element.38.refs_6_), channel_id=1, source_target_pairs={{0,24},{1,25},{2,26},{3,27},{4,28},{5,29},{6,30},{7,31},{8,16},{9,... | collective-permute-start | bytes 307208 | tf_op jit(solution)/shard_map/ppermute | solution.py:59
  5.9 1.5 %collective-permute-start.2 = (f32[5,40,128]{2,1,0:T(8,128)S(1)}, f32[5,40,128]{2,1,0:T(8,128)S(1)}, u32[]{:S(2)}, u32[]{:S(2)}) collective-permute-start(f32[5,40,128]{2,1,0:T(8,128)S(1)} %get-tuple-element.39.refs_7_), channel_id=1, source_target_pairs={{0,1},{1,0},{2,3},{3,2},{4,5},{5,4},{6,7},{7,6},{8,9},{9,8},{10,11... | collective-permute-start | bytes 307208 | tf_op jit(solution)/shard_map/ppermute | solution.py:59
  7.4 5.0 %first_sweep.1 = (f32[5,256,128]{2,1,0:T(8,128)S(1)}, f32[5,256,128]{2,1,0:T(8,128)S(1)}, f32[3,256,128]{2,1,0:T(8,128)S(1)}, f32[5,256,128]{2,1,0:T(8,128)S(1)}...) custom-call(s32[4]{0:T(128)S(1)} %pad_add_fusion.info, ...), custom_call_target="tpu_custom_call" | custom-call | flops 15073280 | bytes 4849664 | tf_op jit(solution)/shard_map/first_sweep/pallas_call | solution.py:288
  12.5 1.1 %next_faces.3 = (f32[5,40,128]{2,1,0:T(8,128)S(1)}, f32[5,40,128]{2,1,0:T(8,128)S(1)}, f32[5,40,128]{2,1,0:T(8,128)S(1)}, f32[5,40,128]{2,1,0:T(8,128)S(1)}) custom-call(s32[4]{0:T(128)S(1)} %pad_add_fusion.info, f32[3,5,5]{2,1,0:T(8,128)S(1)} %copy.22.flux, f32[5,256,128]{2,1,0:T(8,128)S(1)} %get-tuple-element.41.bg.refs_0_, ...), custom_call_target="tpu_custom_call" | custom-call | tf_op jit(solution)/shard_map/next_faces/pallas_call | solution.py:184
  13.6 0.6 collective-permute-start.4
  14.3 3.0 %collective-permute-start.6 = (f32[5,40,128]{2,1,0:T(8,128)S(1)}, f32[5,40,128]{2,1,0:T(8,128)S(1)}, u32[]{:S(2)}, u32[]{:S(2)}) collective-permute-start(f32[5,40,128]{2,1,0:T(8,128)S(1)} %get-tuple-element.50.refs_9_), channel_id=1, source_target_pairs={{0,1},{1,0},{2,3},{3,2},{4,5},{5,4},{6,7},{7,6},{8,9},{9,8},{10,11... | collective-permute-start | bytes 307208 | tf_op jit(solution)/shard_map/ppermute | solution.py:59
  17.3 3.7 %sweep_inner.3 = (f32[5,256,128]{2,1,0:T(8,128)S(1)}, f32[5,256,128]{2,1,0:T(8,128)S(1)}) custom-call(s32[4]{0:T(128)S(1)} %pad_add_fusion.info, f32[3,5,5]{2,1,0:T(8,128)S(1)} %copy.22.flux, f32[5,256,128]{2,1,0:T(8,128)S(1)} %get-tuple-element.41.bg.refs_0_, f32[3,256,128]{2,1,0:T(8,128)S(1)} %get-tuple-element.42.bg_velocity.refs_1_.velocity, ...), custom_call_target="tpu_custom_call" | custom-call | flops 15073280 | bytes 4849664 | tf_op jit(solution)/shard_map/sweep_inner/pallas_call | solution.py:302
  21.0 0.9 %collective-permute-done.6.messages_2_ = f32[5,40,128]{2,1,0:T(8,128)S(1)} collective-permute-done((f32[5,40,128]{2,1,0:T(8,128)S(1)}, f32[5,40,128]{2,1,0:T(8,128)S(1)}, u32[]{:S(2)}, u32[]{:S(2)}) %collective-permute-start.6) | collective-permute-done | bytes 102432 | tf_op jit(solution)/shard_map/ppermute | solution.py:59
  21.9 1.1 %next_faces.4 = (f32[5,40,128]{2,1,0:T(8,128)S(1)}, f32[5,40,128]{2,1,0:T(8,128)S(1)}, f32[5,40,128]{2,1,0:T(8,128)S(1)}, f32[5,40,128]{2,1,0:T(8,128)S(1)}) custom-call(s32[4]{0:T(128)S(1)} %pad_add_fusion.info, f32[3,5,5]{2,1,0:T(8,128)S(1)} %copy.22.flux, f32[5,256,128]{2,1,0:T(8,128)S(1)} %get-tuple-element.52.bg.refs_0_, ...), custom_call_target="tpu_custom_call" | custom-call | tf_op jit(solution)/shard_map/next_faces/pallas_call | solution.py:184
  23.0 2.5 %collective-permute-start.10 = (f32[5,40,128]{2,1,0:T(8,128)S(1)}, f32[5,40,128]{2,1,0:T(8,128)S(1)}, u32[]{:S(2)}, u32[]{:S(2)}) collective-permute-start(f32[5,40,128]{2,1,0:T(8,128)S(1)} %get-tuple-element.56.refs_9_), channel_id=1, source_target_pairs={{0,1},{1,0},{2,3},{3,2},{4,5},{5,4},{6,7},{7,6},{8,9},{9,8},{10,11... | collective-permute-start | bytes 307208 | tf_op jit(solution)/shard_map/ppermute | solution.py:59
  25.5 0.5 collective-permute-start.8
  26.1 1.1 %collective-permute-start.9 = (f32[5,40,128]{2,1,0:T(8,128)S(1)}, f32[5,40,128]{2,1,0:T(8,128)S(1)}, u32[]{:S(2)}, u32[]{:S(2)}) collective-permute-start(f32[5,40,128]{2,1,0:T(8,128)S(1)} %get-tuple-element.55.refs_8_), channel_id=1, source_target_pairs={{0,24},{1,25},{2,26},{3,27},{4,28},{5,29},{6,30},{7,31},{8,16},{9,... | collective-permute-start | bytes 307208 | tf_op jit(solution)/shard_map/ppermute | solution.py:59
  27.2 3.7 %sweep_inner.4 = (f32[5,256,128]{2,1,0:T(8,128)S(1)}, f32[5,256,128]{2,1,0:T(8,128)S(1)}) custom-call(s32[4]{0:T(128)S(1)} %pad_add_fusion.info, f32[3,5,5]{2,1,0:T(8,128)S(1)} %copy.22.flux, f32[5,256,128]{2,1,0:T(8,128)S(1)} %get-tuple-element.52.bg.refs_0_, f32[3,256,128]{2,1,0:T(8,128)S(1)} %get-tuple-element.42.bg_velocity.refs_1_.velocity, ...), custom_call_target="tpu_custom_call" | custom-call | flops 15073280 | bytes 4849664 | tf_op jit(solution)/shard_map/sweep_inner/pallas_call | solution.py:302
  31.1 1.1 %next_faces.5 = (f32[5,40,128]{2,1,0:T(8,128)S(1)}, f32[5,40,128]{2,1,0:T(8,128)S(1)}, f32[5,40,128]{2,1,0:T(8,128)S(1)}, f32[5,40,128]{2,1,0:T(8,128)S(1)}) custom-call(s32[4]{0:T(128)S(1)} %pad_add_fusion.info, f32[3,5,5]{2,1,0:T(8,128)S(1)} %copy.22.flux, f32[5,256,128]{2,1,0:T(8,128)S(1)} %get-tuple-element.58.bg.refs_0_, ...), custom_call_target="tpu_custom_call" | custom-call | tf_op jit(solution)/shard_map/next_faces/pallas_call | solution.py:184
  32.2 0.4 collective-permute-start.12
  32.6 1.3 %collective-permute-start.13 = (f32[5,40,128]{2,1,0:T(8,128)S(1)}, f32[5,40,128]{2,1,0:T(8,128)S(1)}, u32[]{:S(2)}, u32[]{:S(2)}) collective-permute-start(f32[5,40,128]{2,1,0:T(8,128)S(1)} %get-tuple-element.61.refs_8_), channel_id=1, source_target_pairs={{0,24},{1,25},{2,26},{3,27},{4,28},{5,29},{6,30},{7,31},{8,16},{9,... | collective-permute-start | bytes 307208 | tf_op jit(solution)/shard_map/ppermute | solution.py:59
  33.8 2.1 %collective-permute-start.14 = (f32[5,40,128]{2,1,0:T(8,128)S(1)}, f32[5,40,128]{2,1,0:T(8,128)S(1)}, u32[]{:S(2)}, u32[]{:S(2)}) collective-permute-start(f32[5,40,128]{2,1,0:T(8,128)S(1)} %get-tuple-element.62.refs_9_), channel_id=1, source_target_pairs={{0,1},{1,0},{2,3},{3,2},{4,5},{5,4},{6,7},{7,6},{8,9},{9,8},{10,11... | collective-permute-start | bytes 307208 | tf_op jit(solution)/shard_map/ppermute | solution.py:59
  36.1 3.7 %sweep_inner.5 = (f32[5,256,128]{2,1,0:T(8,128)S(1)}, f32[5,256,128]{2,1,0:T(8,128)S(1)}) custom-call(s32[4]{0:T(128)S(1)} %pad_add_fusion.info, f32[3,5,5]{2,1,0:T(8,128)S(1)} %copy.22.flux, f32[5,256,128]{2,1,0:T(8,128)S(1)} %get-tuple-element.58.bg.refs_0_, f32[3,256,128]{2,1,0:T(8,128)S(1)} %get-tuple-element.42.bg_velocity.refs_1_.velocity, ...), custom_call_target="tpu_custom_call" | custom-call | flops 15073280 | bytes 4849664 | tf_op jit(solution)/shard_map/sweep_inner/pallas_call | solution.py:302
  39.8 1.1 %collective-permute-done.14.refs_2_ = f32[5,40,128]{2,1,0:T(8,128)S(1)} collective-permute-done((f32[5,40,128]{2,1,0:T(8,128)S(1)}, f32[5,40,128]{2,1,0:T(8,128)S(1)}, u32[]{:S(2)}, u32[]{:S(2)}) %collective-permute-start.14) | collective-permute-done | bytes 102432 | tf_op jit(solution)/shard_map/ppermute | solution.py:59
  40.9 6.3 %pick.1 = (f32[5,256,128]{2,1,0:T(8,128)}, f32[32,16,128]{2,1,0:T(8,128)S(1)}) custom-call(s32[4]{0:T(128)S(1)} %pad_add_fusion.info, f32[3,5,5]{2,1,0:T(8,128)S(1)} %copy.22.flux, f32[5,256,128]{2,1,0:T(8,128)S(1)} %get-tuple-element.65.inner, f32[3,256,128]{2,1,0:T(8,128)S(1)} %get-tuple-element.46.va_velocity.refs_5_.velocity, ...), custom_call_target="tpu_custom_call" | custom-call | tf_op jit(solution)/shard_map/pick/pallas_call | solution.py:396
  47.2 14.7 %all_to_all.5.refs_4_ = f32[32,16,128]{2,1,0:T(8,128)S(1)} all-to-all(f32[32,16,128]{2,1,0:T(8,128)S(1)} %get-tuple-element.66), channel_id=1, replica_groups=mesh['bulk'=4,'valve'=8] {'bulk','valve'}, dimensions={0} | all-to-all | bytes 524288 | tf_op jit(solution)/shard_map/all_to_all | solution.py:551
  61.9 12.5 %scatter.1 = f32[5,256,128]{2,1,0:T(8,128)} custom-call(s32[4]{0:T(128)S(1)} %pad_add_fusion.info, f32[3,5,5]{2,1,0:T(8,128)S(1)} %copy.22.flux, f32[5,256,128]{2,1,0:T(8,128)S(1)} %get-tuple-element.64.inner, f32[3,256,128]{2,1,0:T(8,128)S(1)} %get-tuple-element.42.bg_velocity.refs_1_.velocity, s32[1,256,128]{2,1,0:T(8,128)S(1)} %get-tuple-element.44.blanking.refs_3_, ...), custom_call_target="tpu_custom_call" | custom-call | tf_op jit(solution)/shard_map/scatter/pallas_call | solution.py:496
  (23 shorter events, 0.7 us)
Async XLA Ops:
  0.7 6.7 %copy-start = (f32[3,5,5]{2,0,1:T(4,128)S(1)}, f32[3,5,5]{2,0,1:T(4,128)}, u32[]{:S(2)}) copy-start(f32[3,5,5]{2,0,1:T(4,128)} %param.19) | copy-start | bytes 904
  2.7 9.7 %collective-permute-start = (f32[5,40,128]{2,1,0:T(8,128)S(1)}, f32[5,40,128]{2,1,0:T(8,128)S(1)}, u32[]{:S(2)}, u32[]{:S(2)}) collective-permute-start(f32[5,40,128]{2,1,0:T(8,128)S(1)} %get-tuple-element.37.refs_5_), channel_id=1, source_target_pairs={{0,8},{1,9},{2,10},{3,11},{4,12},{5,13},{6,14},{7,15},{8,0},{9,1},... | collective-permute-start | bytes 307208 | tf_op jit(solution)/shard_map/ppermute | solution.py:59
  3.3 9.2 %collective-permute-start.1 = (f32[5,40,128]{2,1,0:T(8,128)S(1)}, f32[5,40,128]{2,1,0:T(8,128)S(1)}, u32[]{:S(2)}, u32[]{:S(2)}) collective-permute-start(f32[5,40,128]{2,1,0:T(8,128)S(1)} %get-tuple-element.38.refs_6_), channel_id=1, source_target_pairs={{0,24},{1,25},{2,26},{3,27},{4,28},{5,29},{6,30},{7,31},{8,16},{9,... | collective-permute-start | bytes 307208 | tf_op jit(solution)/shard_map/ppermute | solution.py:59
  5.9 6.6 %collective-permute-start.2 = (f32[5,40,128]{2,1,0:T(8,128)S(1)}, f32[5,40,128]{2,1,0:T(8,128)S(1)}, u32[]{:S(2)}, u32[]{:S(2)}) collective-permute-start(f32[5,40,128]{2,1,0:T(8,128)S(1)} %get-tuple-element.39.refs_7_), channel_id=1, source_target_pairs={{0,1},{1,0},{2,3},{3,2},{4,5},{5,4},{6,7},{7,6},{8,9},{9,8},{10,11... | collective-permute-start | bytes 307208 | tf_op jit(solution)/shard_map/ppermute | solution.py:59
  7.4 5.0 %collective-permute-start.3 = (f32[5,40,128]{2,1,0:T(8,128)S(1)}, f32[5,40,128]{2,1,0:T(8,128)S(1)}, u32[]{:S(2)}, u32[]{:S(2)}) collective-permute-start(f32[5,40,128]{2,1,0:T(8,128)S(1)} %get-tuple-element.40.refs_8_), channel_id=1, source_target_pairs={{0,8},{1,2},{2,1},{3,4},{4,3},{5,6},{6,5},{7,15},{8,0},{9,10},{10,... | collective-permute-start | bytes 307208 | tf_op jit(solution)/shard_map/ppermute | solution.py:59
  13.6 7.4 %collective-permute-start.4 = (f32[5,40,128]{2,1,0:T(8,128)S(1)}, f32[5,40,128]{2,1,0:T(8,128)S(1)}, u32[]{:S(2)}, u32[]{:S(2)}) collective-permute-start(f32[5,40,128]{2,1,0:T(8,128)S(1)} %get-tuple-element.48.refs_7_), channel_id=1, source_target_pairs={{0,8},{1,9},{2,10},{3,11},{4,12},{5,13},{6,14},{7,15},{8,0},{9,1},... | collective-permute-start | bytes 307208 | tf_op jit(solution)/shard_map/ppermute | solution.py:59
  14.1 6.9 %collective-permute-start.5 = (f32[5,40,128]{2,1,0:T(8,128)S(1)}, f32[5,40,128]{2,1,0:T(8,128)S(1)}, u32[]{:S(2)}, u32[]{:S(2)}) collective-permute-start(f32[5,40,128]{2,1,0:T(8,128)S(1)} %get-tuple-element.49.refs_8_), channel_id=1, source_target_pairs={{0,24},{1,25},{2,26},{3,27},{4,28},{5,29},{6,30},{7,31},{8,16},{9,... | collective-permute-start | bytes 307208 | tf_op jit(solution)/shard_map/ppermute | solution.py:59
  14.3 7.5 %collective-permute-start.6 = (f32[5,40,128]{2,1,0:T(8,128)S(1)}, f32[5,40,128]{2,1,0:T(8,128)S(1)}, u32[]{:S(2)}, u32[]{:S(2)}) collective-permute-start(f32[5,40,128]{2,1,0:T(8,128)S(1)} %get-tuple-element.50.refs_9_), channel_id=1, source_target_pairs={{0,1},{1,0},{2,3},{3,2},{4,5},{5,4},{6,7},{7,6},{8,9},{9,8},{10,11... | collective-permute-start | bytes 307208 | tf_op jit(solution)/shard_map/ppermute | solution.py:59
  17.3 4.6 %collective-permute-start.7 = (f32[5,40,128]{2,1,0:T(8,128)S(1)}, f32[5,40,128]{2,1,0:T(8,128)S(1)}, u32[]{:S(2)}, u32[]{:S(2)}) collective-permute-start(f32[5,40,128]{2,1,0:T(8,128)S(1)} %get-tuple-element.51.refs_10_), channel_id=1, source_target_pairs={{0,8},{1,2},{2,1},{3,4},{4,3},{5,6},{6,5},{7,15},{8,0},{9,10},{10,... | collective-permute-start | bytes 307208 | tf_op jit(solution)/shard_map/ppermute | solution.py:59
  23.0 7.8 %collective-permute-start.10 = (f32[5,40,128]{2,1,0:T(8,128)S(1)}, f32[5,40,128]{2,1,0:T(8,128)S(1)}, u32[]{:S(2)}, u32[]{:S(2)}) collective-permute-start(f32[5,40,128]{2,1,0:T(8,128)S(1)} %get-tuple-element.56.refs_9_), channel_id=1, source_target_pairs={{0,1},{1,0},{2,3},{3,2},{4,5},{5,4},{6,7},{7,6},{8,9},{9,8},{10,11... | collective-permute-start | bytes 307208 | tf_op jit(solution)/shard_map/ppermute | solution.py:59
  25.5 5.3 %collective-permute-start.11 = (f32[5,40,128]{2,1,0:T(8,128)S(1)}, f32[5,40,128]{2,1,0:T(8,128)S(1)}, u32[]{:S(2)}, u32[]{:S(2)}) collective-permute-start(f32[5,40,128]{2,1,0:T(8,128)S(1)} %get-tuple-element.57.refs_10_), channel_id=1, source_target_pairs={{0,8},{1,2},{2,1},{3,4},{4,3},{5,6},{6,5},{7,15},{8,0},{9,10},{10,... | collective-permute-start | bytes 307208 | tf_op jit(solution)/shard_map/ppermute | solution.py:59
  25.5 5.3 %collective-permute-start.8 = (f32[5,40,128]{2,1,0:T(8,128)S(1)}, f32[5,40,128]{2,1,0:T(8,128)S(1)}, u32[]{:S(2)}, u32[]{:S(2)}) collective-permute-start(f32[5,40,128]{2,1,0:T(8,128)S(1)} %get-tuple-element.54.refs_7_), channel_id=1, source_target_pairs={{0,8},{1,9},{2,10},{3,11},{4,12},{5,13},{6,14},{7,15},{8,0},{9,1},... | collective-permute-start | bytes 307208 | tf_op jit(solution)/shard_map/ppermute | solution.py:59
  26.1 5.0 %collective-permute-start.9 = (f32[5,40,128]{2,1,0:T(8,128)S(1)}, f32[5,40,128]{2,1,0:T(8,128)S(1)}, u32[]{:S(2)}, u32[]{:S(2)}) collective-permute-start(f32[5,40,128]{2,1,0:T(8,128)S(1)} %get-tuple-element.55.refs_8_), channel_id=1, source_target_pairs={{0,24},{1,25},{2,26},{3,27},{4,28},{5,29},{6,30},{7,31},{8,16},{9,... | collective-permute-start | bytes 307208 | tf_op jit(solution)/shard_map/ppermute | solution.py:59
  32.2 7.6 %collective-permute-start.12 = (f32[5,40,128]{2,1,0:T(8,128)S(1)}, f32[5,40,128]{2,1,0:T(8,128)S(1)}, u32[]{:S(2)}, u32[]{:S(2)}) collective-permute-start(f32[5,40,128]{2,1,0:T(8,128)S(1)} %get-tuple-element.60.refs_7_), channel_id=1, source_target_pairs={{0,8},{1,9},{2,10},{3,11},{4,12},{5,13},{6,14},{7,15},{8,0},{9,1},... | collective-permute-start | bytes 307208 | tf_op jit(solution)/shard_map/ppermute | solution.py:59
  32.6 7.2 %collective-permute-start.13 = (f32[5,40,128]{2,1,0:T(8,128)S(1)}, f32[5,40,128]{2,1,0:T(8,128)S(1)}, u32[]{:S(2)}, u32[]{:S(2)}) collective-permute-start(f32[5,40,128]{2,1,0:T(8,128)S(1)} %get-tuple-element.61.refs_8_), channel_id=1, source_target_pairs={{0,24},{1,25},{2,26},{3,27},{4,28},{5,29},{6,30},{7,31},{8,16},{9,... | collective-permute-start | bytes 307208 | tf_op jit(solution)/shard_map/ppermute | solution.py:59
  33.8 7.1 %collective-permute-start.14 = (f32[5,40,128]{2,1,0:T(8,128)S(1)}, f32[5,40,128]{2,1,0:T(8,128)S(1)}, u32[]{:S(2)}, u32[]{:S(2)}) collective-permute-start(f32[5,40,128]{2,1,0:T(8,128)S(1)} %get-tuple-element.62.refs_9_), channel_id=1, source_target_pairs={{0,1},{1,0},{2,3},{3,2},{4,5},{5,4},{6,7},{7,6},{8,9},{9,8},{10,11... | collective-permute-start | bytes 307208 | tf_op jit(solution)/shard_map/ppermute | solution.py:59
  35.9 5.0 %collective-permute-start.15 = (f32[5,40,128]{2,1,0:T(8,128)S(1)}, f32[5,40,128]{2,1,0:T(8,128)S(1)}, u32[]{:S(2)}, u32[]{:S(2)}) collective-permute-start(f32[5,40,128]{2,1,0:T(8,128)S(1)} %get-tuple-element.63.refs_10_), channel_id=1, source_target_pairs={{0,8},{1,2},{2,1},{3,4},{4,3},{5,6},{6,5},{7,15},{8,0},{9,10},{10,... | collective-permute-start | bytes 307208 | tf_op jit(solution)/shard_map/ppermute | solution.py:59

commit v2 on v1

--- a/solution.py
+++ b/solution.py
@@ -15,7 +15,10 @@
 BZ = 128
 PLANES = BX * BY
 FACE = BY + BX
-SEND_ROWS = 16
+STEP = BY + 16
+SEND_ROWS = 14
+RUN = 2
+RUNS = BZ // RUN
 
 VMEM = pl.BlockSpec(memory_space=pltpu.VMEM)
 SMEM = pl.BlockSpec(memory_space=pltpu.SMEM)
@@ -56,7 +59,9 @@
 
 
 def exchange(faces, plans):
-    return [lax.ppermute(face, ("bulk", "valve"), plan) for face, plan in zip(faces, plans)]
+    order = (2, 3, 0, 1)
+    arrived = {k: lax.ppermute(faces[k], ("bulk", "valve"), plans[k]) for k in order}
+    return [arrived[k] for k in range(4)]
 
 
 def low_high(flip, even, odd):
@@ -192,63 +197,56 @@
 
 
 def fill_padded(faces, grid, padded):
-    edge = jnp.zeros((1, BZ), jnp.float32)
-    plane = jnp.zeros((BY, BZ), jnp.float32)
-    inside = slice(8, 8 + BY)
+    zeros = jnp.zeros((BY, BZ), jnp.float32)
     for c in range(NVAR):
-        padded[c, 0, inside, :] = plane
-        padded[c, BX + 1, inside, :] = plane
-        for x in range(BX):
-            if 0 < x < BX - 1:
-                padded[c, x + 1, inside, :] = grid[c, x * BY : (x + 1) * BY, :]
+        for x in range(-1, BX + 1):
+            if x in (-1, BX):
+                plane = zeros
+            elif x in (0, BX - 1):
+                plane = faces[c][0 if x == 0 else 1]
             else:
-                padded[c, x + 1, inside, :] = faces[c][0 if x == 0 else 1]
-            padded[c, x + 1, 7:8, :] = edge
-            padded[c, x + 1, 8:9, :] = faces[c][2][x : x + 1, :]
-            padded[c, x + 1, 7 + BY : 8 + BY, :] = faces[c][3][x : x + 1, :]
-            padded[c, x + 1, 8 + BY : 9 + BY, :] = edge
+                plane = grid[c, x * BY : (x + 1) * BY, :]
+            padded[c, (x + 1) * STEP + 8 : (x + 1) * STEP + 8 + BY, :] = plane
+        for row, face in ((7, zeros[:BX]), (8, faces[c][2]), (7 + BY, faces[c][3]), (8 + BY, zeros[:BX])):
+            padded[c, pl.ds(STEP + row, BX, stride=STEP), :] = face
 
 
 def sweep(flux, padded, velocity, source, blanking, out):
-    rows = 16
-    depth = lax.broadcasted_iota(jnp.int32, (rows, BZ), 1)
+    depth = lax.broadcasted_iota(jnp.int32, (BY, BZ), 1)
     first, last = depth == 0, depth == BZ - 1
-
-    def plane(x, carry):
-        for part in range(BY // rows):
-            y = part * rows
-            here = pl.ds(pl.multiple_of(x * BY + y, rows), rows)
-            vel = [velocity[d, here, :] for d in range(3)]
-            speed = 1.0 + (vel[0] * vel[0] + vel[1] * vel[1] + vel[2] * vel[2])
-            half = 0.5 * lax.rsqrt(speed)
-            acc = [source[i, here, :] for i in range(NVAR)]
-            for d in range(3):
-                slope = half * vel[d]
-                mixed = []
+    for x in range(BX):
+        here = slice(x * BY, (x + 1) * BY)
+
+        def near(j, dx, dy):
+            start = (x + 1 + dx) * STEP + 8 + dy
+            return padded[j, start : start + BY, :]
+
+        vel = [velocity[d, here, :] for d in range(3)]
+        speed = 1.0 + (vel[0] * vel[0] + vel[1] * vel[1] + vel[2] * vel[2])
+        half = 0.5 * lax.rsqrt(speed)
+        acc = [source[i, here, :] for i in range(NVAR)]
+        for d in range(3):
+            slope = half * vel[d]
+            mixed = []
+            for j in range(NVAR):
+                if d == 0:
+                    low, high = near(j, -1, 0), near(j, 1, 0)
+                elif d == 1:
+                    low, high = near(j, 0, -1), near(j, 0, 1)
+                else:
+                    mid = near(j, 0, 0)
+                    low = jnp.where(first, 0.0, pltpu.roll(mid, 1, 1))
+                    high = jnp.where(last, 0.0, pltpu.roll(mid, BZ - 1, 1))
+                acc[j] = acc[j] + (low + high)
+                mixed.append(slope * (high - low))
+            for i in range(NVAR):
                 for j in range(NVAR):
-                    if d == 0:
-                        low = padded[j, x, y + 8 : y + 8 + rows, :]
-                        high = padded[j, x + 2, y + 8 : y + 8 + rows, :]
-                    elif d == 1:
-                        low = padded[j, x + 1, y + 7 : y + 7 + rows, :]
-                        high = padded[j, x + 1, y + 9 : y + 9 + rows, :]
-                    else:
-                        mid = padded[j, x + 1, y + 8 : y + 8 + rows, :]
-                        low = jnp.where(first, 0.0, pltpu.roll(mid, 1, 1))
-                        high = jnp.where(last, 0.0, pltpu.roll(mid, BZ - 1, 1))
-                    acc[j] = acc[j] + (low + high)
-                    mixed.append(slope * (high - low))
-                for i in range(NVAR):
-                    for j in range(NVAR):
-                        acc[i] = acc[i] + flux[d, j, i] * mixed[j]
-            scale = 1.0 / 12.0
-            if blanking is not None:
-                scale = blanking[0, here, :].astype(jnp.float32) * scale
-            for i in range(NVAR):
-                out[i, here, :] = scale * acc[i]
-        return carry
-
-    lax.fori_loop(0, BX, plane, 0)
+                    acc[i] = acc[i] + flux[d, j, i] * mixed[j]
+        scale = 1.0 / 12.0
+        if blanking is not None:
+            scale = blanking[0, here, :].astype(jnp.float32) * scale
+        for i in range(NVAR):
+            out[i, here, :] = scale * acc[i]
 
 
 def sweep_kernel(info, flux, *refs):
@@ -280,7 +278,7 @@
 
 
 def padded_scratch():
-    return [pltpu.VMEM((NVAR, BX + 2, BY + 16, BZ), jnp.float32)] * 2
+    return [pltpu.VMEM((NVAR, (BX + 2) * STEP, BZ), jnp.float32)] * 2
 
 
 def first_sweep(info, flux, bg, va, bg_fixed, va_fixed, messages):
@@ -316,10 +314,8 @@
         out[c, BY : PLANES - BY, :] = inner[c, BY : PLANES - BY, :]
         out[c, 0:BY, :] = faces[c][0]
         out[c, PLANES - BY : PLANES, :] = faces[c][1]
-        for side in (2, 3):
-            for x in range(1, BX - 1):
-                row = x * BY + (0 if side == 2 else BY - 1)
-                out[c, row : row + 1, :] = faces[c][side][x : x + 1, :]
+        out[c, pl.ds(0, BX, stride=BY), :] = faces[c][2]
+        out[c, pl.ds(BY - 1, BX, stride=BY), :] = faces[c][3]
 
 
 def parts_of(value):
@@ -329,63 +325,64 @@
 
 def pick_kernel(group, info, flux, inner, velocity, *refs):
     arrived, (count, cells, base, weight) = refs[:4], refs[4:8]
-    valve, payload, done, table, hits, next_hits, cells_here, base_here, weight_here, sem = refs[8:]
+    valve, payload, done, table, hits, next_hits, rows_even, rows_odd, sem = refs[8:]
     owners = cells.shape[0]
-    loaded = loads([(weight, weight_here)], sem)
-    loaded += [[pltpu.make_async_copy(cells, cells_here, sem.at[8])]]
-    loaded += [[pltpu.make_async_copy(base, base_here, sem.at[9])]]
-    each(loaded, "start")
     add_faces(swept_faces(info, flux, 1, inner, velocity, None, arrived), inner, done)
-    stored = [[pltpu.make_async_copy(done, valve, sem.at[10])]]
+    stored = [[pltpu.make_async_copy(done, valve, sem.at[0])]]
     each(stored, "start")
     for v in range(NVAR):
         across = done[v].T
         high, low = parts_of(across)
         table[v * BZ : (v + 1) * BZ, 0:PLANES] = high
         table[v * BZ : (v + 1) * BZ, PLANES : 2 * PLANES] = low
-    each(loaded, "wait")
     plane_at = lax.broadcasted_iota(jnp.int32, (PLANES, CAP), 0)
-    depth_at = lax.broadcasted_iota(jnp.int32, (BZ, CAP), 0)
+    row_at = lax.broadcasted_iota(jnp.int32, (8, CAP), 0)
     slot_at = lax.broadcasted_iota(jnp.int32, (1, CAP), 1)
     steps = owners // group
 
     def find(index, target):
         for k in range(group):
-            plane = lax.shift_right_logical(cells_here[pl.ds(index * group + k, 1), :], 7)
+            plane = lax.shift_right_logical(cells[pl.ds(index * group + k, 1), :], 7)
             hit = jnp.where(plane_at == plane, 1.0, 0.0).astype(jnp.bfloat16)
             target[0:PLANES, k * CAP : (k + 1) * CAP] = hit
             target[PLANES:, k * CAP : (k + 1) * CAP] = hit
 
-    def fetch(source):
-        return jnp.dot(table[...], source[...], preferred_element_type=jnp.float32)
+    def fetch(source, target):
+        target[...] = jnp.dot(table[...], source[...], preferred_element_type=jnp.float32)
 
     def put(index, rows):
         for k in range(group):
             owner = index * group + k
-            here = depth_at == jnp.bitwise_and(cells_here[pl.ds(owner, 1), :], BZ - 1)
+            depth = jnp.bitwise_and(cells[pl.ds(owner, 1), :], BZ - 1)
             live = slot_at < count[0, owner]
-            for v in range(NVAR):
-                row = rows[v * BZ : (v + 1) * BZ, k * CAP : (k + 1) * CAP]
-                value = jnp.sum(jnp.where(here, row, 0.0), axis=0, keepdims=True)
-                payload[owner, 8 + v : 9 + v, :] = jnp.where(live, value, 0.0)
-            for corner in range(8):
-                payload[owner, corner : corner + 1, :] = weight_here[corner, pl.ds(owner, 1), :]
-            payload[owner, 13:14, :] = base_here[pl.ds(owner, 1), :].astype(jnp.float32)
-            payload[owner, 14:16, :] = jnp.zeros((2, CAP), jnp.float32)
+            offset = jnp.broadcast_to(depth, (8, CAP)) - row_at
+            found = [jnp.zeros((8, CAP), jnp.float32)] * NVAR
+            for z in range(0, BZ, 8):
+                here = offset == z
+                for v in range(NVAR):
+                    row = rows[v * BZ + z : v * BZ + z + 8, k * CAP : (k + 1) * CAP]
+                    found[v] = jnp.where(here, row, found[v])
+            parts = [weight[corner, pl.ds(owner, 1), :] for corner in range(8)]
+            parts += [jnp.where(live, jnp.sum(found[v], axis=0, keepdims=True), 0.0) for v in range(NVAR)]
+            parts += [base[pl.ds(owner, 1), :].astype(jnp.float32)]
+            for at, part in enumerate(parts):
+                payload[owner, :, at * CAP : (at + 1) * CAP] = part
 
     find(0, hits)
+    fetch(hits, rows_odd)
 
     def step(pair, carry):
         one, two = 2 * pair, 2 * pair + 1
-        rows_one = fetch(hits)
+        find(one, hits)
+        fetch(hits, rows_even)
+        put(jnp.maximum(one - 1, 0), rows_odd)
         find(two, next_hits)
-        rows_two = fetch(next_hits)
-        put(one, rows_one)
-        find(jnp.minimum(two + 1, steps - 1), hits)
-        put(two, rows_two)
+        fetch(next_hits, rows_odd)
+        put(one, rows_even)
         return carry
 
     lax.fori_loop(0, steps // 2, step, 0)
+    put(steps - 1, rows_odd)
     each(stored, "wait")
 
 
@@ -395,34 +392,33 @@
     slots = group * CAP
     return pl.pallas_call(
         functools.partial(pick_kernel, group),
-        out_shape=[f32(NVAR, PLANES, BZ), f32(owners, SEND_ROWS, CAP)],
-        in_specs=[SMEM, SMEM] + [VMEM] * 6 + [SMEM] + [HBM] * 3,
+        out_shape=[f32(NVAR, PLANES, BZ), f32(owners, 1, SEND_ROWS * CAP)],
+        in_specs=[SMEM, SMEM] + [VMEM] * 6 + [SMEM] + [VMEM] * 3,
         out_specs=[HBM, VMEM],
         scratch_shapes=[
             pltpu.VMEM((NVAR, PLANES, BZ), jnp.float32),
             pltpu.VMEM((NVAR * BZ, 2 * PLANES), jnp.bfloat16),
             pltpu.VMEM((2 * PLANES, slots), jnp.bfloat16),
             pltpu.VMEM((2 * PLANES, slots), jnp.bfloat16),
-            pltpu.VMEM(cells.shape, jnp.int32),
-            pltpu.VMEM(base.shape, jnp.int32),
-            pltpu.VMEM(weight.shape, jnp.float32),
-            pltpu.SemaphoreType.DMA((11,)),
+            pltpu.VMEM((NVAR * BZ, slots), jnp.float32),
+            pltpu.VMEM((NVAR * BZ, slots), jnp.float32),
+            pltpu.SemaphoreType.DMA((1,)),
         ],
         compiler_params=params(20),
         name="pick",
-    )(info, flux, inner, velocity, *arrived, in_hbm(count), in_hbm(cells), in_hbm(base), in_hbm(weight))
+    )(info, flux, inner, velocity, *arrived, in_hbm(count), cells, base, weight)
 
 
 def scatter_kernel(group, info, flux, inner, velocity, blanking, *refs):
     arrived, received = refs[:4], refs[4]
-    out, swept, total, spread, placed, next_spread, next_placed, sem = refs[5:]
+    out, swept, total, across, spread, placed, next_spread, next_placed, sem = refs[5:]
     width = group * CAP
     steps = received.shape[0] // group
     tile = 16
     plane_at = lax.broadcasted_iota(jnp.int32, (PLANES // tile, tile, CAP), 0) * tile
     plane_at = plane_at + lax.broadcasted_iota(jnp.int32, (PLANES // tile, tile, CAP), 1)
     plane_at = plane_at.astype(jnp.float32).astype(jnp.bfloat16)
-    depth_at = plane_at[: BZ // tile]
+    run_at, y_at = plane_at[: RUNS // tile], plane_at[: BY // tile]
     zero = jnp.zeros((), jnp.bfloat16)
 
     def wide(row):
@@ -431,39 +427,52 @@
     def wide_parts(row):
         high = row.astype(jnp.bfloat16).astype(jnp.float32)
         return wide(high), wide(row - high)
+
+    def row(sender, at):
+        return received[sender, :, at * CAP : (at + 1) * CAP]
 
     def build(index, spread, placed):
         for k in range(group):
             sender = index * group + k
             cols = [slice(part * width + k * CAP, part * width + (k + 1) * CAP) for part in range(2)]
-            anchor = received[sender, 13:14, :].astype(jnp.int32)
-            plane = lax.shift_right_logical(anchor, 7)
-            at = [plane_at == wide((plane + (i * BY + j)).astype(jnp.float32)) for i in range(2) for j in range(2)]
-            for step_z in range(2):
-                rows = slice(step_z * PLANES, (step_z + 1) * PLANES)
-                high = low = zero
-                for corner in range(4):
-                    row = 2 * corner + step_z
-                    high_row, low_row = wide_parts(received[sender, row : row + 1, :])
-                    high = jnp.where(at[corner], high_row, high)
-                    low = jnp.where(at[corner], low_row, low)
-                spread[rows, cols[0]] = low.reshape(PLANES, CAP)
-                spread[rows, cols[1]] = high.reshape(PLANES, CAP)
-            here = depth_at == wide(jnp.bitwise_and(anchor, BZ - 1).astype(jnp.float32))
+            anchor = row(sender, 13).astype(jnp.int32)
+            depth = jnp.bitwise_and(anchor, BZ - 1)
+            place = jnp.bitwise_and(depth, RUN - 1)
+            row_y = jnp.bitwise_and(lax.shift_right_logical(anchor, 7), BY - 1)
+            row_x = wide(lax.shift_right_logical(anchor, 12).astype(jnp.float32))
+            at_y = [y_at == wide((row_y + j).astype(jnp.float32)) for j in range(2)]
+            at_x = [row_x == jnp.full((), x, jnp.bfloat16) for x in range(-1, BX)]
+            for spot in range(RUN + 1):
+                along_y = []
+                for i in range(2):
+                    high = low = zero
+                    for j in range(2):
+                        weight = jnp.where(place == spot, row(sender, 4 * i + 2 * j), 0.0)
+                        weight = jnp.where(place == spot - 1, row(sender, 4 * i + 2 * j + 1), weight)
+                        high_row, low_row = wide_parts(weight)
+                        high = jnp.where(at_y[j], high_row, high)
+                        low = jnp.where(at_y[j], low_row, low)
+                    along_y.append((low, high))
+                for x in range(BX):
+                    rows = slice(spot * PLANES + x * BY, spot * PLANES + (x + 1) * BY)
+                    for part in range(2):
+                        value = jnp.where(at_x[x], along_y[1][part], zero)
+                        value = jnp.where(at_x[x + 1], along_y[0][part], value)
+                        spread[rows, cols[part]] = value.reshape(BY, CAP)
+            here = run_at == wide(jnp.right_shift(depth, RUN.bit_length() - 1).astype(jnp.float32))
             for v in range(NVAR):
-                rows = slice(v * BZ, (v + 1) * BZ)
-                high_row, low_row = wide_parts(received[sender, 8 + v : 9 + v, :])
-                placed[rows, cols[0]] = jnp.where(here, high_row, zero).reshape(BZ, CAP)
-                placed[rows, cols[1]] = jnp.where(here, low_row, zero).reshape(BZ, CAP)
+                rows = slice(v * RUNS, (v + 1) * RUNS)
+                high_row, low_row = wide_parts(row(sender, 8 + v))
+                placed[rows, cols[0]] = jnp.where(here, high_row, zero).reshape(RUNS, CAP)
+                placed[rows, cols[1]] = jnp.where(here, low_row, zero).reshape(RUNS, CAP)
 
     def add(spread, placed):
         dims = (((1,), (1,)), ((), ()))
-        high = placed[:, :width]
-        both = jnp.concatenate([high, high], axis=1)
-        product = lax.dot_general(both, spread[...], dims, preferred_element_type=jnp.float32)
-        product = product + lax.dot_general(
-            placed[:, width:], spread[:, width:], dims, preferred_element_type=jnp.float32
-        )
+        high_spread = spread[:, width:]
+        product = lax.dot_general(placed[:, :width], spread[:, :width], dims, preferred_element_type=jnp.float32)
+        values = jnp.concatenate([placed[:, :width], placed[:, width:]], axis=0)
+        both = lax.dot_general(values, high_spread, dims, preferred_element_type=jnp.float32)
+        product = product + (both[: NVAR * RUNS] + both[NVAR * RUNS :])
         total[...] += product
 
     add_faces(swept_faces(info, flux, 0, inner, velocity, blanking, arrived), inner, swept)
@@ -479,12 +488,21 @@
         return carry
 
     lax.fori_loop(0, steps // 2, step, 0)
-    depth = lax.broadcasted_iota(jnp.int32, (BZ, PLANES), 0)
+    run = lax.broadcasted_iota(jnp.int32, (RUNS, PLANES), 0)
     stored = [[pltpu.make_async_copy(swept.at[v], out.at[v], sem.at[v])] for v in range(NVAR)]
     for v in range(NVAR):
-        rows = slice(v * BZ, (v + 1) * BZ)
-        upper = jnp.where(depth == 0, 0.0, pltpu.roll(total[rows, PLANES:], 1, 0))
-        swept[v] = swept[v] + (total[rows, :PLANES] + upper).T
+        rows = slice(v * RUNS, (v + 1) * RUNS)
+        for spot in range(RUN):
+            block = total[rows, spot * PLANES : (spot + 1) * PLANES]
+            if spot == 0:
+                after = pltpu.roll(total[rows, RUN * PLANES :], 1, 0)
+                block = block + jnp.where(run == 0, 0.0, after)
+            for half in range(PLANES // CAP):
+                cols = slice(half * CAP, (half + 1) * CAP)
+                across[half, pl.ds(spot, RUNS, stride=RUN), :] = block[:, cols]
+        for half in range(PLANES // CAP):
+            planes = slice(half * CAP, (half + 1) * CAP)
+            swept[v, planes, :] = swept[v, planes, :] + across[half].T
         each(stored[v : v + 1], "start")
     each(stored, "wait")
 
@@ -500,11 +518,12 @@
         out_specs=HBM,
         scratch_shapes=[
             pltpu.VMEM((NVAR, PLANES, BZ), jnp.float32),
-            pltpu.VMEM((NVAR * BZ, 2 * PLANES), jnp.float32),
-            pltpu.VMEM((2 * PLANES, columns), jnp.bfloat16),
-            pltpu.VMEM((NVAR * BZ, columns), jnp.bfloat16),
-            pltpu.VMEM((2 * PLANES, columns), jnp.bfloat16),
-            pltpu.VMEM((NVAR * BZ, columns), jnp.bfloat16),
+            pltpu.VMEM((NVAR * RUNS, (RUN + 1) * PLANES), jnp.float32),
+            pltpu.VMEM((PLANES // CAP, BZ, CAP), jnp.float32),
+            pltpu.VMEM(((RUN + 1) * PLANES, columns), jnp.bfloat16),
+            pltpu.VMEM((NVAR * RUNS, columns), jnp.bfloat16),
+            pltpu.VMEM(((RUN + 1) * PLANES, columns), jnp.bfloat16),
+            pltpu.VMEM((NVAR * RUNS, columns), jnp.bfloat16),
             pltpu.SemaphoreType.DMA((NVAR,)),
         ],
         compiler_params=params(32),

time: 74.8 us -> 70.7 us (0.945)
  Pallas kernels: 40.2 us -> 35.8 us
  waiting for transfers between devices: 2.18 us -> 3.66 us
  blocking collectives: 14.7 us -> 13.5 us
    pallas_call x1, Pallas kernels: 12.5 us -> 10.6 us  [scatter(): pl.pallas_call(functools.partial(scatter_kernel, group), out_shape=f32(NV...]
    ppermute x16, waiting for transfers between devices: 2.18 us -> 3.66 us  [exchange(): lax.ppermute(faces[k], ('bulk', 'valve'), plans[k])]
    pallas_call x3, Pallas kernels: 11 us -> 9.56 us  [sweep_inner(): pl.pallas_call(sweep_kernel, out_shape=[f32(NVAR, PLANES, BZ)] * 2, in_sp...]
    all_to_all x1, blocking collectives: 14.7 us -> 13.5 us  [body(): lax.all_to_all(payload, ('bulk', 'valve'), split_axis=0, concat_axis=0, t...]
  transfers between devices with their start and end apart: 16 -> 16, of which waited for: 3 -> 3; matrix products, arithmetic and copies ran while one was open for 0% -> 0% of each run, Pallas kernels for 22% -> 20%
where the time goes in v2:
time: 70.7 us; the launch traced here: 70.5 us
  Pallas kernels  35.8 us (51%)
  starting transfers between devices  16.5 us (23%)
  blocking collectives  13.5 us (19%)
  waiting for transfers between devices  3.66 us (5%)
  between operations  0.93 us (1%)
    ppermute x16, starting transfers between devices, exchange(): lax.ppermute(faces[k], ('bulk', 'valve'), plans[k])  16.5 us
    all_to_all x1, blocking collectives, body(): lax.all_to_all(payload, ('bulk', 'valve'), split_axis=0, concat_axis=0, t...  13.5 us
    pallas_call x1, Pallas kernels, scatter(): pl.pallas_call(functools.partial(scatter_kernel, group), out_shape=f32(NV...  10.6 us
    pallas_call x3, Pallas kernels, sweep_inner(): pl.pallas_call(sweep_kernel, out_shape=[f32(NVAR, PLANES, BZ)] * 2, in_sp...  9.56 us
    pallas_call x1, Pallas kernels, pick(): pl.pallas_call(functools.partial(pick_kernel, group), out_shape=[f32(NVAR...  5.84 us
    pallas_call x1, Pallas kernels, first_sweep(): pl.pallas_call(first_sweep_kernel, out_shape=[f32(NVAR, PLANES, BZ)] * 2...  4.48 us
    ppermute x16, waiting for transfers between devices, exchange(): lax.ppermute(faces[k], ('bulk', 'valve'), plans[k])  3.66 us
    pallas_call x3, Pallas kernels, next_faces(): pl.pallas_call(faces_kernel, out_shape=[f32(NVAR, FACE, BZ)] * 4, in_spec...  3.32 us
  transfers between devices with their start and end apart: 16, of which 3 were waited for; matrix products, arithmetic and copies ran while one was open for 0% of the time, Pallas kernels for 20%

profile of v2, /device:TPU:0, one launch (start us, length us, event | category | flops | bytes accessed | tf_op | source)
XLA Modules:
  0.0 70.5 jit_solution(6702326810372813629)
XLA Ops:
  0.7 2.0 %first_faces.1 = (f32[5,40,128]{2,1,0:T(8,128)S(1)}, f32[5,40,128]{2,1,0:T(8,128)S(1)}, f32[5,40,128]{2,1,0:T(8,128)S(1)}, f32[5,40,128]{2,1,0:T(8,128)S(1)}, f3...) custom-call(s32[4]{0:T(128)S(1)} %pad_add_fusion.info, f32[5,256,128]{2,1,0:T(8,128)} %bitcast.19, ...), custom_call_target="tpu_custom_call" | custom-call | tf_op jit(solution)/shard_map/first_faces/pallas_call | solution.py:169
  2.7 0.5 collective-permute-start
  3.3 2.6 %collective-permute-start.1 = (f32[5,40,128]{2,1,0:T(8,128)S(1)}, f32[5,40,128]{2,1,0:T(8,128)S(1)}, u32[]{:S(2)}, u32[]{:S(2)}) collective-permute-start(f32[5,40,128]{2,1,0:T(8,128)S(1)} %get-tuple-element.38.refs_6_), channel_id=1, source_target_pairs={{0,24},{1,25},{2,26},{3,27},{4,28},{5,29},{6,30},{7,31},{8,16},{9,... | collective-permute-start | bytes 307208 | tf_op jit(solution)/shard_map/ppermute | solution.py:63
  5.9 1.5 %collective-permute-start.2 = (f32[5,40,128]{2,1,0:T(8,128)S(1)}, f32[5,40,128]{2,1,0:T(8,128)S(1)}, u32[]{:S(2)}, u32[]{:S(2)}) collective-permute-start(f32[5,40,128]{2,1,0:T(8,128)S(1)} %get-tuple-element.39.refs_7_), channel_id=1, source_target_pairs={{0,1},{1,0},{2,3},{3,2},{4,5},{5,4},{6,7},{7,6},{8,9},{9,8},{10,11... | collective-permute-start | bytes 307208 | tf_op jit(solution)/shard_map/ppermute | solution.py:63
  7.4 4.5 %first_sweep.1 = (f32[5,256,128]{2,1,0:T(8,128)S(1)}, f32[5,256,128]{2,1,0:T(8,128)S(1)}, f32[3,256,128]{2,1,0:T(8,128)S(1)}, f32[5,256,128]{2,1,0:T(8,128)S(1)}...) custom-call(s32[4]{0:T(128)S(1)} %pad_add_fusion.info, ...), custom_call_target="tpu_custom_call" | custom-call | flops 15073280 | bytes 4849664 | tf_op jit(solution)/shard_map/first_sweep/pallas_call | solution.py:286
  12.0 1.1 %next_faces.3 = (f32[5,40,128]{2,1,0:T(8,128)S(1)}, f32[5,40,128]{2,1,0:T(8,128)S(1)}, f32[5,40,128]{2,1,0:T(8,128)S(1)}, f32[5,40,128]{2,1,0:T(8,128)S(1)}) custom-call(s32[4]{0:T(128)S(1)} %pad_add_fusion.info, f32[3,5,5]{2,1,0:T(8,128)S(1)} %copy.22.flux, f32[5,256,128]{2,1,0:T(8,128)S(1)} %get-tuple-element.41.bg.refs_0_, ...), custom_call_target="tpu_custom_call" | custom-call | tf_op jit(solution)/shard_map/next_faces/pallas_call | solution.py:189
  13.1 0.5 collective-permute-start.4
  13.8 3.0 %collective-permute-start.6 = (f32[5,40,128]{2,1,0:T(8,128)S(1)}, f32[5,40,128]{2,1,0:T(8,128)S(1)}, u32[]{:S(2)}, u32[]{:S(2)}) collective-permute-start(f32[5,40,128]{2,1,0:T(8,128)S(1)} %get-tuple-element.50.refs_9_), channel_id=1, source_target_pairs={{0,1},{1,0},{2,3},{3,2},{4,5},{5,4},{6,7},{7,6},{8,9},{9,8},{10,11... | collective-permute-start | bytes 307208 | tf_op jit(solution)/shard_map/ppermute | solution.py:63
  16.8 3.1 %sweep_inner.3 = (f32[5,256,128]{2,1,0:T(8,128)S(1)}, f32[5,256,128]{2,1,0:T(8,128)S(1)}) custom-call(s32[4]{0:T(128)S(1)} %pad_add_fusion.info, f32[3,5,5]{2,1,0:T(8,128)S(1)} %copy.22.flux, f32[5,256,128]{2,1,0:T(8,128)S(1)} %get-tuple-element.41.bg.refs_0_, f32[3,256,128]{2,1,0:T(8,128)S(1)} %get-tuple-element.42.bg_velocity.refs_1_.velocity, ...), custom_call_target="tpu_custom_call" | custom-call | flops 15073280 | bytes 4849664 | tf_op jit(solution)/shard_map/sweep_inner/pallas_call | solution.py:300
  20.0 1.4 %collective-permute-done.6.messages_2_ = f32[5,40,128]{2,1,0:T(8,128)S(1)} collective-permute-done((f32[5,40,128]{2,1,0:T(8,128)S(1)}, f32[5,40,128]{2,1,0:T(8,128)S(1)}, u32[]{:S(2)}, u32[]{:S(2)}) %collective-permute-start.6) | collective-permute-done | bytes 102432 | tf_op jit(solution)/shard_map/ppermute | solution.py:63
  21.4 1.1 %next_faces.4 = (f32[5,40,128]{2,1,0:T(8,128)S(1)}, f32[5,40,128]{2,1,0:T(8,128)S(1)}, f32[5,40,128]{2,1,0:T(8,128)S(1)}, f32[5,40,128]{2,1,0:T(8,128)S(1)}) custom-call(s32[4]{0:T(128)S(1)} %pad_add_fusion.info, f32[3,5,5]{2,1,0:T(8,128)S(1)} %copy.22.flux, f32[5,256,128]{2,1,0:T(8,128)S(1)} %get-tuple-element.52.bg.refs_0_, ...), custom_call_target="tpu_custom_call" | custom-call | tf_op jit(solution)/shard_map/next_faces/pallas_call | solution.py:189
  22.5 2.5 %collective-permute-start.10 = (f32[5,40,128]{2,1,0:T(8,128)S(1)}, f32[5,40,128]{2,1,0:T(8,128)S(1)}, u32[]{:S(2)}, u32[]{:S(2)}) collective-permute-start(f32[5,40,128]{2,1,0:T(8,128)S(1)} %get-tuple-element.56.refs_9_), channel_id=1, source_target_pairs={{0,1},{1,0},{2,3},{3,2},{4,5},{5,4},{6,7},{7,6},{8,9},{9,8},{10,11... | collective-permute-start | bytes 307208 | tf_op jit(solution)/shard_map/ppermute | solution.py:63
  25.0 0.5 collective-permute-start.8
  25.5 1.1 %collective-permute-start.9 = (f32[5,40,128]{2,1,0:T(8,128)S(1)}, f32[5,40,128]{2,1,0:T(8,128)S(1)}, u32[]{:S(2)}, u32[]{:S(2)}) collective-permute-start(f32[5,40,128]{2,1,0:T(8,128)S(1)} %get-tuple-element.55.refs_8_), channel_id=1, source_target_pairs={{0,24},{1,25},{2,26},{3,27},{4,28},{5,29},{6,30},{7,31},{8,16},{9,... | collective-permute-start | bytes 307208 | tf_op jit(solution)/shard_map/ppermute | solution.py:63
  26.6 3.1 %sweep_inner.4 = (f32[5,256,128]{2,1,0:T(8,128)S(1)}, f32[5,256,128]{2,1,0:T(8,128)S(1)}) custom-call(s32[4]{0:T(128)S(1)} %pad_add_fusion.info, f32[3,5,5]{2,1,0:T(8,128)S(1)} %copy.22.flux, f32[5,256,128]{2,1,0:T(8,128)S(1)} %get-tuple-element.52.bg.refs_0_, f32[3,256,128]{2,1,0:T(8,128)S(1)} %get-tuple-element.42.bg_velocity.refs_1_.velocity, ...), custom_call_target="tpu_custom_call" | custom-call | flops 15073280 | bytes 4849664 | tf_op jit(solution)/shard_map/sweep_inner/pallas_call | solution.py:300
  29.8 0.7 %collective-permute-done.9.messages_1_ = f32[5,40,128]{2,1,0:T(8,128)S(1)} collective-permute-done((f32[5,40,128]{2,1,0:T(8,128)S(1)}, f32[5,40,128]{2,1,0:T(8,128)S(1)}, u32[]{:S(2)}, u32[]{:S(2)}) %collective-permute-start.9) | collective-permute-done | bytes 102432 | tf_op jit(solution)/shard_map/ppermute | solution.py:63
  30.5 1.1 %next_faces.5 = (f32[5,40,128]{2,1,0:T(8,128)S(1)}, f32[5,40,128]{2,1,0:T(8,128)S(1)}, f32[5,40,128]{2,1,0:T(8,128)S(1)}, f32[5,40,128]{2,1,0:T(8,128)S(1)}) custom-call(s32[4]{0:T(128)S(1)} %pad_add_fusion.info, f32[3,5,5]{2,1,0:T(8,128)S(1)} %copy.22.flux, f32[5,256,128]{2,1,0:T(8,128)S(1)} %get-tuple-element.58.bg.refs_0_, ...), custom_call_target="tpu_custom_call" | custom-call | tf_op jit(solution)/shard_map/next_faces/pallas_call | solution.py:189
  31.8 1.5 %collective-permute-start.13 = (f32[5,40,128]{2,1,0:T(8,128)S(1)}, f32[5,40,128]{2,1,0:T(8,128)S(1)}, u32[]{:S(2)}, u32[]{:S(2)}) collective-permute-start(f32[5,40,128]{2,1,0:T(8,128)S(1)} %get-tuple-element.61.refs_8_), channel_id=1, source_target_pairs={{0,24},{1,25},{2,26},{3,27},{4,28},{5,29},{6,30},{7,31},{8,16},{9,... | collective-permute-start | bytes 307208 | tf_op jit(solution)/shard_map/ppermute | solution.py:63
  33.3 2.1 %collective-permute-start.14 = (f32[5,40,128]{2,1,0:T(8,128)S(1)}, f32[5,40,128]{2,1,0:T(8,128)S(1)}, u32[]{:S(2)}, u32[]{:S(2)}) collective-permute-start(f32[5,40,128]{2,1,0:T(8,128)S(1)} %get-tuple-element.62.refs_9_), channel_id=1, source_target_pairs={{0,1},{1,0},{2,3},{3,2},{4,5},{5,4},{6,7},{7,6},{8,9},{9,8},{10,11... | collective-permute-start | bytes 307208 | tf_op jit(solution)/shard_map/ppermute | solution.py:63
  35.6 3.3 %sweep_inner.5 = (f32[5,256,128]{2,1,0:T(8,128)S(1)}, f32[5,256,128]{2,1,0:T(8,128)S(1)}) custom-call(s32[4]{0:T(128)S(1)} %pad_add_fusion.info, f32[3,5,5]{2,1,0:T(8,128)S(1)} %copy.22.flux, f32[5,256,128]{2,1,0:T(8,128)S(1)} %get-tuple-element.58.bg.refs_0_, f32[3,256,128]{2,1,0:T(8,128)S(1)} %get-tuple-element.42.bg_velocity.refs_1_.velocity, ...), custom_call_target="tpu_custom_call" | custom-call | flops 15073280 | bytes 4849664 | tf_op jit(solution)/shard_map/sweep_inner/pallas_call | solution.py:300
  38.9 1.4 %collective-permute-done.14.refs_2_ = f32[5,40,128]{2,1,0:T(8,128)S(1)} collective-permute-done((f32[5,40,128]{2,1,0:T(8,128)S(1)}, f32[5,40,128]{2,1,0:T(8,128)S(1)}, u32[]{:S(2)}, u32[]{:S(2)}) %collective-permute-start.14) | collective-permute-done | bytes 102432 | tf_op jit(solution)/shard_map/ppermute | solution.py:63
  40.4 5.8 %pick.1 = (f32[5,256,128]{2,1,0:T(8,128)}, f32[32,1,1792]{2,1,0:T(1,128)S(1)}) custom-call(s32[4]{0:T(128)S(1)} %pad_add_fusion.info, f32[3,5,5]{2,1,0:T(8,128)S(1)} %copy.22.flux, f32[5,256,128]{2,1,0:T(8,128)S(1)} %get-tuple-element.65.inner, f32[3,256,128]{2,1,0:T(8,128)S(1)} %get-tuple-element.46.va_velocity.refs_5_.velocity, ...), custom_call_target="tpu_custom_call" | custom-call | tf_op jit(solution)/shard_map/pick/pallas_call | solution.py:393
  46.2 13.5 %all_to_all.5.refs_4_ = f32[32,1,1792]{2,1,0:T(1,128)S(1)} all-to-all(f32[32,1,1792]{2,1,0:T(1,128)S(1)} %get-tuple-element.66), channel_id=1, replica_groups=mesh['bulk'=4,'valve'=8] {'bulk','valve'}, dimensions={0} | all-to-all | bytes 458752 | tf_op jit(solution)/shard_map/all_to_all | solution.py:570
  59.7 10.6 %scatter.1 = f32[5,256,128]{2,1,0:T(8,128)} custom-call(s32[4]{0:T(128)S(1)} %pad_add_fusion.info, f32[3,5,5]{2,1,0:T(8,128)S(1)} %copy.22.flux, f32[5,256,128]{2,1,0:T(8,128)S(1)} %get-tuple-element.64.inner, f32[3,256,128]{2,1,0:T(8,128)S(1)} %get-tuple-element.42.bg_velocity.refs_1_.velocity, s32[1,256,128]{2,1,0:T(8,128)S(1)} %get-tuple-element.44.blanking.refs_3_, ...), custom_call_target="tpu_custom_call" | custom-call | tf_op jit(solution)/shard_map/scatter/pallas_call | solution.py:514
  (29 shorter events, 0.7 us)
Async XLA Ops:
  0.7 6.7 %copy-start.3 = (f32[3,5,5]{2,0,1:T(4,128)S(1)}, f32[3,5,5]{2,0,1:T(4,128)}, u32[]{:S(2)}) copy-start(f32[3,5,5]{2,0,1:T(4,128)} %param.19) | copy-start | bytes 904
  2.7 9.2 %collective-permute-start = (f32[5,40,128]{2,1,0:T(8,128)S(1)}, f32[5,40,128]{2,1,0:T(8,128)S(1)}, u32[]{:S(2)}, u32[]{:S(2)}) collective-permute-start(f32[5,40,128]{2,1,0:T(8,128)S(1)} %get-tuple-element.37.refs_5_), channel_id=1, source_target_pairs={{0,8},{1,9},{2,10},{3,11},{4,12},{5,13},{6,14},{7,15},{8,0},{9,1},... | collective-permute-start | bytes 307208 | tf_op jit(solution)/shard_map/ppermute | solution.py:63
  3.3 8.7 %collective-permute-start.1 = (f32[5,40,128]{2,1,0:T(8,128)S(1)}, f32[5,40,128]{2,1,0:T(8,128)S(1)}, u32[]{:S(2)}, u32[]{:S(2)}) collective-permute-start(f32[5,40,128]{2,1,0:T(8,128)S(1)} %get-tuple-element.38.refs_6_), channel_id=1, source_target_pairs={{0,24},{1,25},{2,26},{3,27},{4,28},{5,29},{6,30},{7,31},{8,16},{9,... | collective-permute-start | bytes 307208 | tf_op jit(solution)/shard_map/ppermute | solution.py:63
  5.9 6.1 %collective-permute-start.2 = (f32[5,40,128]{2,1,0:T(8,128)S(1)}, f32[5,40,128]{2,1,0:T(8,128)S(1)}, u32[]{:S(2)}, u32[]{:S(2)}) collective-permute-start(f32[5,40,128]{2,1,0:T(8,128)S(1)} %get-tuple-element.39.refs_7_), channel_id=1, source_target_pairs={{0,1},{1,0},{2,3},{3,2},{4,5},{5,4},{6,7},{7,6},{8,9},{9,8},{10,11... | collective-permute-start | bytes 307208 | tf_op jit(solution)/shard_map/ppermute | solution.py:63
  7.4 4.6 %collective-permute-start.3 = (f32[5,40,128]{2,1,0:T(8,128)S(1)}, f32[5,40,128]{2,1,0:T(8,128)S(1)}, u32[]{:S(2)}, u32[]{:S(2)}) collective-permute-start(f32[5,40,128]{2,1,0:T(8,128)S(1)} %get-tuple-element.40.refs_8_), channel_id=1, source_target_pairs={{0,8},{1,2},{2,1},{3,4},{4,3},{5,6},{6,5},{7,15},{8,0},{9,10},{10,... | collective-permute-start | bytes 307208 | tf_op jit(solution)/shard_map/ppermute | solution.py:63
  13.1 6.9 %collective-permute-start.4 = (f32[5,40,128]{2,1,0:T(8,128)S(1)}, f32[5,40,128]{2,1,0:T(8,128)S(1)}, u32[]{:S(2)}, u32[]{:S(2)}) collective-permute-start(f32[5,40,128]{2,1,0:T(8,128)S(1)} %get-tuple-element.48.refs_7_), channel_id=1, source_target_pairs={{0,8},{1,9},{2,10},{3,11},{4,12},{5,13},{6,14},{7,15},{8,0},{9,1},... | collective-permute-start | bytes 307208 | tf_op jit(solution)/shard_map/ppermute | solution.py:63
  13.6 6.3 %collective-permute-start.5 = (f32[5,40,128]{2,1,0:T(8,128)S(1)}, f32[5,40,128]{2,1,0:T(8,128)S(1)}, u32[]{:S(2)}, u32[]{:S(2)}) collective-permute-start(f32[5,40,128]{2,1,0:T(8,128)S(1)} %get-tuple-element.49.refs_8_), channel_id=1, source_target_pairs={{0,24},{1,25},{2,26},{3,27},{4,28},{5,29},{6,30},{7,31},{8,16},{9,... | collective-permute-start | bytes 307208 | tf_op jit(solution)/shard_map/ppermute | solution.py:63
  13.8 7.5 %collective-permute-start.6 = (f32[5,40,128]{2,1,0:T(8,128)S(1)}, f32[5,40,128]{2,1,0:T(8,128)S(1)}, u32[]{:S(2)}, u32[]{:S(2)}) collective-permute-start(f32[5,40,128]{2,1,0:T(8,128)S(1)} %get-tuple-element.50.refs_9_), channel_id=1, source_target_pairs={{0,1},{1,0},{2,3},{3,2},{4,5},{5,4},{6,7},{7,6},{8,9},{9,8},{10,11... | collective-permute-start | bytes 307208 | tf_op jit(solution)/shard_map/ppermute | solution.py:63
  16.8 4.6 %collective-permute-start.7 = (f32[5,40,128]{2,1,0:T(8,128)S(1)}, f32[5,40,128]{2,1,0:T(8,128)S(1)}, u32[]{:S(2)}, u32[]{:S(2)}) collective-permute-start(f32[5,40,128]{2,1,0:T(8,128)S(1)} %get-tuple-element.51.refs_10_), channel_id=1, source_target_pairs={{0,8},{1,2},{2,1},{3,4},{4,3},{5,6},{6,5},{7,15},{8,0},{9,10},{10,... | collective-permute-start | bytes 307208 | tf_op jit(solution)/shard_map/ppermute | solution.py:63
  22.5 7.3 %collective-permute-start.10 = (f32[5,40,128]{2,1,0:T(8,128)S(1)}, f32[5,40,128]{2,1,0:T(8,128)S(1)}, u32[]{:S(2)}, u32[]{:S(2)}) collective-permute-start(f32[5,40,128]{2,1,0:T(8,128)S(1)} %get-tuple-element.56.refs_9_), channel_id=1, source_target_pairs={{0,1},{1,0},{2,3},{3,2},{4,5},{5,4},{6,7},{7,6},{8,9},{9,8},{10,11... | collective-permute-start | bytes 307208 | tf_op jit(solution)/shard_map/ppermute | solution.py:63
  25.0 4.8 %collective-permute-start.11 = (f32[5,40,128]{2,1,0:T(8,128)S(1)}, f32[5,40,128]{2,1,0:T(8,128)S(1)}, u32[]{:S(2)}, u32[]{:S(2)}) collective-permute-start(f32[5,40,128]{2,1,0:T(8,128)S(1)} %get-tuple-element.57.refs_10_), channel_id=1, source_target_pairs={{0,8},{1,2},{2,1},{3,4},{4,3},{5,6},{6,5},{7,15},{8,0},{9,10},{10,... | collective-permute-start | bytes 307208 | tf_op jit(solution)/shard_map/ppermute | solution.py:63
  25.0 4.8 %collective-permute-start.8 = (f32[5,40,128]{2,1,0:T(8,128)S(1)}, f32[5,40,128]{2,1,0:T(8,128)S(1)}, u32[]{:S(2)}, u32[]{:S(2)}) collective-permute-start(f32[5,40,128]{2,1,0:T(8,128)S(1)} %get-tuple-element.54.refs_7_), channel_id=1, source_target_pairs={{0,8},{1,9},{2,10},{3,11},{4,12},{5,13},{6,14},{7,15},{8,0},{9,1},... | collective-permute-start | bytes 307208 | tf_op jit(solution)/shard_map/ppermute | solution.py:63
  25.5 5.0 %collective-permute-start.9 = (f32[5,40,128]{2,1,0:T(8,128)S(1)}, f32[5,40,128]{2,1,0:T(8,128)S(1)}, u32[]{:S(2)}, u32[]{:S(2)}) collective-permute-start(f32[5,40,128]{2,1,0:T(8,128)S(1)} %get-tuple-element.55.refs_8_), channel_id=1, source_target_pairs={{0,24},{1,25},{2,26},{3,27},{4,28},{5,29},{6,30},{7,31},{8,16},{9,... | collective-permute-start | bytes 307208 | tf_op jit(solution)/shard_map/ppermute | solution.py:63
  31.6 7.3 %collective-permute-start.12 = (f32[5,40,128]{2,1,0:T(8,128)S(1)}, f32[5,40,128]{2,1,0:T(8,128)S(1)}, u32[]{:S(2)}, u32[]{:S(2)}) collective-permute-start(f32[5,40,128]{2,1,0:T(8,128)S(1)} %get-tuple-element.60.refs_7_), channel_id=1, source_target_pairs={{0,8},{1,9},{2,10},{3,11},{4,12},{5,13},{6,14},{7,15},{8,0},{9,1},... | collective-permute-start | bytes 307208 | tf_op jit(solution)/shard_map/ppermute | solution.py:63
  31.8 7.1 %collective-permute-start.13 = (f32[5,40,128]{2,1,0:T(8,128)S(1)}, f32[5,40,128]{2,1,0:T(8,128)S(1)}, u32[]{:S(2)}, u32[]{:S(2)}) collective-permute-start(f32[5,40,128]{2,1,0:T(8,128)S(1)} %get-tuple-element.61.refs_8_), channel_id=1, source_target_pairs={{0,24},{1,25},{2,26},{3,27},{4,28},{5,29},{6,30},{7,31},{8,16},{9,... | collective-permute-start | bytes 307208 | tf_op jit(solution)/shard_map/ppermute | solution.py:63
  33.3 7.1 %collective-permute-start.14 = (f32[5,40,128]{2,1,0:T(8,128)S(1)}, f32[5,40,128]{2,1,0:T(8,128)S(1)}, u32[]{:S(2)}, u32[]{:S(2)}) collective-permute-start(f32[5,40,128]{2,1,0:T(8,128)S(1)} %get-tuple-element.62.refs_9_), channel_id=1, source_target_pairs={{0,1},{1,0},{2,3},{3,2},{4,5},{5,4},{6,7},{7,6},{8,9},{9,8},{10,11... | collective-permute-start | bytes 307208 | tf_op jit(solution)/shard_map/ppermute | solution.py:63
  35.4 5.0 %copy-start = (f32[8,1,32,128]{3,2,1,0:T(8,128)S(1)}, f32[8,1,32,128]{3,2,1,0:T(8,128)}, u32[]{:S(2)}) copy-start(f32[8,1,32,128]{3,2,1,0:T(8,128)} %param.22) | copy-start | bytes 393220
  35.4 4.9 %collective-permute-start.15 = (f32[5,40,128]{2,1,0:T(8,128)S(1)}, f32[5,40,128]{2,1,0:T(8,128)S(1)}, u32[]{:S(2)}, u32[]{:S(2)}) collective-permute-start(f32[5,40,128]{2,1,0:T(8,128)S(1)} %get-tuple-element.63.refs_10_), channel_id=1, source_target_pairs={{0,8},{1,2},{2,1},{3,4},{4,3},{5,6},{6,5},{7,15},{8,0},{9,10},{10,... | collective-permute-start | bytes 307208 | tf_op jit(solution)/shard_map/ppermute | solution.py:63
  35.6 4.8 %copy-start.1 = (s32[1,32,128]{2,1,0:T(8,128)S(1)}, s32[1,32,128]{2,1,0:T(8,128)}, u32[]{:S(2)}) copy-start(s32[1,32,128]{2,1,0:T(8,128)} %param.20) | copy-start | bytes 49156
  35.6 4.8 %copy-start.2 = (s32[1,32,128]{2,1,0:T(8,128)S(1)}, s32[1,32,128]{2,1,0:T(8,128)}, u32[]{:S(2)}) copy-start(s32[1,32,128]{2,1,0:T(8,128)} %param.21) | copy-start | bytes 49156

commit v3 on v2

--- a/solution.py
+++ b/solution.py
@@ -19,6 +19,7 @@
 SEND_ROWS = 14
 RUN = 2
 RUNS = BZ // RUN
+PLACE = {(1, 0): 0, (1, 1): 1, (0, 1): 2, (0, 0): 3}
 
 VMEM = pl.BlockSpec(memory_space=pltpu.VMEM)
 SMEM = pl.BlockSpec(memory_space=pltpu.SMEM)
@@ -43,19 +44,17 @@
 
 def face_plans(bulk, valve):
     number = lambda b, v: b * valve + v
-    plans = []
+    cells = [(b, v) for b in range(bulk) for v in range(valve)]
+    plans = {}
     for odd in (0, 1):
-        swap = swap_pairs(bulk, odd)
-        plans.append([(number(b, v), number(swap[b], v)) for b in range(bulk) for v in range(valve)])
-    for odd in (0, 1):
-        swap = swap_pairs(valve, odd)
-        pairs = []
-        for b in range(bulk):
-            for v in range(valve):
-                end = odd and v in (0, valve - 1)
-                pairs.append((number(b, v), number(b ^ 1, v) if end else number(b, swap[v])))
-        plans.append(pairs)
-    return plans
+        along_bulk, along_valve = swap_pairs(bulk, odd), swap_pairs(valve, odd)
+        bulk_pairs, valve_pairs = [], []
+        for b, v in cells:
+            valve_end = odd and v in (0, valve - 1)
+            bulk_pairs.append((number(b, v), number(along_bulk[b], v)))
+            valve_pairs.append((number(b, v), number(b ^ 1, v) if valve_end else number(b, along_valve[v])))
+        plans[0, odd], plans[1, odd] = bulk_pairs, valve_pairs
+    return [plans[key] for key in sorted(PLACE, key=PLACE.get)]
 
 
 def exchange(faces, plans):
@@ -64,37 +63,48 @@
     return [arrived[k] for k in range(4)]
 
 
-def low_high(flip, even, odd):
-    return jnp.where(flip == 0, odd, even), jnp.where(flip == 0, even, odd)
-
-
-def own_faces(info, grid, axis_x, messages):
+def tall(tile, rows):
+    return tile if rows == 8 else jnp.concatenate([tile] * (rows // 8), axis=0)
+
+
+def flags(index, count):
+    return [index % 2 == 0, index > 0, index < count - 1]
+
+
+def flag(info, axis, which, rows):
+    return tall(info[3 * axis + which], rows) != 0
+
+
+def own_faces(info, axis_x, messages):
     faces = []
     for c in range(NVAR):
         sides = []
-        for axis, rows in ((axis_x, slice(0, BY)), (1 - axis_x, slice(BY, FACE))):
-            even, odd = messages[2 * axis], messages[2 * axis + 1]
-            sides += low_high(info[axis] % 2, even[c, rows, :], odd[c, rows, :])
+        for axis, start, size in ((axis_x, 0, BY), (1 - axis_x, BY, BX)):
+            rows = slice(start, start + size)
+            even, odd = messages[PLACE[axis, 0]][c, rows, :], messages[PLACE[axis, 1]][c, rows, :]
+            is_even = flag(info, axis, 0, size)
+            sides += [jnp.where(is_even, odd, even), jnp.where(is_even, even, odd)]
         faces.append(sides)
     return faces
 
 
 def arrived_faces(info, axis_x, messages):
-    faces = own_faces(info, None, axis_x, messages)
+    faces = own_faces(info, axis_x, messages)
     for c in range(NVAR):
-        for at, axis in ((0, axis_x), (2, 1 - axis_x)):
-            faces[c][at] = jnp.where(info[axis] > 0, faces[c][at], 0.0)
-            faces[c][at + 1] = jnp.where(info[axis] < info[2 + axis] - 1, faces[c][at + 1], 0.0)
+        for at, axis, size in ((0, axis_x, BY), (2, 1 - axis_x, BX)):
+            for high in range(2):
+                faces[c][at + high] = jnp.where(flag(info, axis, 1 + high, size), faces[c][at + high], 0.0)
     return faces
 
 
 def send_faces(info, axis_x, faces, messages):
     for c in range(NVAR):
-        for at, axis, rows in ((0, axis_x, slice(0, BY)), (2, 1 - axis_x, slice(BY, FACE))):
+        for at, axis, start, size in ((0, axis_x, 0, BY), (2, 1 - axis_x, BY, BX)):
+            rows = slice(start, start + size)
             low, high = faces[c][at : at + 2]
-            even = info[axis] % 2 == 0
-            messages[2 * axis][c, rows, :] = jnp.where(even, high, low)
-            messages[2 * axis + 1][c, rows, :] = jnp.where(even, low, high)
+            is_even = flag(info, axis, 0, size)
+            messages[PLACE[axis, 0]][c, rows, :] = jnp.where(is_even, high, low)
+            messages[PLACE[axis, 1]][c, rows, :] = jnp.where(is_even, low, high)
 
 
 def block_face(ref, c, side):
@@ -121,7 +131,7 @@
         for i in range(NVAR):
             total = halos[i][side]
             for j in range(NVAR):
-                total = total + flux[d, j, i] * mixed[j]
+                total = total + tall(flux[(d * NVAR + j) * NVAR + i], BY if d == 0 else BX) * mixed[j]
             share.append(scale * total)
         shares.append(share)
     x_row = lax.broadcasted_iota(jnp.int32, (BY, BZ), 0)
@@ -169,7 +179,7 @@
     return pl.pallas_call(
         first_kernel,
         out_shape=[f32(NVAR, FACE, BZ)] * 4 + [f32(NVAR, PLANES, BZ)] * 2,
-        in_specs=[SMEM, HBM, HBM],
+        in_specs=[VMEM, HBM, HBM],
         out_specs=[VMEM] * 6,
         scratch_shapes=[pltpu.SemaphoreType.DMA((2 * NVAR,))],
         compiler_params=params(4),
@@ -189,7 +199,7 @@
     return pl.pallas_call(
         faces_kernel,
         out_shape=[f32(NVAR, FACE, BZ)] * 4,
-        in_specs=[SMEM, SMEM] + [VMEM] * 9,
+        in_specs=[VMEM] * 11,
         out_specs=[VMEM] * 4,
         compiler_params=params(4),
         name="next_faces",
@@ -241,7 +251,7 @@
                 mixed.append(slope * (high - low))
             for i in range(NVAR):
                 for j in range(NVAR):
-                    acc[i] = acc[i] + flux[d, j, i] * mixed[j]
+                    acc[i] = acc[i] + tall(flux[(d * NVAR + j) * NVAR + i], BY) * mixed[j]
         scale = 1.0 / 12.0
         if blanking is not None:
             scale = blanking[0, here, :].astype(jnp.float32) * scale
@@ -252,24 +262,34 @@
 def sweep_kernel(info, flux, *refs):
     bg, bg_velocity, bg_source, blanking, va, va_velocity, va_source = refs[:7]
     messages, (bg_out, va_out, bg_padded, va_padded) = refs[7:11], refs[11:]
-    fill_padded(own_faces(info, bg, 0, messages), bg, bg_padded)
-    fill_padded(own_faces(info, va, 1, messages), va, va_padded)
+    fill_padded(own_faces(info, 0, messages), bg, bg_padded)
+    fill_padded(own_faces(info, 1, messages), va, va_padded)
     sweep(flux, bg_padded, bg_velocity, bg_source, blanking, bg_out)
     sweep(flux, va_padded, va_velocity, va_source, None, va_out)
 
 
 def first_sweep_kernel(info, flux, bg, va, *refs):
-    fixed, messages, outs = refs[:5], refs[5:9], refs[9:]
-    bg_out, va_out, here = outs[0], outs[1], outs[2:7]
-    bg_padded, va_padded, sem = outs[7:]
-    copies = loads(list(zip(fixed, here)), sem)
+    fixed, count, messages, outs = refs[:5], refs[5], refs[6:10], refs[10:]
+    bg_out, va_out, here, wide, live = outs[0], outs[1], outs[2:7], outs[7], outs[8]
+    bg_padded, va_padded, count_here, sem = outs[9:]
+    copies = loads(list(zip(fixed, here)) + [(count, count_here)], sem)
     each(copies, "start")
-    fill_padded(own_faces(info, bg, 0, messages), bg, bg_padded)
-    fill_padded(own_faces(info, va, 1, messages), va, va_padded)
+    fill_padded(own_faces(info, 0, messages), bg, bg_padded)
+    fill_padded(own_faces(info, 1, messages), va, va_padded)
     each(copies[:3], "wait")
-    sweep(flux, bg_padded, here[0], here[1], here[2], bg_out)
+    for d in range(3):
+        for j in range(NVAR):
+            for i in range(NVAR):
+                wide[(d * NVAR + j) * NVAR + i] = jnp.broadcast_to(flux[d, j : j + 1, i : i + 1], (8, BZ))
+    sweep(wide, bg_padded, here[0], here[1], here[2], bg_out)
     each(copies[3:], "wait")
-    sweep(flux, va_padded, here[3], here[4], None, va_out)
+    sweep(wide, va_padded, here[3], here[4], None, va_out)
+    owners = count.shape[-1]
+    counts = jnp.broadcast_to(count_here[0].astype(jnp.float32), (owners, owners))
+    same = lax.broadcasted_iota(jnp.int32, (owners, owners), 0) == lax.broadcasted_iota(jnp.int32, (owners, owners), 1)
+    counts = jnp.sum(jnp.where(same, counts, 0.0), axis=1, keepdims=True)
+    slot_at = lax.broadcasted_iota(jnp.int32, (owners, CAP), 1).astype(jnp.float32)
+    live[...] = jnp.where(slot_at < counts, 1.0, 0.0)
 
 
 def sweep_cost():
@@ -281,26 +301,28 @@
     return [pltpu.VMEM((NVAR, (BX + 2) * STEP, BZ), jnp.float32)] * 2
 
 
-def first_sweep(info, flux, bg, va, bg_fixed, va_fixed, messages):
+def first_sweep(info, flux, bg, va, bg_fixed, va_fixed, count, messages):
     fixed = (*bg_fixed, *va_fixed)
     outs = pl.pallas_call(
         first_sweep_kernel,
-        out_shape=[f32(NVAR, PLANES, BZ)] * 2 + [jax.ShapeDtypeStruct(x.shape, x.dtype) for x in fixed],
-        in_specs=[SMEM, SMEM] + [VMEM] * 2 + [HBM] * 5 + [VMEM] * 4,
-        out_specs=[VMEM] * 7,
-        scratch_shapes=padded_scratch() + [pltpu.SemaphoreType.DMA((sum(x.shape[0] for x in fixed),))],
+        out_shape=[f32(NVAR, PLANES, BZ)] * 2 + [jax.ShapeDtypeStruct(x.shape, x.dtype) for x in fixed]
+        + [f32(3 * NVAR * NVAR, 8, BZ), f32(count.shape[-1], CAP)],
+        in_specs=[VMEM] * 4 + [HBM] * 6 + [VMEM] * 4,
+        out_specs=[VMEM] * 9,
+        scratch_shapes=padded_scratch()
+        + [pltpu.VMEM(count.shape, jnp.int32), pltpu.SemaphoreType.DMA((sum(x.shape[0] for x in fixed) + 1,))],
         compiler_params=params(8),
         cost_estimate=sweep_cost(),
         name="first_sweep",
-    )(info, flux, bg, va, *map(in_hbm, fixed), *messages)
-    return outs[0], outs[1], tuple(outs[2:5]), tuple(outs[5:7])
+    )(info, flux, bg, va, *map(in_hbm, (*fixed, count)), *messages)
+    return outs[0], outs[1], tuple(outs[2:5]), tuple(outs[5:7]), outs[7], outs[8]
 
 
 def sweep_inner(info, flux, bg, va, messages):
     return pl.pallas_call(
         sweep_kernel,
         out_shape=[f32(NVAR, PLANES, BZ)] * 2,
-        in_specs=[SMEM, SMEM] + [VMEM] * 11,
+        in_specs=[VMEM] * 13,
         out_specs=[VMEM] * 2,
         scratch_shapes=padded_scratch(),
         compiler_params=params(8),
@@ -324,7 +346,7 @@
 
 
 def pick_kernel(group, info, flux, inner, velocity, *refs):
-    arrived, (count, cells, base, weight) = refs[:4], refs[4:8]
+    arrived, (live, cells, base, weight) = refs[:4], refs[4:8]
     valve, payload, done, table, hits, next_hits, rows_even, rows_odd, sem = refs[8:]
     owners = cells.shape[0]
     add_faces(swept_faces(info, flux, 1, inner, velocity, None, arrived), inner, done)
@@ -337,7 +359,6 @@
         table[v * BZ : (v + 1) * BZ, PLANES : 2 * PLANES] = low
     plane_at = lax.broadcasted_iota(jnp.int32, (PLANES, CAP), 0)
     row_at = lax.broadcasted_iota(jnp.int32, (8, CAP), 0)
-    slot_at = lax.broadcasted_iota(jnp.int32, (1, CAP), 1)
     steps = owners // group
 
     def find(index, target):
@@ -354,7 +375,6 @@
         for k in range(group):
             owner = index * group + k
             depth = jnp.bitwise_and(cells[pl.ds(owner, 1), :], BZ - 1)
-            live = slot_at < count[0, owner]
             offset = jnp.broadcast_to(depth, (8, CAP)) - row_at
             found = [jnp.zeros((8, CAP), jnp.float32)] * NVAR
             for z in range(0, BZ, 8):
@@ -363,7 +383,7 @@
                     row = rows[v * BZ + z : v * BZ + z + 8, k * CAP : (k + 1) * CAP]
                     found[v] = jnp.where(here, row, found[v])
             parts = [weight[corner, pl.ds(owner, 1), :] for corner in range(8)]
-            parts += [jnp.where(live, jnp.sum(found[v], axis=0, keepdims=True), 0.0) for v in range(NVAR)]
+            parts += [jnp.where(live[pl.ds(owner, 1), :] != 0.0, jnp.sum(found[v], axis=0, keepdims=True), 0.0) for v in range(NVAR)]
             parts += [base[pl.ds(owner, 1), :].astype(jnp.float32)]
             for at, part in enumerate(parts):
                 payload[owner, :, at * CAP : (at + 1) * CAP] = part
@@ -386,14 +406,14 @@
     each(stored, "wait")
 
 
-def pick(info, flux, inner, velocity, arrived, count, cells, base, weight):
+def pick(info, flux, inner, velocity, arrived, live, cells, base, weight):
     owners = cells.shape[0]
     group = 4 if owners % 8 == 0 else 1
     slots = group * CAP
     return pl.pallas_call(
         functools.partial(pick_kernel, group),
         out_shape=[f32(NVAR, PLANES, BZ), f32(owners, 1, SEND_ROWS * CAP)],
-        in_specs=[SMEM, SMEM] + [VMEM] * 6 + [SMEM] + [VMEM] * 3,
+        in_specs=[VMEM] * 12,
         out_specs=[HBM, VMEM],
         scratch_shapes=[
             pltpu.VMEM((NVAR, PLANES, BZ), jnp.float32),
@@ -406,7 +426,7 @@
         ],
         compiler_params=params(20),
         name="pick",
-    )(info, flux, inner, velocity, *arrived, in_hbm(count), cells, base, weight)
+    )(info, flux, inner, velocity, *arrived, live, cells, base, weight)
 
 
 def scatter_kernel(group, info, flux, inner, velocity, blanking, *refs):
@@ -514,7 +534,7 @@
     return pl.pallas_call(
         functools.partial(scatter_kernel, group),
         out_shape=f32(NVAR, PLANES, BZ),
-        in_specs=[SMEM, SMEM] + [VMEM] * 8,
+        in_specs=[VMEM] * 10,
         out_specs=HBM,
         scratch_shapes=[
             pltpu.VMEM((NVAR, PLANES, BZ), jnp.float32),
@@ -548,9 +568,8 @@
     slot_count,
 ):
     plans = face_plans(bulk, valve)
-    info = jnp.stack(
-        [lax.axis_index("bulk"), lax.axis_index("valve"), jnp.int32(bulk), jnp.int32(valve)]
-    ).astype(jnp.int32)
+    info = flags(lax.axis_index("bulk"), bulk) + flags(lax.axis_index("valve"), valve)
+    info = jnp.broadcast_to(jnp.stack(info).astype(jnp.int32)[:, None, None], (6, 8, BZ))
     flat = lambda block: block.reshape(-1, PLANES, BZ)
     bg, va = flat(bg_adjoint), flat(valve_adjoint)
     bg_fixed = (flat(bg_velocity), flat(bg_source), flat(bg_iblank))
@@ -559,16 +578,18 @@
     for repeat in range(ITERS):
         arrived = exchange(faces, plans)
         if repeat == 0:
-            bg, va, bg_fixed, va_fixed = first_sweep(info, flux_mix, bg, va, bg_fixed, va_fixed, faces)
+            bg, va, bg_fixed, va_fixed, flux_wide, live = first_sweep(
+                info, flux_mix, bg, va, bg_fixed, va_fixed, slot_count[:, None], faces
+            )
         else:
-            bg, va = sweep_inner(info, flux_mix, (bg, *bg_fixed), (va, *va_fixed), faces)
+            bg, va = sweep_inner(info, flux_wide, (bg, *bg_fixed), (va, *va_fixed), faces)
         if repeat < ITERS - 1:
-            faces = next_faces(info, flux_mix, bg, bg_fixed[0], bg_fixed[2], va, va_fixed[0], arrived)
+            faces = next_faces(info, flux_wide, bg, bg_fixed[0], bg_fixed[2], va, va_fixed[0], arrived)
     va, payload = pick(
-        info, flux_mix, va, va_fixed[0], arrived, slot_count, rec_cell[0], donor_base[0], donor_weight[:, 0]
+        info, flux_wide, va, va_fixed[0], arrived, live, rec_cell[0], donor_base[0], donor_weight[:, 0]
     )
     received = lax.all_to_all(payload, ("bulk", "valve"), split_axis=0, concat_axis=0, tiled=True)
-    bg = scatter(info, flux_mix, bg, bg_fixed[0], bg_fixed[2], arrived, received)
+    bg = scatter(info, flux_wide, bg, bg_fixed[0], bg_fixed[2], arrived, received)
     return (bg.reshape(bg_adjoint.shape), va.reshape(valve_adjoint.shape))
 
 

time: 70.7 us -> 65 us (0.919)
  Pallas kernels: 35.8 us -> 29.9 us
    pallas_call x3, Pallas kernels: 3.32 us -> 1.15 us  [next_faces(): pl.pallas_call(faces_kernel, out_shape=[f32(NVAR, FACE, BZ)] * 4, in_spec...]
    pallas_call x3, Pallas kernels: 9.56 us -> 8.18 us  [sweep_inner(): pl.pallas_call(sweep_kernel, out_shape=[f32(NVAR, PLANES, BZ)] * 2, in_sp...]
    pallas_call x1, Pallas kernels: 5.84 us -> 5.03 us  [pick(): pl.pallas_call(functools.partial(pick_kernel, group), out_shape=[f32(NVAR...]
    pallas_call x1, Pallas kernels: 10.6 us -> 9.86 us  [scatter(): pl.pallas_call(functools.partial(scatter_kernel, group), out_shape=f32(NV...]
  transfers between devices with their start and end apart: 16 -> 16, of which waited for: 3 -> 3; matrix products, arithmetic and copies ran while one was open for 0% -> 0% of each run, Pallas kernels for 20% -> 19%
where the time goes in v3:
time: 65 us; the launch traced here: 64.8 us
  Pallas kernels  29.9 us (46%)
  starting transfers between devices  16.5 us (25%)
  blocking collectives  13.7 us (21%)
  waiting for transfers between devices  3.64 us (6%)
  between operations  0.96 us (1%)
    ppermute x16, starting transfers between devices, exchange(): lax.ppermute(faces[k], ('bulk', 'valve'), plans[k])  16.5 us
    all_to_all x1, blocking collectives, body(): lax.all_to_all(payload, ('bulk', 'valve'), split_axis=0, concat_axis=0, t...  13.7 us
    pallas_call x1, Pallas kernels, scatter(): pl.pallas_call(functools.partial(scatter_kernel, group), out_shape=f32(NV...  9.86 us
    pallas_call x3, Pallas kernels, sweep_inner(): pl.pallas_call(sweep_kernel, out_shape=[f32(NVAR, PLANES, BZ)] * 2, in_sp...  8.18 us
    pallas_call x1, Pallas kernels, pick(): pl.pallas_call(functools.partial(pick_kernel, group), out_shape=[f32(NVAR...  5.03 us
    pallas_call x1, Pallas kernels, first_sweep(): pl.pallas_call(first_sweep_kernel, out_shape=[f32(NVAR, PLANES, BZ)] * 2...  4.19 us
    ppermute x16, waiting for transfers between devices, exchange(): lax.ppermute(faces[k], ('bulk', 'valve'), plans[k])  3.64 us
    pallas_call x1, Pallas kernels, first_faces(): pl.pallas_call(first_kernel, out_shape=[f32(NVAR, FACE, BZ)] * 4 + [f32(N...  1.5 us
  transfers between devices with their start and end apart: 16, of which 3 were waited for; matrix products, arithmetic and copies ran while one was open for 0% of the time, Pallas kernels for 19%

profile of v3, /device:TPU:0, one launch (start us, length us, event | category | flops | bytes accessed | tf_op | source)
XLA Modules:
  0.0 64.8 jit_solution(16603055310174243812)
XLA Ops:
  0.7 0.1 stack.27
  0.8 0.1 broadcast_in_dim.4.info
  0.8 1.5 %first_faces.1 = (f32[5,40,128]{2,1,0:T(8,128)S(1)}, f32[5,40,128]{2,1,0:T(8,128)S(1)}, f32[5,40,128]{2,1,0:T(8,128)S(1)}, f32[5,40,128]{2,1,0:T(8,128)S(1)}, f3...) custom-call(s32[6,8,128]{2,1,0:T(8,128)S(1)} %broadcast_in_dim.4.info, f32[5,256,128]{2,1,0:T(8,128)} %bitcast.24, ...), custom_call_target="tpu_custom_call" | custom-call | tf_op jit(solution)/shard_map/first_faces/pallas_call | solution.py:179
  2.3 3.0 %collective-permute-start = (f32[5,40,128]{2,1,0:T(8,128)S(1)}, f32[5,40,128]{2,1,0:T(8,128)S(1)}, u32[]{:S(2)}, u32[]{:S(2)}) collective-permute-start(f32[5,40,128]{2,1,0:T(8,128)S(1)} %get-tuple-element.39.refs_6_), channel_id=1, source_target_pairs={{0,1},{1,0},{2,3},{3,2},{4,5},{5,4},{6,7},{7,6},{8,9},{9,8},{10,11... | collective-permute-start | bytes 307208 | tf_op jit(solution)/shard_map/ppermute | solution.py:62
  5.4 1.6 %collective-permute-start.2 = (f32[5,40,128]{2,1,0:T(8,128)S(1)}, f32[5,40,128]{2,1,0:T(8,128)S(1)}, u32[]{:S(2)}, u32[]{:S(2)}) collective-permute-start(f32[5,40,128]{2,1,0:T(8,128)S(1)} %get-tuple-element.41.refs_8_), channel_id=1, source_target_pairs={{0,24},{1,25},{2,26},{3,27},{4,28},{5,29},{6,30},{7,31},{8,16},{9,... | collective-permute-start | bytes 307208 | tf_op jit(solution)/shard_map/ppermute | solution.py:62
  7.0 4.2 %first_sweep.1 = (f32[5,256,128]{2,1,0:T(8,128)S(1)}, f32[5,256,128]{2,1,0:T(8,128)S(1)}, f32[3,256,128]{2,1,0:T(8,128)S(1)}, f32[5,256,128]{2,1,0:T(8,128)S(1)}...) custom-call(s32[6,8,128]{2,1,0:T(8,128)S(1)} %broadcast_in_dim.4.inf, ...), custom_call_target="tpu_custom_call" | custom-call | flops 15073280 | bytes 4849664 | tf_op jit(solution)/shard_map/first_sweep/pallas_call | solution.py:306
  11.2 0.4 next_faces.3
  11.6 3.1 %collective-permute-start.4 = (f32[5,40,128]{2,1,0:T(8,128)S(1)}, f32[5,40,128]{2,1,0:T(8,128)S(1)}, u32[]{:S(2)}, u32[]{:S(2)}) collective-permute-start(f32[5,40,128]{2,1,0:T(8,128)S(1)} %get-tuple-element.51.refs_7_), channel_id=1, source_target_pairs={{0,1},{1,0},{2,3},{3,2},{4,5},{5,4},{6,7},{7,6},{8,9},{9,8},{10,11... | collective-permute-start | bytes 307208 | tf_op jit(solution)/shard_map/ppermute | solution.py:62
  14.7 0.6 collective-permute-start.6
  15.4 2.7 %sweep_inner.3 = (f32[5,256,128]{2,1,0:T(8,128)S(1)}, f32[5,256,128]{2,1,0:T(8,128)S(1)}) custom-call(s32[6,8,128]{2,1,0:T(8,128)S(1)} %broadcast_in_dim.4.info, f32[75,8,128]{2,1,0:T(8,128)S(1)} %get-tuple-element.43.flux, f32[5,256,128]{2,1,0:T(8,128)S(1)} %get-tuple-element.44.bg.refs_0_, ...), custom_call_target="tpu_custom_call" | custom-call | flops 15073280 | bytes 4849664 | tf_op jit(solution)/shard_map/sweep_inner/pallas_call | solution.py:322
  18.1 1.2 %collective-permute-done.4.messages_0_ = f32[5,40,128]{2,1,0:T(8,128)S(1)} collective-permute-done((f32[5,40,128]{2,1,0:T(8,128)S(1)}, f32[5,40,128]{2,1,0:T(8,128)S(1)}, u32[]{:S(2)}, u32[]{:S(2)}) %collective-permute-start.4) | collective-permute-done | bytes 102432 | tf_op jit(solution)/shard_map/ppermute | solution.py:62
  19.3 0.4 next_faces.4
  19.6 0.7 %collective-permute-start.10 = (f32[5,40,128]{2,1,0:T(8,128)S(1)}, f32[5,40,128]{2,1,0:T(8,128)S(1)}, u32[]{:S(2)}, u32[]{:S(2)}) collective-permute-start(f32[5,40,128]{2,1,0:T(8,128)S(1)} %get-tuple-element.59.refs_9_), channel_id=1, source_target_pairs={{0,24},{1,25},{2,26},{3,27},{4,28},{5,29},{6,30},{7,31},{8,16},{9,... | collective-permute-start | bytes 307208 | tf_op jit(solution)/shard_map/ppermute | solution.py:62
  20.4 3.6 %collective-permute-start.8 = (f32[5,40,128]{2,1,0:T(8,128)S(1)}, f32[5,40,128]{2,1,0:T(8,128)S(1)}, u32[]{:S(2)}, u32[]{:S(2)}) collective-permute-start(f32[5,40,128]{2,1,0:T(8,128)S(1)} %get-tuple-element.57.refs_7_), channel_id=1, source_target_pairs={{0,1},{1,0},{2,3},{3,2},{4,5},{5,4},{6,7},{7,6},{8,9},{9,8},{10,11... | collective-permute-start | bytes 307208 | tf_op jit(solution)/shard_map/ppermute | solution.py:62
  24.0 2.7 %sweep_inner.4 = (f32[5,256,128]{2,1,0:T(8,128)S(1)}, f32[5,256,128]{2,1,0:T(8,128)S(1)}) custom-call(s32[6,8,128]{2,1,0:T(8,128)S(1)} %broadcast_in_dim.4.info, f32[75,8,128]{2,1,0:T(8,128)S(1)} %get-tuple-element.43.flux, f32[5,256,128]{2,1,0:T(8,128)S(1)} %get-tuple-element.55.bg.refs_0_, ...), custom_call_target="tpu_custom_call" | custom-call | flops 15073280 | bytes 4849664 | tf_op jit(solution)/shard_map/sweep_inner/pallas_call | solution.py:322
  26.7 1.9 %collective-permute-done.8.messages_0_ = f32[5,40,128]{2,1,0:T(8,128)S(1)} collective-permute-done((f32[5,40,128]{2,1,0:T(8,128)S(1)}, f32[5,40,128]{2,1,0:T(8,128)S(1)}, u32[]{:S(2)}, u32[]{:S(2)}) %collective-permute-start.8) | collective-permute-done | bytes 102432 | tf_op jit(solution)/shard_map/ppermute | solution.py:62
  28.6 0.4 next_faces.5
  29.0 2.5 %collective-permute-start.12 = (f32[5,40,128]{2,1,0:T(8,128)S(1)}, f32[5,40,128]{2,1,0:T(8,128)S(1)}, u32[]{:S(2)}, u32[]{:S(2)}) collective-permute-start(f32[5,40,128]{2,1,0:T(8,128)S(1)} %get-tuple-element.63.refs_7_), channel_id=1, source_target_pairs={{0,1},{1,0},{2,3},{3,2},{4,5},{5,4},{6,7},{7,6},{8,9},{9,8},{10,11... | collective-permute-start | bytes 307208 | tf_op jit(solution)/shard_map/ppermute | solution.py:62
  31.5 1.2 %collective-permute-start.14 = (f32[5,40,128]{2,1,0:T(8,128)S(1)}, f32[5,40,128]{2,1,0:T(8,128)S(1)}, u32[]{:S(2)}, u32[]{:S(2)}) collective-permute-start(f32[5,40,128]{2,1,0:T(8,128)S(1)} %get-tuple-element.65.refs_9_), channel_id=1, source_target_pairs={{0,24},{1,25},{2,26},{3,27},{4,28},{5,29},{6,30},{7,31},{8,16},{9,... | collective-permute-start | bytes 307208 | tf_op jit(solution)/shard_map/ppermute | solution.py:62
  32.7 2.8 %sweep_inner.5 = (f32[5,256,128]{2,1,0:T(8,128)S(1)}, f32[5,256,128]{2,1,0:T(8,128)S(1)}) custom-call(s32[6,8,128]{2,1,0:T(8,128)S(1)} %broadcast_in_dim.4.info, f32[75,8,128]{2,1,0:T(8,128)S(1)} %get-tuple-element.43.flux, f32[5,256,128]{2,1,0:T(8,128)S(1)} %get-tuple-element.61.bg.refs_0_, ...), custom_call_target="tpu_custom_call" | custom-call | flops 15073280 | bytes 4849664 | tf_op jit(solution)/shard_map/sweep_inner/pallas_call | solution.py:322
  35.6 0.5 collective-permute-done.14.refs_2_
  36.1 5.0 %pick.1 = (f32[5,256,128]{2,1,0:T(8,128)}, f32[32,1,1792]{2,1,0:T(1,128)S(1)}) custom-call(s32[6,8,128]{2,1,0:T(8,128)S(1)} %broadcast_in_dim.4.info, f32[75,8,128]{2,1,0:T(8,128)S(1)} %get-tuple-element.43.flux, f32[5,256,128]{2,1,0:T(8,128)S(1)} %get-tuple-element.68.inner, f32[3,256,128]{2,1,0:T(8,128)S(1)} %get-tuple-element.49.va_velocity.refs_5_.velocity, ...), custom_call_target="tpu_custom_call" | custom-call | tf_op jit(solution)/shard_map/pick/pallas_call | solution.py:413
  41.1 13.7 %all_to_all.5.refs_4_ = f32[32,1,1792]{2,1,0:T(1,128)S(1)} all-to-all(f32[32,1,1792]{2,1,0:T(1,128)S(1)} %get-tuple-element.70), channel_id=1, replica_groups=mesh['bulk'=4,'valve'=8] {'bulk','valve'}, dimensions={0} | all-to-all | bytes 458752 | tf_op jit(solution)/shard_map/all_to_all | solution.py:591
  54.8 9.9 %scatter.1 = f32[5,256,128]{2,1,0:T(8,128)} custom-call(s32[6,8,128]{2,1,0:T(8,128)S(1)} %broadcast_in_dim.4.info, f32[75,8,128]{2,1,0:T(8,128)S(1)} %get-tuple-element.43.flux, f32[5,256,128]{2,1,0:T(8,128)S(1)} %get-tuple-element.67.inner, f32[3,256,128]{2,1,0:T(8,128)S(1)} %get-tuple-element.45.bg_velocity.refs_1_.velocity, ...), custom_call_target="tpu_custom_call" | custom-call | tf_op jit(solution)/shard_map/scatter/pallas_call | solution.py:534
  (31 shorter events, 0.1 us)
Async XLA Ops:
  0.8 6.2 %copy-start.3 = (f32[3,5,5]{2,0,1:T(4,128)S(1)}, f32[3,5,5]{2,0,1:T(4,128)}, u32[]{:S(2)}) copy-start(f32[3,5,5]{2,0,1:T(4,128)} %param.19) | copy-start | bytes 904
  2.3 8.8 %collective-permute-start = (f32[5,40,128]{2,1,0:T(8,128)S(1)}, f32[5,40,128]{2,1,0:T(8,128)S(1)}, u32[]{:S(2)}, u32[]{:S(2)}) collective-permute-start(f32[5,40,128]{2,1,0:T(8,128)S(1)} %get-tuple-element.39.refs_6_), channel_id=1, source_target_pairs={{0,1},{1,0},{2,3},{3,2},{4,5},{5,4},{6,7},{7,6},{8,9},{9,8},{10,11... | collective-permute-start | bytes 307208 | tf_op jit(solution)/shard_map/ppermute | solution.py:62
  5.4 5.8 %collective-permute-start.1 = (f32[5,40,128]{2,1,0:T(8,128)S(1)}, f32[5,40,128]{2,1,0:T(8,128)S(1)}, u32[]{:S(2)}, u32[]{:S(2)}) collective-permute-start(f32[5,40,128]{2,1,0:T(8,128)S(1)} %get-tuple-element.40.refs_7_), channel_id=1, source_target_pairs={{0,8},{1,2},{2,1},{3,4},{4,3},{5,6},{6,5},{7,15},{8,0},{9,10},{10,... | collective-permute-start | bytes 307208 | tf_op jit(solution)/shard_map/ppermute | solution.py:62
  5.4 5.8 %collective-permute-start.2 = (f32[5,40,128]{2,1,0:T(8,128)S(1)}, f32[5,40,128]{2,1,0:T(8,128)S(1)}, u32[]{:S(2)}, u32[]{:S(2)}) collective-permute-start(f32[5,40,128]{2,1,0:T(8,128)S(1)} %get-tuple-element.41.refs_8_), channel_id=1, source_target_pairs={{0,24},{1,25},{2,26},{3,27},{4,28},{5,29},{6,30},{7,31},{8,16},{9,... | collective-permute-start | bytes 307208 | tf_op jit(solution)/shard_map/ppermute | solution.py:62
  7.0 4.2 %collective-permute-start.3 = (f32[5,40,128]{2,1,0:T(8,128)S(1)}, f32[5,40,128]{2,1,0:T(8,128)S(1)}, u32[]{:S(2)}, u32[]{:S(2)}) collective-permute-start(f32[5,40,128]{2,1,0:T(8,128)S(1)} %get-tuple-element.42.refs_9_), channel_id=1, source_target_pairs={{0,8},{1,9},{2,10},{3,11},{4,12},{5,13},{6,14},{7,15},{8,0},{9,1},... | collective-permute-start | bytes 307208 | tf_op jit(solution)/shard_map/ppermute | solution.py:62
  11.6 7.6 %collective-permute-start.4 = (f32[5,40,128]{2,1,0:T(8,128)S(1)}, f32[5,40,128]{2,1,0:T(8,128)S(1)}, u32[]{:S(2)}, u32[]{:S(2)}) collective-permute-start(f32[5,40,128]{2,1,0:T(8,128)S(1)} %get-tuple-element.51.refs_7_), channel_id=1, source_target_pairs={{0,1},{1,0},{2,3},{3,2},{4,5},{5,4},{6,7},{7,6},{8,9},{9,8},{10,11... | collective-permute-start | bytes 307208 | tf_op jit(solution)/shard_map/ppermute | solution.py:62
  14.7 4.5 %collective-permute-start.5 = (f32[5,40,128]{2,1,0:T(8,128)S(1)}, f32[5,40,128]{2,1,0:T(8,128)S(1)}, u32[]{:S(2)}, u32[]{:S(2)}) collective-permute-start(f32[5,40,128]{2,1,0:T(8,128)S(1)} %get-tuple-element.52.refs_8_), channel_id=1, source_target_pairs={{0,8},{1,2},{2,1},{3,4},{4,3},{5,6},{6,5},{7,15},{8,0},{9,10},{10,... | collective-permute-start | bytes 307208 | tf_op jit(solution)/shard_map/ppermute | solution.py:62
  14.7 4.5 %collective-permute-start.6 = (f32[5,40,128]{2,1,0:T(8,128)S(1)}, f32[5,40,128]{2,1,0:T(8,128)S(1)}, u32[]{:S(2)}, u32[]{:S(2)}) collective-permute-start(f32[5,40,128]{2,1,0:T(8,128)S(1)} %get-tuple-element.53.refs_9_), channel_id=1, source_target_pairs={{0,24},{1,25},{2,26},{3,27},{4,28},{5,29},{6,30},{7,31},{8,16},{9,... | collective-permute-start | bytes 307208 | tf_op jit(solution)/shard_map/ppermute | solution.py:62
  15.4 3.9 %collective-permute-start.7 = (f32[5,40,128]{2,1,0:T(8,128)S(1)}, f32[5,40,128]{2,1,0:T(8,128)S(1)}, u32[]{:S(2)}, u32[]{:S(2)}) collective-permute-start(f32[5,40,128]{2,1,0:T(8,128)S(1)} %get-tuple-element.54.refs_10_), channel_id=1, source_target_pairs={{0,8},{1,9},{2,10},{3,11},{4,12},{5,13},{6,14},{7,15},{8,0},{9,1},... | collective-permute-start | bytes 307208 | tf_op jit(solution)/shard_map/ppermute | solution.py:62
  19.6 7.0 %collective-permute-start.10 = (f32[5,40,128]{2,1,0:T(8,128)S(1)}, f32[5,40,128]{2,1,0:T(8,128)S(1)}, u32[]{:S(2)}, u32[]{:S(2)}) collective-permute-start(f32[5,40,128]{2,1,0:T(8,128)S(1)} %get-tuple-element.59.refs_9_), channel_id=1, source_target_pairs={{0,24},{1,25},{2,26},{3,27},{4,28},{5,29},{6,30},{7,31},{8,16},{9,... | collective-permute-start | bytes 307208 | tf_op jit(solution)/shard_map/ppermute | solution.py:62
  20.3 6.4 %collective-permute-start.11 = (f32[5,40,128]{2,1,0:T(8,128)S(1)}, f32[5,40,128]{2,1,0:T(8,128)S(1)}, u32[]{:S(2)}, u32[]{:S(2)}) collective-permute-start(f32[5,40,128]{2,1,0:T(8,128)S(1)} %get-tuple-element.60.refs_10_), channel_id=1, source_target_pairs={{0,8},{1,9},{2,10},{3,11},{4,12},{5,13},{6,14},{7,15},{8,0},{9,1},... | collective-permute-start | bytes 307208 | tf_op jit(solution)/shard_map/ppermute | solution.py:62
  20.4 8.3 %collective-permute-start.8 = (f32[5,40,128]{2,1,0:T(8,128)S(1)}, f32[5,40,128]{2,1,0:T(8,128)S(1)}, u32[]{:S(2)}, u32[]{:S(2)}) collective-permute-start(f32[5,40,128]{2,1,0:T(8,128)S(1)} %get-tuple-element.57.refs_7_), channel_id=1, source_target_pairs={{0,1},{1,0},{2,3},{3,2},{4,5},{5,4},{6,7},{7,6},{8,9},{9,8},{10,11... | collective-permute-start | bytes 307208 | tf_op jit(solution)/shard_map/ppermute | solution.py:62
  24.0 4.6 %collective-permute-start.9 = (f32[5,40,128]{2,1,0:T(8,128)S(1)}, f32[5,40,128]{2,1,0:T(8,128)S(1)}, u32[]{:S(2)}, u32[]{:S(2)}) collective-permute-start(f32[5,40,128]{2,1,0:T(8,128)S(1)} %get-tuple-element.58.refs_8_), channel_id=1, source_target_pairs={{0,8},{1,2},{2,1},{3,4},{4,3},{5,6},{6,5},{7,15},{8,0},{9,10},{10,... | collective-permute-start | bytes 307208 | tf_op jit(solution)/shard_map/ppermute | solution.py:62
  29.0 6.6 %collective-permute-start.12 = (f32[5,40,128]{2,1,0:T(8,128)S(1)}, f32[5,40,128]{2,1,0:T(8,128)S(1)}, u32[]{:S(2)}, u32[]{:S(2)}) collective-permute-start(f32[5,40,128]{2,1,0:T(8,128)S(1)} %get-tuple-element.63.refs_7_), channel_id=1, source_target_pairs={{0,1},{1,0},{2,3},{3,2},{4,5},{5,4},{6,7},{7,6},{8,9},{9,8},{10,11... | collective-permute-start | bytes 307208 | tf_op jit(solution)/shard_map/ppermute | solution.py:62
  31.5 4.0 %collective-permute-start.13 = (f32[5,40,128]{2,1,0:T(8,128)S(1)}, f32[5,40,128]{2,1,0:T(8,128)S(1)}, u32[]{:S(2)}, u32[]{:S(2)}) collective-permute-start(f32[5,40,128]{2,1,0:T(8,128)S(1)} %get-tuple-element.64.refs_8_), channel_id=1, source_target_pairs={{0,8},{1,2},{2,1},{3,4},{4,3},{5,6},{6,5},{7,15},{8,0},{9,10},{10,... | collective-permute-start | bytes 307208 | tf_op jit(solution)/shard_map/ppermute | solution.py:62
  31.5 4.5 %collective-permute-start.14 = (f32[5,40,128]{2,1,0:T(8,128)S(1)}, f32[5,40,128]{2,1,0:T(8,128)S(1)}, u32[]{:S(2)}, u32[]{:S(2)}) collective-permute-start(f32[5,40,128]{2,1,0:T(8,128)S(1)} %get-tuple-element.65.refs_9_), channel_id=1, source_target_pairs={{0,24},{1,25},{2,26},{3,27},{4,28},{5,29},{6,30},{7,31},{8,16},{9,... | collective-permute-start | bytes 307208 | tf_op jit(solution)/shard_map/ppermute | solution.py:62
  32.7 3.4 %copy-start = (f32[8,1,32,128]{3,2,1,0:T(8,128)S(1)}, f32[8,1,32,128]{3,2,1,0:T(8,128)}, u32[]{:S(2)}) copy-start(f32[8,1,32,128]{3,2,1,0:T(8,128)} %param.22) | copy-start | bytes 393220
  32.7 3.4 %collective-permute-start.15 = (f32[5,40,128]{2,1,0:T(8,128)S(1)}, f32[5,40,128]{2,1,0:T(8,128)S(1)}, u32[]{:S(2)}, u32[]{:S(2)}) collective-permute-start(f32[5,40,128]{2,1,0:T(8,128)S(1)} %get-tuple-element.66.refs_10_), channel_id=1, source_target_pairs={{0,8},{1,9},{2,10},{3,11},{4,12},{5,13},{6,14},{7,15},{8,0},{9,1},... | collective-permute-start | bytes 307208 | tf_op jit(solution)/shard_map/ppermute | solution.py:62
  32.7 3.4 %copy-start.1 = (s32[1,32,128]{2,1,0:T(8,128)S(1)}, s32[1,32,128]{2,1,0:T(8,128)}, u32[]{:S(2)}) copy-start(s32[1,32,128]{2,1,0:T(8,128)} %param.20) | copy-start | bytes 49156
  32.7 3.4 %copy-start.2 = (s32[1,32,128]{2,1,0:T(8,128)S(1)}, s32[1,32,128]{2,1,0:T(8,128)}, u32[]{:S(2)}) copy-start(s32[1,32,128]{2,1,0:T(8,128)} %param.21) | copy-start | bytes 49156

commit v4 on v3

--- a/solution.py
+++ b/solution.py
@@ -16,7 +16,7 @@
 PLANES = BX * BY
 FACE = BY + BX
 STEP = BY + 16
-SEND_ROWS = 14
+SEND_ROWS = 13
 RUN = 2
 RUNS = BZ // RUN
 PLACE = {(1, 0): 0, (1, 1): 1, (0, 1): 2, (0, 0): 3}
@@ -382,26 +382,29 @@
                 for v in range(NVAR):
                     row = rows[v * BZ + z : v * BZ + z + 8, k * CAP : (k + 1) * CAP]
                     found[v] = jnp.where(here, row, found[v])
-            parts = [weight[corner, pl.ds(owner, 1), :] for corner in range(8)]
+            parts = [weight[corner, pl.ds(owner, 1), :] for corner in range(7)]
             parts += [jnp.where(live[pl.ds(owner, 1), :] != 0.0, jnp.sum(found[v], axis=0, keepdims=True), 0.0) for v in range(NVAR)]
             parts += [base[pl.ds(owner, 1), :].astype(jnp.float32)]
             for at, part in enumerate(parts):
                 payload[owner, :, at * CAP : (at + 1) * CAP] = part
 
     find(0, hits)
-    fetch(hits, rows_odd)
+    fetch(hits, rows_even)
+    find(1, next_hits)
+    fetch(next_hits, rows_odd)
+    put(0, rows_even)
 
     def step(pair, carry):
         one, two = 2 * pair, 2 * pair + 1
         find(one, hits)
         fetch(hits, rows_even)
-        put(jnp.maximum(one - 1, 0), rows_odd)
+        put(one - 1, rows_odd)
         find(two, next_hits)
         fetch(next_hits, rows_odd)
         put(one, rows_even)
         return carry
 
-    lax.fori_loop(0, steps // 2, step, 0)
+    lax.fori_loop(1, steps // 2, step, 0)
     put(steps - 1, rows_odd)
     each(stored, "wait")
 
@@ -455,7 +458,9 @@
         for k in range(group):
             sender = index * group + k
             cols = [slice(part * width + k * CAP, part * width + (k + 1) * CAP) for part in range(2)]
-            anchor = row(sender, 13).astype(jnp.int32)
+            anchor = row(sender, 12).astype(jnp.int32)
+            weights = [row(sender, corner) for corner in range(7)]
+            weights.append(1.0 - sum(weights))
             depth = jnp.bitwise_and(anchor, BZ - 1)
             place = jnp.bitwise_and(depth, RUN - 1)
             row_y = jnp.bitwise_and(lax.shift_right_logical(anchor, 7), BY - 1)
@@ -467,8 +472,8 @@
                 for i in range(2):
                     high = low = zero
                     for j in range(2):
-                        weight = jnp.where(place == spot, row(sender, 4 * i + 2 * j), 0.0)
-                        weight = jnp.where(place == spot - 1, row(sender, 4 * i + 2 * j + 1), weight)
+                        weight = jnp.where(place == spot, weights[4 * i + 2 * j], 0.0)
+                        weight = jnp.where(place == spot - 1, weights[4 * i + 2 * j + 1], weight)
                         high_row, low_row = wide_parts(weight)
                         high = jnp.where(at_y[j], high_row, high)
                         low = jnp.where(at_y[j], low_row, low)
@@ -482,7 +487,7 @@
             here = run_at == wide(jnp.right_shift(depth, RUN.bit_length() - 1).astype(jnp.float32))
             for v in range(NVAR):
                 rows = slice(v * RUNS, (v + 1) * RUNS)
-                high_row, low_row = wide_parts(row(sender, 8 + v))
+                high_row, low_row = wide_parts(row(sender, 7 + v))
                 placed[rows, cols[0]] = jnp.where(here, high_row, zero).reshape(RUNS, CAP)
                 placed[rows, cols[1]] = jnp.where(here, low_row, zero).reshape(RUNS, CAP)
 
@@ -495,19 +500,21 @@
         product = product + (both[: NVAR * RUNS] + both[NVAR * RUNS :])
         total[...] += product
 
-    add_faces(swept_faces(info, flux, 0, inner, velocity, blanking, arrived), inner, swept)
     total[...] = jnp.zeros_like(total)
     build(0, spread, placed)
 
     def step(pair, carry):
-        two = 2 * pair + 1
         add(spread, placed)
-        build(two, next_spread, next_placed)
+        build(2 * pair + 1, next_spread, next_placed)
         add(next_spread, next_placed)
-        build(jnp.minimum(two + 1, steps - 1), spread, placed)
+        build(2 * pair + 2, spread, placed)
         return carry
 
-    lax.fori_loop(0, steps // 2, step, 0)
+    lax.fori_loop(0, steps // 2 - 1, step, 0)
+    add(spread, placed)
+    build(steps - 1, next_spread, next_placed)
+    add_faces(swept_faces(info, flux, 0, inner, velocity, blanking, arrived), inner, swept)
+    add(next_spread, next_placed)
     run = lax.broadcasted_iota(jnp.int32, (RUNS, PLANES), 0)
     stored = [[pltpu.make_async_copy(swept.at[v], out.at[v], sem.at[v])] for v in range(NVAR)]
     for v in range(NVAR):

time: 65 us -> 63.3 us (0.974)
  Pallas kernels: 29.9 us -> 28.9 us
  blocking collectives: 13.7 us -> 12.9 us
    all_to_all x1, blocking collectives: 13.7 us -> 12.9 us  [body(): lax.all_to_all(payload, ('bulk', 'valve'), split_axis=0, concat_axis=0, t...]
    pallas_call x1, Pallas kernels: 5.03 us -> 4.31 us  [pick(): pl.pallas_call(functools.partial(pick_kernel, group), out_shape=[f32(NVAR...]
  transfers between devices with their start and end apart: 16 -> 16, of which waited for: 3 -> 3; matrix products, arithmetic and copies ran while one was open for 0% -> 0% of each run, Pallas kernels for 19% -> 20%
where the time goes in v4:
time: 63.3 us; the launch traced here: 63.1 us
  Pallas kernels  28.9 us (46%)
  starting transfers between devices  16.5 us (26%)
  blocking collectives  12.9 us (20%)
  waiting for transfers between devices  3.64 us (6%)
  between operations  0.96 us (2%)
    ppermute x16, starting transfers between devices, exchange(): lax.ppermute(faces[k], ('bulk', 'valve'), plans[k])  16.5 us
    all_to_all x1, blocking collectives, body(): lax.all_to_all(payload, ('bulk', 'valve'), split_axis=0, concat_axis=0, t...  12.9 us
    pallas_call x1, Pallas kernels, scatter(): pl.pallas_call(functools.partial(scatter_kernel, group), out_shape=f32(NV...  9.57 us
    pallas_call x3, Pallas kernels, sweep_inner(): pl.pallas_call(sweep_kernel, out_shape=[f32(NVAR, PLANES, BZ)] * 2, in_sp...  8.18 us
    pallas_call x1, Pallas kernels, pick(): pl.pallas_call(functools.partial(pick_kernel, group), out_shape=[f32(NVAR...  4.31 us
    pallas_call x1, Pallas kernels, first_sweep(): pl.pallas_call(first_sweep_kernel, out_shape=[f32(NVAR, PLANES, BZ)] * 2...  4.19 us
    ppermute x16, waiting for transfers between devices, exchange(): lax.ppermute(faces[k], ('bulk', 'valve'), plans[k])  3.64 us
    pallas_call x1, Pallas kernels, first_faces(): pl.pallas_call(first_kernel, out_shape=[f32(NVAR, FACE, BZ)] * 4 + [f32(N...  1.5 us
  transfers between devices with their start and end apart: 16, of which 3 were waited for; matrix products, arithmetic and copies ran while one was open for 0% of the time, Pallas kernels for 20%

profile of v4, /device:TPU:0, one launch (start us, length us, event | category | flops | bytes accessed | tf_op | source)
XLA Modules:
  0.0 63.1 jit_solution(18117891997681586852)
XLA Ops:
  0.7 0.1 stack.27
  0.8 0.1 broadcast_in_dim.4.info
  0.8 1.5 %first_faces.1 = (f32[5,40,128]{2,1,0:T(8,128)S(1)}, f32[5,40,128]{2,1,0:T(8,128)S(1)}, f32[5,40,128]{2,1,0:T(8,128)S(1)}, f32[5,40,128]{2,1,0:T(8,128)S(1)}, f3...) custom-call(s32[6,8,128]{2,1,0:T(8,128)S(1)} %broadcast_in_dim.4.info, f32[5,256,128]{2,1,0:T(8,128)} %bitcast.24, ...), custom_call_target="tpu_custom_call" | custom-call | tf_op jit(solution)/shard_map/first_faces/pallas_call | solution.py:179
  2.3 3.0 %collective-permute-start = (f32[5,40,128]{2,1,0:T(8,128)S(1)}, f32[5,40,128]{2,1,0:T(8,128)S(1)}, u32[]{:S(2)}, u32[]{:S(2)}) collective-permute-start(f32[5,40,128]{2,1,0:T(8,128)S(1)} %get-tuple-element.39.refs_6_), channel_id=1, source_target_pairs={{0,1},{1,0},{2,3},{3,2},{4,5},{5,4},{6,7},{7,6},{8,9},{9,8},{10,11... | collective-permute-start | bytes 307208 | tf_op jit(solution)/shard_map/ppermute | solution.py:62
  5.4 1.6 %collective-permute-start.2 = (f32[5,40,128]{2,1,0:T(8,128)S(1)}, f32[5,40,128]{2,1,0:T(8,128)S(1)}, u32[]{:S(2)}, u32[]{:S(2)}) collective-permute-start(f32[5,40,128]{2,1,0:T(8,128)S(1)} %get-tuple-element.41.refs_8_), channel_id=1, source_target_pairs={{0,24},{1,25},{2,26},{3,27},{4,28},{5,29},{6,30},{7,31},{8,16},{9,... | collective-permute-start | bytes 307208 | tf_op jit(solution)/shard_map/ppermute | solution.py:62
  7.0 4.2 %first_sweep.1 = (f32[5,256,128]{2,1,0:T(8,128)S(1)}, f32[5,256,128]{2,1,0:T(8,128)S(1)}, f32[3,256,128]{2,1,0:T(8,128)S(1)}, f32[5,256,128]{2,1,0:T(8,128)S(1)}...) custom-call(s32[6,8,128]{2,1,0:T(8,128)S(1)} %broadcast_in_dim.4.inf, ...), custom_call_target="tpu_custom_call" | custom-call | flops 15073280 | bytes 4849664 | tf_op jit(solution)/shard_map/first_sweep/pallas_call | solution.py:306
  11.2 0.4 next_faces.3
  11.6 3.1 %collective-permute-start.4 = (f32[5,40,128]{2,1,0:T(8,128)S(1)}, f32[5,40,128]{2,1,0:T(8,128)S(1)}, u32[]{:S(2)}, u32[]{:S(2)}) collective-permute-start(f32[5,40,128]{2,1,0:T(8,128)S(1)} %get-tuple-element.51.refs_7_), channel_id=1, source_target_pairs={{0,1},{1,0},{2,3},{3,2},{4,5},{5,4},{6,7},{7,6},{8,9},{9,8},{10,11... | collective-permute-start | bytes 307208 | tf_op jit(solution)/shard_map/ppermute | solution.py:62
  14.7 0.6 %collective-permute-start.6 = (f32[5,40,128]{2,1,0:T(8,128)S(1)}, f32[5,40,128]{2,1,0:T(8,128)S(1)}, u32[]{:S(2)}, u32[]{:S(2)}) collective-permute-start(f32[5,40,128]{2,1,0:T(8,128)S(1)} %get-tuple-element.53.refs_9_), channel_id=1, source_target_pairs={{0,24},{1,25},{2,26},{3,27},{4,28},{5,29},{6,30},{7,31},{8,16},{9,... | collective-permute-start | bytes 307208 | tf_op jit(solution)/shard_map/ppermute | solution.py:62
  15.4 2.7 %sweep_inner.3 = (f32[5,256,128]{2,1,0:T(8,128)S(1)}, f32[5,256,128]{2,1,0:T(8,128)S(1)}) custom-call(s32[6,8,128]{2,1,0:T(8,128)S(1)} %broadcast_in_dim.4.info, f32[75,8,128]{2,1,0:T(8,128)S(1)} %get-tuple-element.43.flux, f32[5,256,128]{2,1,0:T(8,128)S(1)} %get-tuple-element.44.bg.refs_0_, ...), custom_call_target="tpu_custom_call" | custom-call | flops 15073280 | bytes 4849664 | tf_op jit(solution)/shard_map/sweep_inner/pallas_call | solution.py:322
  18.1 1.2 %collective-permute-done.4.messages_0_ = f32[5,40,128]{2,1,0:T(8,128)S(1)} collective-permute-done((f32[5,40,128]{2,1,0:T(8,128)S(1)}, f32[5,40,128]{2,1,0:T(8,128)S(1)}, u32[]{:S(2)}, u32[]{:S(2)}) %collective-permute-start.4) | collective-permute-done | bytes 102432 | tf_op jit(solution)/shard_map/ppermute | solution.py:62
  19.3 0.4 next_faces.4
  19.6 0.7 %collective-permute-start.10 = (f32[5,40,128]{2,1,0:T(8,128)S(1)}, f32[5,40,128]{2,1,0:T(8,128)S(1)}, u32[]{:S(2)}, u32[]{:S(2)}) collective-permute-start(f32[5,40,128]{2,1,0:T(8,128)S(1)} %get-tuple-element.59.refs_9_), channel_id=1, source_target_pairs={{0,24},{1,25},{2,26},{3,27},{4,28},{5,29},{6,30},{7,31},{8,16},{9,... | collective-permute-start | bytes 307208 | tf_op jit(solution)/shard_map/ppermute | solution.py:62
  20.4 3.6 %collective-permute-start.8 = (f32[5,40,128]{2,1,0:T(8,128)S(1)}, f32[5,40,128]{2,1,0:T(8,128)S(1)}, u32[]{:S(2)}, u32[]{:S(2)}) collective-permute-start(f32[5,40,128]{2,1,0:T(8,128)S(1)} %get-tuple-element.57.refs_7_), channel_id=1, source_target_pairs={{0,1},{1,0},{2,3},{3,2},{4,5},{5,4},{6,7},{7,6},{8,9},{9,8},{10,11... | collective-permute-start | bytes 307208 | tf_op jit(solution)/shard_map/ppermute | solution.py:62
  24.0 2.7 %sweep_inner.4 = (f32[5,256,128]{2,1,0:T(8,128)S(1)}, f32[5,256,128]{2,1,0:T(8,128)S(1)}) custom-call(s32[6,8,128]{2,1,0:T(8,128)S(1)} %broadcast_in_dim.4.info, f32[75,8,128]{2,1,0:T(8,128)S(1)} %get-tuple-element.43.flux, f32[5,256,128]{2,1,0:T(8,128)S(1)} %get-tuple-element.55.bg.refs_0_, ...), custom_call_target="tpu_custom_call" | custom-call | flops 15073280 | bytes 4849664 | tf_op jit(solution)/shard_map/sweep_inner/pallas_call | solution.py:322
  26.7 1.9 %collective-permute-done.8.messages_0_ = f32[5,40,128]{2,1,0:T(8,128)S(1)} collective-permute-done((f32[5,40,128]{2,1,0:T(8,128)S(1)}, f32[5,40,128]{2,1,0:T(8,128)S(1)}, u32[]{:S(2)}, u32[]{:S(2)}) %collective-permute-start.8) | collective-permute-done | bytes 102432 | tf_op jit(solution)/shard_map/ppermute | solution.py:62
  28.6 0.4 next_faces.5
  29.0 2.5 %collective-permute-start.12 = (f32[5,40,128]{2,1,0:T(8,128)S(1)}, f32[5,40,128]{2,1,0:T(8,128)S(1)}, u32[]{:S(2)}, u32[]{:S(2)}) collective-permute-start(f32[5,40,128]{2,1,0:T(8,128)S(1)} %get-tuple-element.63.refs_7_), channel_id=1, source_target_pairs={{0,1},{1,0},{2,3},{3,2},{4,5},{5,4},{6,7},{7,6},{8,9},{9,8},{10,11... | collective-permute-start | bytes 307208 | tf_op jit(solution)/shard_map/ppermute | solution.py:62
  31.5 1.2 %collective-permute-start.14 = (f32[5,40,128]{2,1,0:T(8,128)S(1)}, f32[5,40,128]{2,1,0:T(8,128)S(1)}, u32[]{:S(2)}, u32[]{:S(2)}) collective-permute-start(f32[5,40,128]{2,1,0:T(8,128)S(1)} %get-tuple-element.65.refs_9_), channel_id=1, source_target_pairs={{0,24},{1,25},{2,26},{3,27},{4,28},{5,29},{6,30},{7,31},{8,16},{9,... | collective-permute-start | bytes 307208 | tf_op jit(solution)/shard_map/ppermute | solution.py:62
  32.7 2.8 %sweep_inner.5 = (f32[5,256,128]{2,1,0:T(8,128)S(1)}, f32[5,256,128]{2,1,0:T(8,128)S(1)}) custom-call(s32[6,8,128]{2,1,0:T(8,128)S(1)} %broadcast_in_dim.4.info, f32[75,8,128]{2,1,0:T(8,128)S(1)} %get-tuple-element.43.flux, f32[5,256,128]{2,1,0:T(8,128)S(1)} %get-tuple-element.61.bg.refs_0_, ...), custom_call_target="tpu_custom_call" | custom-call | flops 15073280 | bytes 4849664 | tf_op jit(solution)/shard_map/sweep_inner/pallas_call | solution.py:322
  35.6 0.5 collective-permute-done.14.refs_2_
  36.1 4.3 %pick.1 = (f32[5,256,128]{2,1,0:T(8,128)}, f32[32,1,1664]{2,1,0:T(1,128)S(1)}) custom-call(s32[6,8,128]{2,1,0:T(8,128)S(1)} %broadcast_in_dim.4.info, f32[75,8,128]{2,1,0:T(8,128)S(1)} %get-tuple-element.43.flux, f32[5,256,128]{2,1,0:T(8,128)S(1)} %get-tuple-element.68.inner, f32[3,256,128]{2,1,0:T(8,128)S(1)} %get-tuple-element.49.va_velocity.refs_5_.velocity, ...), custom_call_target="tpu_custom_call" | custom-call | tf_op jit(solution)/shard_map/pick/pallas_call | solution.py:416
  40.4 12.9 %all_to_all.5.refs_4_ = f32[32,1,1664]{2,1,0:T(1,128)S(1)} all-to-all(f32[32,1,1664]{2,1,0:T(1,128)S(1)} %get-tuple-element.70), channel_id=1, replica_groups=mesh['bulk'=4,'valve'=8] {'bulk','valve'}, dimensions={0} | all-to-all | bytes 425984 | tf_op jit(solution)/shard_map/all_to_all | solution.py:598
  53.3 9.6 %scatter.1 = f32[5,256,128]{2,1,0:T(8,128)} custom-call(s32[6,8,128]{2,1,0:T(8,128)S(1)} %broadcast_in_dim.4.info, f32[75,8,128]{2,1,0:T(8,128)S(1)} %get-tuple-element.43.flux, f32[5,256,128]{2,1,0:T(8,128)S(1)} %get-tuple-element.67.inner, f32[3,256,128]{2,1,0:T(8,128)S(1)} %get-tuple-element.45.bg_velocity.refs_1_.velocity, ...), custom_call_target="tpu_custom_call" | custom-call | tf_op jit(solution)/shard_map/scatter/pallas_call | solution.py:541
  (31 shorter events, 0.1 us)
Async XLA Ops:
  0.8 6.2 %copy-start.3 = (f32[3,5,5]{2,0,1:T(4,128)S(1)}, f32[3,5,5]{2,0,1:T(4,128)}, u32[]{:S(2)}) copy-start(f32[3,5,5]{2,0,1:T(4,128)} %param.19) | copy-start | bytes 904
  2.3 8.8 %collective-permute-start = (f32[5,40,128]{2,1,0:T(8,128)S(1)}, f32[5,40,128]{2,1,0:T(8,128)S(1)}, u32[]{:S(2)}, u32[]{:S(2)}) collective-permute-start(f32[5,40,128]{2,1,0:T(8,128)S(1)} %get-tuple-element.39.refs_6_), channel_id=1, source_target_pairs={{0,1},{1,0},{2,3},{3,2},{4,5},{5,4},{6,7},{7,6},{8,9},{9,8},{10,11... | collective-permute-start | bytes 307208 | tf_op jit(solution)/shard_map/ppermute | solution.py:62
  5.4 5.8 %collective-permute-start.1 = (f32[5,40,128]{2,1,0:T(8,128)S(1)}, f32[5,40,128]{2,1,0:T(8,128)S(1)}, u32[]{:S(2)}, u32[]{:S(2)}) collective-permute-start(f32[5,40,128]{2,1,0:T(8,128)S(1)} %get-tuple-element.40.refs_7_), channel_id=1, source_target_pairs={{0,8},{1,2},{2,1},{3,4},{4,3},{5,6},{6,5},{7,15},{8,0},{9,10},{10,... | collective-permute-start | bytes 307208 | tf_op jit(solution)/shard_map/ppermute | solution.py:62
  5.4 5.8 %collective-permute-start.2 = (f32[5,40,128]{2,1,0:T(8,128)S(1)}, f32[5,40,128]{2,1,0:T(8,128)S(1)}, u32[]{:S(2)}, u32[]{:S(2)}) collective-permute-start(f32[5,40,128]{2,1,0:T(8,128)S(1)} %get-tuple-element.41.refs_8_), channel_id=1, source_target_pairs={{0,24},{1,25},{2,26},{3,27},{4,28},{5,29},{6,30},{7,31},{8,16},{9,... | collective-permute-start | bytes 307208 | tf_op jit(solution)/shard_map/ppermute | solution.py:62
  7.0 4.2 %collective-permute-start.3 = (f32[5,40,128]{2,1,0:T(8,128)S(1)}, f32[5,40,128]{2,1,0:T(8,128)S(1)}, u32[]{:S(2)}, u32[]{:S(2)}) collective-permute-start(f32[5,40,128]{2,1,0:T(8,128)S(1)} %get-tuple-element.42.refs_9_), channel_id=1, source_target_pairs={{0,8},{1,9},{2,10},{3,11},{4,12},{5,13},{6,14},{7,15},{8,0},{9,1},... | collective-permute-start | bytes 307208 | tf_op jit(solution)/shard_map/ppermute | solution.py:62
  11.6 7.6 %collective-permute-start.4 = (f32[5,40,128]{2,1,0:T(8,128)S(1)}, f32[5,40,128]{2,1,0:T(8,128)S(1)}, u32[]{:S(2)}, u32[]{:S(2)}) collective-permute-start(f32[5,40,128]{2,1,0:T(8,128)S(1)} %get-tuple-element.51.refs_7_), channel_id=1, source_target_pairs={{0,1},{1,0},{2,3},{3,2},{4,5},{5,4},{6,7},{7,6},{8,9},{9,8},{10,11... | collective-permute-start | bytes 307208 | tf_op jit(solution)/shard_map/ppermute | solution.py:62
  14.7 4.5 %collective-permute-start.5 = (f32[5,40,128]{2,1,0:T(8,128)S(1)}, f32[5,40,128]{2,1,0:T(8,128)S(1)}, u32[]{:S(2)}, u32[]{:S(2)}) collective-permute-start(f32[5,40,128]{2,1,0:T(8,128)S(1)} %get-tuple-element.52.refs_8_), channel_id=1, source_target_pairs={{0,8},{1,2},{2,1},{3,4},{4,3},{5,6},{6,5},{7,15},{8,0},{9,10},{10,... | collective-permute-start | bytes 307208 | tf_op jit(solution)/shard_map/ppermute | solution.py:62
  14.7 4.5 %collective-permute-start.6 = (f32[5,40,128]{2,1,0:T(8,128)S(1)}, f32[5,40,128]{2,1,0:T(8,128)S(1)}, u32[]{:S(2)}, u32[]{:S(2)}) collective-permute-start(f32[5,40,128]{2,1,0:T(8,128)S(1)} %get-tuple-element.53.refs_9_), channel_id=1, source_target_pairs={{0,24},{1,25},{2,26},{3,27},{4,28},{5,29},{6,30},{7,31},{8,16},{9,... | collective-permute-start | bytes 307208 | tf_op jit(solution)/shard_map/ppermute | solution.py:62
  15.4 3.9 %collective-permute-start.7 = (f32[5,40,128]{2,1,0:T(8,128)S(1)}, f32[5,40,128]{2,1,0:T(8,128)S(1)}, u32[]{:S(2)}, u32[]{:S(2)}) collective-permute-start(f32[5,40,128]{2,1,0:T(8,128)S(1)} %get-tuple-element.54.refs_10_), channel_id=1, source_target_pairs={{0,8},{1,9},{2,10},{3,11},{4,12},{5,13},{6,14},{7,15},{8,0},{9,1},... | collective-permute-start | bytes 307208 | tf_op jit(solution)/shard_map/ppermute | solution.py:62
  19.6 7.0 %collective-permute-start.10 = (f32[5,40,128]{2,1,0:T(8,128)S(1)}, f32[5,40,128]{2,1,0:T(8,128)S(1)}, u32[]{:S(2)}, u32[]{:S(2)}) collective-permute-start(f32[5,40,128]{2,1,0:T(8,128)S(1)} %get-tuple-element.59.refs_9_), channel_id=1, source_target_pairs={{0,24},{1,25},{2,26},{3,27},{4,28},{5,29},{6,30},{7,31},{8,16},{9,... | collective-permute-start | bytes 307208 | tf_op jit(solution)/shard_map/ppermute | solution.py:62
  20.3 6.4 %collective-permute-start.11 = (f32[5,40,128]{2,1,0:T(8,128)S(1)}, f32[5,40,128]{2,1,0:T(8,128)S(1)}, u32[]{:S(2)}, u32[]{:S(2)}) collective-permute-start(f32[5,40,128]{2,1,0:T(8,128)S(1)} %get-tuple-element.60.refs_10_), channel_id=1, source_target_pairs={{0,8},{1,9},{2,10},{3,11},{4,12},{5,13},{6,14},{7,15},{8,0},{9,1},... | collective-permute-start | bytes 307208 | tf_op jit(solution)/shard_map/ppermute | solution.py:62
  20.4 8.3 %collective-permute-start.8 = (f32[5,40,128]{2,1,0:T(8,128)S(1)}, f32[5,40,128]{2,1,0:T(8,128)S(1)}, u32[]{:S(2)}, u32[]{:S(2)}) collective-permute-start(f32[5,40,128]{2,1,0:T(8,128)S(1)} %get-tuple-element.57.refs_7_), channel_id=1, source_target_pairs={{0,1},{1,0},{2,3},{3,2},{4,5},{5,4},{6,7},{7,6},{8,9},{9,8},{10,11... | collective-permute-start | bytes 307208 | tf_op jit(solution)/shard_map/ppermute | solution.py:62
  24.0 4.6 %collective-permute-start.9 = (f32[5,40,128]{2,1,0:T(8,128)S(1)}, f32[5,40,128]{2,1,0:T(8,128)S(1)}, u32[]{:S(2)}, u32[]{:S(2)}) collective-permute-start(f32[5,40,128]{2,1,0:T(8,128)S(1)} %get-tuple-element.58.refs_8_), channel_id=1, source_target_pairs={{0,8},{1,2},{2,1},{3,4},{4,3},{5,6},{6,5},{7,15},{8,0},{9,10},{10,... | collective-permute-start | bytes 307208 | tf_op jit(solution)/shard_map/ppermute | solution.py:62
  29.0 6.6 %collective-permute-start.12 = (f32[5,40,128]{2,1,0:T(8,128)S(1)}, f32[5,40,128]{2,1,0:T(8,128)S(1)}, u32[]{:S(2)}, u32[]{:S(2)}) collective-permute-start(f32[5,40,128]{2,1,0:T(8,128)S(1)} %get-tuple-element.63.refs_7_), channel_id=1, source_target_pairs={{0,1},{1,0},{2,3},{3,2},{4,5},{5,4},{6,7},{7,6},{8,9},{9,8},{10,11... | collective-permute-start | bytes 307208 | tf_op jit(solution)/shard_map/ppermute | solution.py:62
  31.5 4.0 %collective-permute-start.13 = (f32[5,40,128]{2,1,0:T(8,128)S(1)}, f32[5,40,128]{2,1,0:T(8,128)S(1)}, u32[]{:S(2)}, u32[]{:S(2)}) collective-permute-start(f32[5,40,128]{2,1,0:T(8,128)S(1)} %get-tuple-element.64.refs_8_), channel_id=1, source_target_pairs={{0,8},{1,2},{2,1},{3,4},{4,3},{5,6},{6,5},{7,15},{8,0},{9,10},{10,... | collective-permute-start | bytes 307208 | tf_op jit(solution)/shard_map/ppermute | solution.py:62
  31.5 4.5 %collective-permute-start.14 = (f32[5,40,128]{2,1,0:T(8,128)S(1)}, f32[5,40,128]{2,1,0:T(8,128)S(1)}, u32[]{:S(2)}, u32[]{:S(2)}) collective-permute-start(f32[5,40,128]{2,1,0:T(8,128)S(1)} %get-tuple-element.65.refs_9_), channel_id=1, source_target_pairs={{0,24},{1,25},{2,26},{3,27},{4,28},{5,29},{6,30},{7,31},{8,16},{9,... | collective-permute-start | bytes 307208 | tf_op jit(solution)/shard_map/ppermute | solution.py:62
  32.7 3.4 %copy-start = (f32[8,1,32,128]{3,2,1,0:T(8,128)S(1)}, f32[8,1,32,128]{3,2,1,0:T(8,128)}, u32[]{:S(2)}) copy-start(f32[8,1,32,128]{3,2,1,0:T(8,128)} %param.22) | copy-start | bytes 393220
  32.7 3.4 %collective-permute-start.15 = (f32[5,40,128]{2,1,0:T(8,128)S(1)}, f32[5,40,128]{2,1,0:T(8,128)S(1)}, u32[]{:S(2)}, u32[]{:S(2)}) collective-permute-start(f32[5,40,128]{2,1,0:T(8,128)S(1)} %get-tuple-element.66.refs_10_), channel_id=1, source_target_pairs={{0,8},{1,9},{2,10},{3,11},{4,12},{5,13},{6,14},{7,15},{8,0},{9,1},... | collective-permute-start | bytes 307208 | tf_op jit(solution)/shard_map/ppermute | solution.py:62
  32.7 3.4 %copy-start.1 = (s32[1,32,128]{2,1,0:T(8,128)S(1)}, s32[1,32,128]{2,1,0:T(8,128)}, u32[]{:S(2)}) copy-start(s32[1,32,128]{2,1,0:T(8,128)} %param.20) | copy-start | bytes 49156
  32.7 3.4 %copy-start.2 = (s32[1,32,128]{2,1,0:T(8,128)S(1)}, s32[1,32,128]{2,1,0:T(8,128)}, u32[]{:S(2)}) copy-start(s32[1,32,128]{2,1,0:T(8,128)} %param.21) | copy-start | bytes 49156

commit v5 on v4

--- a/solution.py
+++ b/solution.py
@@ -345,7 +345,7 @@
     return high, (value - high.astype(jnp.float32)).astype(jnp.bfloat16)
 
 
-def pick_kernel(group, info, flux, inner, velocity, *refs):
+def pick_kernel(group, apart, info, flux, inner, velocity, *refs):
     arrived, (live, cells, base, weight) = refs[:4], refs[4:8]
     valve, payload, done, table, hits, next_hits, rows_even, rows_odd, sem = refs[8:]
     owners = cells.shape[0]
@@ -359,11 +359,12 @@
         table[v * BZ : (v + 1) * BZ, PLANES : 2 * PLANES] = low
     plane_at = lax.broadcasted_iota(jnp.int32, (PLANES, CAP), 0)
     row_at = lax.broadcasted_iota(jnp.int32, (8, CAP), 0)
-    steps = owners // group
+    unit = group + apart
+    steps = owners // unit
 
     def find(index, target):
         for k in range(group):
-            plane = lax.shift_right_logical(cells[pl.ds(index * group + k, 1), :], 7)
+            plane = lax.shift_right_logical(cells[pl.ds(index * unit + k, 1), :], 7)
             hit = jnp.where(plane_at == plane, 1.0, 0.0).astype(jnp.bfloat16)
             target[0:PLANES, k * CAP : (k + 1) * CAP] = hit
             target[PLANES:, k * CAP : (k + 1) * CAP] = hit
@@ -371,9 +372,17 @@
     def fetch(source, target):
         target[...] = jnp.dot(table[...], source[...], preferred_element_type=jnp.float32)
 
+    def send(owner, found):
+        keep = live[pl.ds(owner, 1), :] != 0.0
+        parts = [weight[corner, pl.ds(owner, 1), :] for corner in range(7)]
+        parts += [jnp.where(keep, jnp.sum(found[v], axis=0, keepdims=True), 0.0) for v in range(NVAR)]
+        parts += [base[pl.ds(owner, 1), :].astype(jnp.float32)]
+        for at, part in enumerate(parts):
+            payload[owner, :, at * CAP : (at + 1) * CAP] = part
+
     def put(index, rows):
         for k in range(group):
-            owner = index * group + k
+            owner = index * unit + k
             depth = jnp.bitwise_and(cells[pl.ds(owner, 1), :], BZ - 1)
             offset = jnp.broadcast_to(depth, (8, CAP)) - row_at
             found = [jnp.zeros((8, CAP), jnp.float32)] * NVAR
@@ -382,26 +391,40 @@
                 for v in range(NVAR):
                     row = rows[v * BZ + z : v * BZ + z + 8, k * CAP : (k + 1) * CAP]
                     found[v] = jnp.where(here, row, found[v])
-            parts = [weight[corner, pl.ds(owner, 1), :] for corner in range(7)]
-            parts += [jnp.where(live[pl.ds(owner, 1), :] != 0.0, jnp.sum(found[v], axis=0, keepdims=True), 0.0) for v in range(NVAR)]
-            parts += [base[pl.ds(owner, 1), :].astype(jnp.float32)]
-            for at, part in enumerate(parts):
-                payload[owner, :, at * CAP : (at + 1) * CAP] = part
+            send(owner, found)
+
+    def look_up(index):
+        for k in range(apart):
+            owner = index * unit + group + k
+            cell = jnp.broadcast_to(cells[pl.ds(owner, 1), :], (8, CAP))
+            depth = jnp.bitwise_and(cell, BZ - 1)
+            offset = lax.shift_right_logical(cell, 7) - row_at
+            found = [jnp.zeros((8, CAP), jnp.float32)] * NVAR
+            for p in range(0, PLANES, 8):
+                here = offset == p
+                for v in range(NVAR):
+                    row = jnp.take_along_axis(done[v, p : p + 8, :], depth, axis=1)
+                    found[v] = jnp.where(here, row, found[v])
+            send(owner, found)
 
     find(0, hits)
     fetch(hits, rows_even)
+    look_up(0)
     find(1, next_hits)
     fetch(next_hits, rows_odd)
     put(0, rows_even)
+    look_up(1)
 
     def step(pair, carry):
         one, two = 2 * pair, 2 * pair + 1
         find(one, hits)
         fetch(hits, rows_even)
         put(one - 1, rows_odd)
+        look_up(one)
         find(two, next_hits)
         fetch(next_hits, rows_odd)
         put(one, rows_even)
+        look_up(two)
         return carry
 
     lax.fori_loop(1, steps // 2, step, 0)
@@ -411,10 +434,10 @@
 
 def pick(info, flux, inner, velocity, arrived, live, cells, base, weight):
     owners = cells.shape[0]
-    group = 4 if owners % 8 == 0 else 1
+    group, apart = (12, 4) if owners % (2 * (12 + 4)) == 0 else (1, 0)
     slots = group * CAP
     return pl.pallas_call(
-        functools.partial(pick_kernel, group),
+        functools.partial(pick_kernel, group, apart),
         out_shape=[f32(NVAR, PLANES, BZ), f32(owners, 1, SEND_ROWS * CAP)],
         in_specs=[VMEM] * 12,
         out_specs=[HBM, VMEM],

time: 63.3 us -> 61.6 us (0.973)
  Pallas kernels: 28.9 us -> 27.3 us
    pallas_call x1, Pallas kernels: 4.31 us -> 2.69 us  [pick(): pl.pallas_call(functools.partial(pick_kernel, group, apart), out_shape=[f...]
where the time goes in v5:
time: 61.6 us; the launch traced here: 61.4 us
  Pallas kernels  27.3 us (44%)
  starting transfers between devices  16.5 us (27%)
  blocking collectives  12.9 us (21%)
  waiting for transfers between devices  3.64 us (6%)
  between operations  0.96 us (2%)
    ppermute x16, starting transfers between devices, exchange(): lax.ppermute(faces[k], ('bulk', 'valve'), plans[k])  16.5 us
    all_to_all x1, blocking collectives, body(): lax.all_to_all(payload, ('bulk', 'valve'), split_axis=0, concat_axis=0, t...  12.9 us
    pallas_call x1, Pallas kernels, scatter(): pl.pallas_call(functools.partial(scatter_kernel, group), out_shape=f32(NV...  9.57 us
    pallas_call x3, Pallas kernels, sweep_inner(): pl.pallas_call(sweep_kernel, out_shape=[f32(NVAR, PLANES, BZ)] * 2, in_sp...  8.18 us
    pallas_call x1, Pallas kernels, first_sweep(): pl.pallas_call(first_sweep_kernel, out_shape=[f32(NVAR, PLANES, BZ)] * 2...  4.19 us
    ppermute x16, waiting for transfers between devices, exchange(): lax.ppermute(faces[k], ('bulk', 'valve'), plans[k])  3.64 us
    pallas_call x1, Pallas kernels, pick(): pl.pallas_call(functools.partial(pick_kernel, group, apart), out_shape=[f...  2.69 us
    pallas_call x1, Pallas kernels, first_faces(): pl.pallas_call(first_kernel, out_shape=[f32(NVAR, FACE, BZ)] * 4 + [f32(N...  1.5 us
  transfers between devices with their start and end apart: 16, of which 3 were waited for; matrix products, arithmetic and copies ran while one was open for 0% of the time, Pallas kernels for 20%

profile of v5, /device:TPU:0, one launch (start us, length us, event | category | flops | bytes accessed | tf_op | source)
XLA Modules:
  0.0 61.4 jit_solution(2531025385104217378)
XLA Ops:
  0.7 0.1 stack.27
  0.8 0.1 broadcast_in_dim.4.info
  0.8 1.5 %first_faces.1 = (f32[5,40,128]{2,1,0:T(8,128)S(1)}, f32[5,40,128]{2,1,0:T(8,128)S(1)}, f32[5,40,128]{2,1,0:T(8,128)S(1)}, f32[5,40,128]{2,1,0:T(8,128)S(1)}, f3...) custom-call(s32[6,8,128]{2,1,0:T(8,128)S(1)} %broadcast_in_dim.4.info, f32[5,256,128]{2,1,0:T(8,128)} %bitcast.24, ...), custom_call_target="tpu_custom_call" | custom-call | tf_op jit(solution)/shard_map/first_faces/pallas_call | solution.py:179
  2.3 3.0 %collective-permute-start = (f32[5,40,128]{2,1,0:T(8,128)S(1)}, f32[5,40,128]{2,1,0:T(8,128)S(1)}, u32[]{:S(2)}, u32[]{:S(2)}) collective-permute-start(f32[5,40,128]{2,1,0:T(8,128)S(1)} %get-tuple-element.39.refs_6_), channel_id=1, source_target_pairs={{0,1},{1,0},{2,3},{3,2},{4,5},{5,4},{6,7},{7,6},{8,9},{9,8},{10,11... | collective-permute-start | bytes 307208 | tf_op jit(solution)/shard_map/ppermute | solution.py:62
  5.4 1.6 %collective-permute-start.2 = (f32[5,40,128]{2,1,0:T(8,128)S(1)}, f32[5,40,128]{2,1,0:T(8,128)S(1)}, u32[]{:S(2)}, u32[]{:S(2)}) collective-permute-start(f32[5,40,128]{2,1,0:T(8,128)S(1)} %get-tuple-element.41.refs_8_), channel_id=1, source_target_pairs={{0,24},{1,25},{2,26},{3,27},{4,28},{5,29},{6,30},{7,31},{8,16},{9,... | collective-permute-start | bytes 307208 | tf_op jit(solution)/shard_map/ppermute | solution.py:62
  7.0 4.2 %first_sweep.1 = (f32[5,256,128]{2,1,0:T(8,128)S(1)}, f32[5,256,128]{2,1,0:T(8,128)S(1)}, f32[3,256,128]{2,1,0:T(8,128)S(1)}, f32[5,256,128]{2,1,0:T(8,128)S(1)}...) custom-call(s32[6,8,128]{2,1,0:T(8,128)S(1)} %broadcast_in_dim.4.inf, ...), custom_call_target="tpu_custom_call" | custom-call | flops 15073280 | bytes 4849664 | tf_op jit(solution)/shard_map/first_sweep/pallas_call | solution.py:306
  11.2 0.4 next_faces.3
  11.6 3.1 %collective-permute-start.4 = (f32[5,40,128]{2,1,0:T(8,128)S(1)}, f32[5,40,128]{2,1,0:T(8,128)S(1)}, u32[]{:S(2)}, u32[]{:S(2)}) collective-permute-start(f32[5,40,128]{2,1,0:T(8,128)S(1)} %get-tuple-element.51.refs_7_), channel_id=1, source_target_pairs={{0,1},{1,0},{2,3},{3,2},{4,5},{5,4},{6,7},{7,6},{8,9},{9,8},{10,11... | collective-permute-start | bytes 307208 | tf_op jit(solution)/shard_map/ppermute | solution.py:62
  14.7 0.6 %collective-permute-start.6 = (f32[5,40,128]{2,1,0:T(8,128)S(1)}, f32[5,40,128]{2,1,0:T(8,128)S(1)}, u32[]{:S(2)}, u32[]{:S(2)}) collective-permute-start(f32[5,40,128]{2,1,0:T(8,128)S(1)} %get-tuple-element.53.refs_9_), channel_id=1, source_target_pairs={{0,24},{1,25},{2,26},{3,27},{4,28},{5,29},{6,30},{7,31},{8,16},{9,... | collective-permute-start | bytes 307208 | tf_op jit(solution)/shard_map/ppermute | solution.py:62
  15.4 2.7 %sweep_inner.3 = (f32[5,256,128]{2,1,0:T(8,128)S(1)}, f32[5,256,128]{2,1,0:T(8,128)S(1)}) custom-call(s32[6,8,128]{2,1,0:T(8,128)S(1)} %broadcast_in_dim.4.info, f32[75,8,128]{2,1,0:T(8,128)S(1)} %get-tuple-element.43.flux, f32[5,256,128]{2,1,0:T(8,128)S(1)} %get-tuple-element.44.bg.refs_0_, ...), custom_call_target="tpu_custom_call" | custom-call | flops 15073280 | bytes 4849664 | tf_op jit(solution)/shard_map/sweep_inner/pallas_call | solution.py:322
  18.1 1.2 %collective-permute-done.4.messages_0_ = f32[5,40,128]{2,1,0:T(8,128)S(1)} collective-permute-done((f32[5,40,128]{2,1,0:T(8,128)S(1)}, f32[5,40,128]{2,1,0:T(8,128)S(1)}, u32[]{:S(2)}, u32[]{:S(2)}) %collective-permute-start.4) | collective-permute-done | bytes 102432 | tf_op jit(solution)/shard_map/ppermute | solution.py:62
  19.3 0.4 next_faces.4
  19.6 0.7 %collective-permute-start.10 = (f32[5,40,128]{2,1,0:T(8,128)S(1)}, f32[5,40,128]{2,1,0:T(8,128)S(1)}, u32[]{:S(2)}, u32[]{:S(2)}) collective-permute-start(f32[5,40,128]{2,1,0:T(8,128)S(1)} %get-tuple-element.59.refs_9_), channel_id=1, source_target_pairs={{0,24},{1,25},{2,26},{3,27},{4,28},{5,29},{6,30},{7,31},{8,16},{9,... | collective-permute-start | bytes 307208 | tf_op jit(solution)/shard_map/ppermute | solution.py:62
  20.4 3.6 %collective-permute-start.8 = (f32[5,40,128]{2,1,0:T(8,128)S(1)}, f32[5,40,128]{2,1,0:T(8,128)S(1)}, u32[]{:S(2)}, u32[]{:S(2)}) collective-permute-start(f32[5,40,128]{2,1,0:T(8,128)S(1)} %get-tuple-element.57.refs_7_), channel_id=1, source_target_pairs={{0,1},{1,0},{2,3},{3,2},{4,5},{5,4},{6,7},{7,6},{8,9},{9,8},{10,11... | collective-permute-start | bytes 307208 | tf_op jit(solution)/shard_map/ppermute | solution.py:62
  24.0 2.7 %sweep_inner.4 = (f32[5,256,128]{2,1,0:T(8,128)S(1)}, f32[5,256,128]{2,1,0:T(8,128)S(1)}) custom-call(s32[6,8,128]{2,1,0:T(8,128)S(1)} %broadcast_in_dim.4.info, f32[75,8,128]{2,1,0:T(8,128)S(1)} %get-tuple-element.43.flux, f32[5,256,128]{2,1,0:T(8,128)S(1)} %get-tuple-element.55.bg.refs_0_, ...), custom_call_target="tpu_custom_call" | custom-call | flops 15073280 | bytes 4849664 | tf_op jit(solution)/shard_map/sweep_inner/pallas_call | solution.py:322
  26.7 1.9 %collective-permute-done.8.messages_0_ = f32[5,40,128]{2,1,0:T(8,128)S(1)} collective-permute-done((f32[5,40,128]{2,1,0:T(8,128)S(1)}, f32[5,40,128]{2,1,0:T(8,128)S(1)}, u32[]{:S(2)}, u32[]{:S(2)}) %collective-permute-start.8) | collective-permute-done | bytes 102432 | tf_op jit(solution)/shard_map/ppermute | solution.py:62
  28.6 0.4 next_faces.5
  29.0 2.5 %collective-permute-start.12 = (f32[5,40,128]{2,1,0:T(8,128)S(1)}, f32[5,40,128]{2,1,0:T(8,128)S(1)}, u32[]{:S(2)}, u32[]{:S(2)}) collective-permute-start(f32[5,40,128]{2,1,0:T(8,128)S(1)} %get-tuple-element.63.refs_7_), channel_id=1, source_target_pairs={{0,1},{1,0},{2,3},{3,2},{4,5},{5,4},{6,7},{7,6},{8,9},{9,8},{10,11... | collective-permute-start | bytes 307208 | tf_op jit(solution)/shard_map/ppermute | solution.py:62
  31.5 1.2 %collective-permute-start.14 = (f32[5,40,128]{2,1,0:T(8,128)S(1)}, f32[5,40,128]{2,1,0:T(8,128)S(1)}, u32[]{:S(2)}, u32[]{:S(2)}) collective-permute-start(f32[5,40,128]{2,1,0:T(8,128)S(1)} %get-tuple-element.65.refs_9_), channel_id=1, source_target_pairs={{0,24},{1,25},{2,26},{3,27},{4,28},{5,29},{6,30},{7,31},{8,16},{9,... | collective-permute-start | bytes 307208 | tf_op jit(solution)/shard_map/ppermute | solution.py:62
  32.7 2.8 %sweep_inner.5 = (f32[5,256,128]{2,1,0:T(8,128)S(1)}, f32[5,256,128]{2,1,0:T(8,128)S(1)}) custom-call(s32[6,8,128]{2,1,0:T(8,128)S(1)} %broadcast_in_dim.4.info, f32[75,8,128]{2,1,0:T(8,128)S(1)} %get-tuple-element.43.flux, f32[5,256,128]{2,1,0:T(8,128)S(1)} %get-tuple-element.61.bg.refs_0_, ...), custom_call_target="tpu_custom_call" | custom-call | flops 15073280 | bytes 4849664 | tf_op jit(solution)/shard_map/sweep_inner/pallas_call | solution.py:322
  35.6 0.5 collective-permute-done.14.refs_2_
  36.1 2.7 %pick.1 = (f32[5,256,128]{2,1,0:T(8,128)}, f32[32,1,1664]{2,1,0:T(1,128)S(1)}) custom-call(s32[6,8,128]{2,1,0:T(8,128)S(1)} %broadcast_in_dim.4.info, f32[75,8,128]{2,1,0:T(8,128)S(1)} %get-tuple-element.43.flux, f32[5,256,128]{2,1,0:T(8,128)S(1)} %get-tuple-element.68.inner, f32[3,256,128]{2,1,0:T(8,128)S(1)} %get-tuple-element.49.va_velocity.refs_5_.velocity, ...), custom_call_target="tpu_custom_call" | custom-call | tf_op jit(solution)/shard_map/pick/pallas_call | solution.py:439
  38.8 12.9 %all_to_all.5.refs_4_ = f32[32,1,1664]{2,1,0:T(1,128)S(1)} all-to-all(f32[32,1,1664]{2,1,0:T(1,128)S(1)} %get-tuple-element.70), channel_id=1, replica_groups=mesh['bulk'=4,'valve'=8] {'bulk','valve'}, dimensions={0} | all-to-all | bytes 425984 | tf_op jit(solution)/shard_map/all_to_all | solution.py:621
  51.7 9.6 %scatter.1 = f32[5,256,128]{2,1,0:T(8,128)} custom-call(s32[6,8,128]{2,1,0:T(8,128)S(1)} %broadcast_in_dim.4.info, f32[75,8,128]{2,1,0:T(8,128)S(1)} %get-tuple-element.43.flux, f32[5,256,128]{2,1,0:T(8,128)S(1)} %get-tuple-element.67.inner, f32[3,256,128]{2,1,0:T(8,128)S(1)} %get-tuple-element.45.bg_velocity.refs_1_.velocity, ...), custom_call_target="tpu_custom_call" | custom-call | tf_op jit(solution)/shard_map/scatter/pallas_call | solution.py:564
  (31 shorter events, 0.1 us)
Async XLA Ops:
  0.8 6.2 %copy-start.3 = (f32[3,5,5]{2,0,1:T(4,128)S(1)}, f32[3,5,5]{2,0,1:T(4,128)}, u32[]{:S(2)}) copy-start(f32[3,5,5]{2,0,1:T(4,128)} %param.19) | copy-start | bytes 904
  2.3 8.8 %collective-permute-start = (f32[5,40,128]{2,1,0:T(8,128)S(1)}, f32[5,40,128]{2,1,0:T(8,128)S(1)}, u32[]{:S(2)}, u32[]{:S(2)}) collective-permute-start(f32[5,40,128]{2,1,0:T(8,128)S(1)} %get-tuple-element.39.refs_6_), channel_id=1, source_target_pairs={{0,1},{1,0},{2,3},{3,2},{4,5},{5,4},{6,7},{7,6},{8,9},{9,8},{10,11... | collective-permute-start | bytes 307208 | tf_op jit(solution)/shard_map/ppermute | solution.py:62
  5.4 5.8 %collective-permute-start.1 = (f32[5,40,128]{2,1,0:T(8,128)S(1)}, f32[5,40,128]{2,1,0:T(8,128)S(1)}, u32[]{:S(2)}, u32[]{:S(2)}) collective-permute-start(f32[5,40,128]{2,1,0:T(8,128)S(1)} %get-tuple-element.40.refs_7_), channel_id=1, source_target_pairs={{0,8},{1,2},{2,1},{3,4},{4,3},{5,6},{6,5},{7,15},{8,0},{9,10},{10,... | collective-permute-start | bytes 307208 | tf_op jit(solution)/shard_map/ppermute | solution.py:62
  5.4 5.8 %collective-permute-start.2 = (f32[5,40,128]{2,1,0:T(8,128)S(1)}, f32[5,40,128]{2,1,0:T(8,128)S(1)}, u32[]{:S(2)}, u32[]{:S(2)}) collective-permute-start(f32[5,40,128]{2,1,0:T(8,128)S(1)} %get-tuple-element.41.refs_8_), channel_id=1, source_target_pairs={{0,24},{1,25},{2,26},{3,27},{4,28},{5,29},{6,30},{7,31},{8,16},{9,... | collective-permute-start | bytes 307208 | tf_op jit(solution)/shard_map/ppermute | solution.py:62
  7.0 4.2 %collective-permute-start.3 = (f32[5,40,128]{2,1,0:T(8,128)S(1)}, f32[5,40,128]{2,1,0:T(8,128)S(1)}, u32[]{:S(2)}, u32[]{:S(2)}) collective-permute-start(f32[5,40,128]{2,1,0:T(8,128)S(1)} %get-tuple-element.42.refs_9_), channel_id=1, source_target_pairs={{0,8},{1,9},{2,10},{3,11},{4,12},{5,13},{6,14},{7,15},{8,0},{9,1},... | collective-permute-start | bytes 307208 | tf_op jit(solution)/shard_map/ppermute | solution.py:62
  11.6 7.6 %collective-permute-start.4 = (f32[5,40,128]{2,1,0:T(8,128)S(1)}, f32[5,40,128]{2,1,0:T(8,128)S(1)}, u32[]{:S(2)}, u32[]{:S(2)}) collective-permute-start(f32[5,40,128]{2,1,0:T(8,128)S(1)} %get-tuple-element.51.refs_7_), channel_id=1, source_target_pairs={{0,1},{1,0},{2,3},{3,2},{4,5},{5,4},{6,7},{7,6},{8,9},{9,8},{10,11... | collective-permute-start | bytes 307208 | tf_op jit(solution)/shard_map/ppermute | solution.py:62
  14.7 4.5 %collective-permute-start.5 = (f32[5,40,128]{2,1,0:T(8,128)S(1)}, f32[5,40,128]{2,1,0:T(8,128)S(1)}, u32[]{:S(2)}, u32[]{:S(2)}) collective-permute-start(f32[5,40,128]{2,1,0:T(8,128)S(1)} %get-tuple-element.52.refs_8_), channel_id=1, source_target_pairs={{0,8},{1,2},{2,1},{3,4},{4,3},{5,6},{6,5},{7,15},{8,0},{9,10},{10,... | collective-permute-start | bytes 307208 | tf_op jit(solution)/shard_map/ppermute | solution.py:62
  14.7 4.5 %collective-permute-start.6 = (f32[5,40,128]{2,1,0:T(8,128)S(1)}, f32[5,40,128]{2,1,0:T(8,128)S(1)}, u32[]{:S(2)}, u32[]{:S(2)}) collective-permute-start(f32[5,40,128]{2,1,0:T(8,128)S(1)} %get-tuple-element.53.refs_9_), channel_id=1, source_target_pairs={{0,24},{1,25},{2,26},{3,27},{4,28},{5,29},{6,30},{7,31},{8,16},{9,... | collective-permute-start | bytes 307208 | tf_op jit(solution)/shard_map/ppermute | solution.py:62
  15.4 3.9 %collective-permute-start.7 = (f32[5,40,128]{2,1,0:T(8,128)S(1)}, f32[5,40,128]{2,1,0:T(8,128)S(1)}, u32[]{:S(2)}, u32[]{:S(2)}) collective-permute-start(f32[5,40,128]{2,1,0:T(8,128)S(1)} %get-tuple-element.54.refs_10_), channel_id=1, source_target_pairs={{0,8},{1,9},{2,10},{3,11},{4,12},{5,13},{6,14},{7,15},{8,0},{9,1},... | collective-permute-start | bytes 307208 | tf_op jit(solution)/shard_map/ppermute | solution.py:62
  19.6 7.0 %collective-permute-start.10 = (f32[5,40,128]{2,1,0:T(8,128)S(1)}, f32[5,40,128]{2,1,0:T(8,128)S(1)}, u32[]{:S(2)}, u32[]{:S(2)}) collective-permute-start(f32[5,40,128]{2,1,0:T(8,128)S(1)} %get-tuple-element.59.refs_9_), channel_id=1, source_target_pairs={{0,24},{1,25},{2,26},{3,27},{4,28},{5,29},{6,30},{7,31},{8,16},{9,... | collective-permute-start | bytes 307208 | tf_op jit(solution)/shard_map/ppermute | solution.py:62
  20.3 6.4 %collective-permute-start.11 = (f32[5,40,128]{2,1,0:T(8,128)S(1)}, f32[5,40,128]{2,1,0:T(8,128)S(1)}, u32[]{:S(2)}, u32[]{:S(2)}) collective-permute-start(f32[5,40,128]{2,1,0:T(8,128)S(1)} %get-tuple-element.60.refs_10_), channel_id=1, source_target_pairs={{0,8},{1,9},{2,10},{3,11},{4,12},{5,13},{6,14},{7,15},{8,0},{9,1},... | collective-permute-start | bytes 307208 | tf_op jit(solution)/shard_map/ppermute | solution.py:62
  20.4 8.3 %collective-permute-start.8 = (f32[5,40,128]{2,1,0:T(8,128)S(1)}, f32[5,40,128]{2,1,0:T(8,128)S(1)}, u32[]{:S(2)}, u32[]{:S(2)}) collective-permute-start(f32[5,40,128]{2,1,0:T(8,128)S(1)} %get-tuple-element.57.refs_7_), channel_id=1, source_target_pairs={{0,1},{1,0},{2,3},{3,2},{4,5},{5,4},{6,7},{7,6},{8,9},{9,8},{10,11... | collective-permute-start | bytes 307208 | tf_op jit(solution)/shard_map/ppermute | solution.py:62
  24.0 4.6 %collective-permute-start.9 = (f32[5,40,128]{2,1,0:T(8,128)S(1)}, f32[5,40,128]{2,1,0:T(8,128)S(1)}, u32[]{:S(2)}, u32[]{:S(2)}) collective-permute-start(f32[5,40,128]{2,1,0:T(8,128)S(1)} %get-tuple-element.58.refs_8_), channel_id=1, source_target_pairs={{0,8},{1,2},{2,1},{3,4},{4,3},{5,6},{6,5},{7,15},{8,0},{9,10},{10,... | collective-permute-start | bytes 307208 | tf_op jit(solution)/shard_map/ppermute | solution.py:62
  29.0 6.6 %collective-permute-start.12 = (f32[5,40,128]{2,1,0:T(8,128)S(1)}, f32[5,40,128]{2,1,0:T(8,128)S(1)}, u32[]{:S(2)}, u32[]{:S(2)}) collective-permute-start(f32[5,40,128]{2,1,0:T(8,128)S(1)} %get-tuple-element.63.refs_7_), channel_id=1, source_target_pairs={{0,1},{1,0},{2,3},{3,2},{4,5},{5,4},{6,7},{7,6},{8,9},{9,8},{10,11... | collective-permute-start | bytes 307208 | tf_op jit(solution)/shard_map/ppermute | solution.py:62
  31.5 4.0 %collective-permute-start.13 = (f32[5,40,128]{2,1,0:T(8,128)S(1)}, f32[5,40,128]{2,1,0:T(8,128)S(1)}, u32[]{:S(2)}, u32[]{:S(2)}) collective-permute-start(f32[5,40,128]{2,1,0:T(8,128)S(1)} %get-tuple-element.64.refs_8_), channel_id=1, source_target_pairs={{0,8},{1,2},{2,1},{3,4},{4,3},{5,6},{6,5},{7,15},{8,0},{9,10},{10,... | collective-permute-start | bytes 307208 | tf_op jit(solution)/shard_map/ppermute | solution.py:62
  31.5 4.5 %collective-permute-start.14 = (f32[5,40,128]{2,1,0:T(8,128)S(1)}, f32[5,40,128]{2,1,0:T(8,128)S(1)}, u32[]{:S(2)}, u32[]{:S(2)}) collective-permute-start(f32[5,40,128]{2,1,0:T(8,128)S(1)} %get-tuple-element.65.refs_9_), channel_id=1, source_target_pairs={{0,24},{1,25},{2,26},{3,27},{4,28},{5,29},{6,30},{7,31},{8,16},{9,... | collective-permute-start | bytes 307208 | tf_op jit(solution)/shard_map/ppermute | solution.py:62
  32.7 3.4 %copy-start = (f32[8,1,32,128]{3,2,1,0:T(8,128)S(1)}, f32[8,1,32,128]{3,2,1,0:T(8,128)}, u32[]{:S(2)}) copy-start(f32[8,1,32,128]{3,2,1,0:T(8,128)} %param.22) | copy-start | bytes 393220
  32.7 3.4 %collective-permute-start.15 = (f32[5,40,128]{2,1,0:T(8,128)S(1)}, f32[5,40,128]{2,1,0:T(8,128)S(1)}, u32[]{:S(2)}, u32[]{:S(2)}) collective-permute-start(f32[5,40,128]{2,1,0:T(8,128)S(1)} %get-tuple-element.66.refs_10_), channel_id=1, source_target_pairs={{0,8},{1,9},{2,10},{3,11},{4,12},{5,13},{6,14},{7,15},{8,0},{9,1},... | collective-permute-start | bytes 307208 | tf_op jit(solution)/shard_map/ppermute | solution.py:62
  32.7 3.4 %copy-start.1 = (s32[1,32,128]{2,1,0:T(8,128)S(1)}, s32[1,32,128]{2,1,0:T(8,128)}, u32[]{:S(2)}) copy-start(s32[1,32,128]{2,1,0:T(8,128)} %param.20) | copy-start | bytes 49156
  32.7 3.4 %copy-start.2 = (s32[1,32,128]{2,1,0:T(8,128)S(1)}, s32[1,32,128]{2,1,0:T(8,128)}, u32[]{:S(2)}) copy-start(s32[1,32,128]{2,1,0:T(8,128)} %param.21) | copy-start | bytes 49156

commit v6 on v5

--- a/solution.py
+++ b/solution.py
@@ -269,21 +269,22 @@
 
 
 def first_sweep_kernel(info, flux, bg, va, *refs):
-    fixed, count, messages, outs = refs[:5], refs[5], refs[6:10], refs[10:]
-    bg_out, va_out, here, wide, live = outs[0], outs[1], outs[2:7], outs[7], outs[8]
-    bg_padded, va_padded, count_here, sem = outs[9:]
-    copies = loads(list(zip(fixed, here)) + [(count, count_here)], sem)
+    bg_velocity, blanking, va_velocity, sources, count = refs[0], refs[1], refs[2], refs[3:5], refs[5]
+    messages, outs = refs[6:10], refs[10:]
+    bg_out, va_out, here, wide, live = outs[0], outs[1], outs[2:4], outs[4], outs[5]
+    bg_padded, va_padded, count_here, sem = outs[6:]
+    copies = loads(list(zip(sources, here)) + [(count, count_here)], sem)
     each(copies, "start")
     fill_padded(own_faces(info, 0, messages), bg, bg_padded)
     fill_padded(own_faces(info, 1, messages), va, va_padded)
-    each(copies[:3], "wait")
+    each(copies[:1], "wait")
     for d in range(3):
         for j in range(NVAR):
             for i in range(NVAR):
                 wide[(d * NVAR + j) * NVAR + i] = jnp.broadcast_to(flux[d, j : j + 1, i : i + 1], (8, BZ))
-    sweep(wide, bg_padded, here[0], here[1], here[2], bg_out)
-    each(copies[3:], "wait")
-    sweep(wide, va_padded, here[3], here[4], None, va_out)
+    sweep(wide, bg_padded, bg_velocity, here[0], blanking, bg_out)
+    each(copies[1:], "wait")
+    sweep(wide, va_padded, va_velocity, here[1], None, va_out)
     owners = count.shape[-1]
     counts = jnp.broadcast_to(count_here[0].astype(jnp.float32), (owners, owners))
     same = lax.broadcasted_iota(jnp.int32, (owners, owners), 0) == lax.broadcasted_iota(jnp.int32, (owners, owners), 1)
@@ -302,20 +303,20 @@
 
 
 def first_sweep(info, flux, bg, va, bg_fixed, va_fixed, count, messages):
-    fixed = (*bg_fixed, *va_fixed)
+    sources = (bg_fixed[1], va_fixed[1])
     outs = pl.pallas_call(
         first_sweep_kernel,
-        out_shape=[f32(NVAR, PLANES, BZ)] * 2 + [jax.ShapeDtypeStruct(x.shape, x.dtype) for x in fixed]
+        out_shape=[f32(NVAR, PLANES, BZ)] * 2 + [f32(NVAR, PLANES, BZ)] * 2
         + [f32(3 * NVAR * NVAR, 8, BZ), f32(count.shape[-1], CAP)],
-        in_specs=[VMEM] * 4 + [HBM] * 6 + [VMEM] * 4,
-        out_specs=[VMEM] * 9,
+        in_specs=[VMEM] * 7 + [HBM] * 3 + [VMEM] * 4,
+        out_specs=[VMEM] * 6,
         scratch_shapes=padded_scratch()
-        + [pltpu.VMEM(count.shape, jnp.int32), pltpu.SemaphoreType.DMA((sum(x.shape[0] for x in fixed) + 1,))],
+        + [pltpu.VMEM(count.shape, jnp.int32), pltpu.SemaphoreType.DMA((2 * NVAR + 1,))],
         compiler_params=params(8),
         cost_estimate=sweep_cost(),
         name="first_sweep",
-    )(info, flux, bg, va, *map(in_hbm, (*fixed, count)), *messages)
-    return outs[0], outs[1], tuple(outs[2:5]), tuple(outs[5:7]), outs[7], outs[8]
+    )(info, flux, bg, va, bg_fixed[0], bg_fixed[2], va_fixed[0], *map(in_hbm, (*sources, count)), *messages)
+    return outs[0], outs[1], (bg_fixed[0], outs[2], bg_fixed[2]), (va_fixed[0], outs[3]), outs[4], outs[5]
 
 
 def sweep_inner(info, flux, bg, va, messages):

time: 61.6 us -> 61.6 us (level)
  no operation moved by 1% of the time
where the time goes in v6:
time: 61.6 us; the launch traced here: 61.4 us
  Pallas kernels  27.3 us (44%)
  starting transfers between devices  16.5 us (27%)
  blocking collectives  12.9 us (21%)
  waiting for transfers between devices  3.51 us (6%)
  between operations  0.99 us (2%)
    ppermute x16, starting transfers between devices, exchange(): lax.ppermute(faces[k], ('bulk', 'valve'), plans[k])  16.5 us
    all_to_all x1, blocking collectives, body(): lax.all_to_all(payload, ('bulk', 'valve'), split_axis=0, concat_axis=0, t...  12.9 us
    pallas_call x1, Pallas kernels, scatter(): pl.pallas_call(functools.partial(scatter_kernel, group), out_shape=f32(NV...  9.59 us
    pallas_call x3, Pallas kernels, sweep_inner(): pl.pallas_call(sweep_kernel, out_shape=[f32(NVAR, PLANES, BZ)] * 2, in_sp...  8.31 us
    pallas_call x1, Pallas kernels, first_sweep(): pl.pallas_call(first_sweep_kernel, out_shape=[f32(NVAR, PLANES, BZ)] * 2...  4.02 us
    ppermute x16, waiting for transfers between devices, exchange(): lax.ppermute(faces[k], ('bulk', 'valve'), plans[k])  3.51 us
    pallas_call x1, Pallas kernels, pick(): pl.pallas_call(functools.partial(pick_kernel, group, apart), out_shape=[f...  2.7 us
    pallas_call x1, Pallas kernels, first_faces(): pl.pallas_call(first_kernel, out_shape=[f32(NVAR, FACE, BZ)] * 4 + [f32(N...  1.56 us
  transfers between devices with their start and end apart: 16, of which 3 were waited for; matrix products, arithmetic and copies ran while one was open for 0% of the time, Pallas kernels for 20%

profile of v6, /device:TPU:0, one launch (start us, length us, event | category | flops | bytes accessed | tf_op | source)
XLA Modules:
  0.0 61.4 jit_solution(46581515037605749)
XLA Ops:
  0.7 0.1 stack.27
  0.8 0.1 broadcast_in_dim.4.info
  0.9 1.6 %first_faces.1 = (f32[5,40,128]{2,1,0:T(8,128)S(1)}, f32[5,40,128]{2,1,0:T(8,128)S(1)}, f32[5,40,128]{2,1,0:T(8,128)S(1)}, f32[5,40,128]{2,1,0:T(8,128)S(1)}, f3...) custom-call(s32[6,8,128]{2,1,0:T(8,128)S(1)} %broadcast_in_dim.4.info, f32[5,256,128]{2,1,0:T(8,128)} %bitcast.48, ...), custom_call_target="tpu_custom_call" | custom-call | tf_op jit(solution)/shard_map/first_faces/pallas_call | solution.py:179
  2.4 3.0 %collective-permute-start = (f32[5,40,128]{2,1,0:T(8,128)S(1)}, f32[5,40,128]{2,1,0:T(8,128)S(1)}, u32[]{:S(2)}, u32[]{:S(2)}) collective-permute-start(f32[5,40,128]{2,1,0:T(8,128)S(1)} %get-tuple-element.36.refs_6_), channel_id=1, source_target_pairs={{0,1},{1,0},{2,3},{3,2},{4,5},{5,4},{6,7},{7,6},{8,9},{9,8},{10,11... | collective-permute-start | bytes 307208 | tf_op jit(solution)/shard_map/ppermute | solution.py:62
  5.5 1.6 %collective-permute-start.2 = (f32[5,40,128]{2,1,0:T(8,128)S(1)}, f32[5,40,128]{2,1,0:T(8,128)S(1)}, u32[]{:S(2)}, u32[]{:S(2)}) collective-permute-start(f32[5,40,128]{2,1,0:T(8,128)S(1)} %get-tuple-element.38.refs_8_), channel_id=1, source_target_pairs={{0,24},{1,25},{2,26},{3,27},{4,28},{5,29},{6,30},{7,31},{8,16},{9,... | collective-permute-start | bytes 307208 | tf_op jit(solution)/shard_map/ppermute | solution.py:62
  7.1 4.0 %first_sweep.1 = (f32[5,256,128]{2,1,0:T(8,128)S(1)}, f32[5,256,128]{2,1,0:T(8,128)S(1)}, f32[5,256,128]{2,1,0:T(8,128)S(1)}, f32[5,256,128]{2,1,0:T(8,128)S(1)}...) custom-call(s32[6,8,128]{2,1,0:T(8,128)S(1)} %broadcast_in_dim.4.info, f32[3,5,5]{2,1,0:T(8,128)S(1)} %copy.14.flux, ...), custom_call_target="tpu_custom_call" | custom-call | flops 15073280 | bytes 4849664 | tf_op jit(solution)/shard_map/first_sweep/pallas_call | solution.py:307
  11.2 0.4 next_faces.3
  11.6 3.1 %collective-permute-start.4 = (f32[5,40,128]{2,1,0:T(8,128)S(1)}, f32[5,40,128]{2,1,0:T(8,128)S(1)}, u32[]{:S(2)}, u32[]{:S(2)}) collective-permute-start(f32[5,40,128]{2,1,0:T(8,128)S(1)} %get-tuple-element.45.refs_7_), channel_id=1, source_target_pairs={{0,1},{1,0},{2,3},{3,2},{4,5},{5,4},{6,7},{7,6},{8,9},{9,8},{10,11... | collective-permute-start | bytes 307208 | tf_op jit(solution)/shard_map/ppermute | solution.py:62
  14.7 0.6 %collective-permute-start.6 = (f32[5,40,128]{2,1,0:T(8,128)S(1)}, f32[5,40,128]{2,1,0:T(8,128)S(1)}, u32[]{:S(2)}, u32[]{:S(2)}) collective-permute-start(f32[5,40,128]{2,1,0:T(8,128)S(1)} %get-tuple-element.47.refs_9_), channel_id=1, source_target_pairs={{0,24},{1,25},{2,26},{3,27},{4,28},{5,29},{6,30},{7,31},{8,16},{9,... | collective-permute-start | bytes 307208 | tf_op jit(solution)/shard_map/ppermute | solution.py:62
  15.3 2.7 %sweep_inner.3 = (f32[5,256,128]{2,1,0:T(8,128)S(1)}, f32[5,256,128]{2,1,0:T(8,128)S(1)}) custom-call(s32[6,8,128]{2,1,0:T(8,128)S(1)} %broadcast_in_dim.4.info, f32[75,8,128]{2,1,0:T(8,128)S(1)} %get-tuple-element.40.flux, f32[5,256,128]{2,1,0:T(8,128)S(1)} %get-tuple-element.41.bg.refs_0_, f32[3,256,128]{2,1,0:T(8,128)S(1)} %bitcast.29, ...), custom_call_target="tpu_custom_call" | custom-call | flops 15073280 | bytes 4849664 | tf_op jit(solution)/shard_map/sweep_inner/pallas_call | solution.py:323
  18.0 1.1 %collective-permute-done.4.messages_0_ = f32[5,40,128]{2,1,0:T(8,128)S(1)} collective-permute-done((f32[5,40,128]{2,1,0:T(8,128)S(1)}, f32[5,40,128]{2,1,0:T(8,128)S(1)}, u32[]{:S(2)}, u32[]{:S(2)}) %collective-permute-start.4) | collective-permute-done | bytes 102432 | tf_op jit(solution)/shard_map/ppermute | solution.py:62
  19.2 0.4 next_faces.4
  19.6 0.7 %collective-permute-start.10 = (f32[5,40,128]{2,1,0:T(8,128)S(1)}, f32[5,40,128]{2,1,0:T(8,128)S(1)}, u32[]{:S(2)}, u32[]{:S(2)}) collective-permute-start(f32[5,40,128]{2,1,0:T(8,128)S(1)} %get-tuple-element.53.refs_9_), channel_id=1, source_target_pairs={{0,24},{1,25},{2,26},{3,27},{4,28},{5,29},{6,30},{7,31},{8,16},{9,... | collective-permute-start | bytes 307208 | tf_op jit(solution)/shard_map/ppermute | solution.py:62
  20.3 3.6 %collective-permute-start.8 = (f32[5,40,128]{2,1,0:T(8,128)S(1)}, f32[5,40,128]{2,1,0:T(8,128)S(1)}, u32[]{:S(2)}, u32[]{:S(2)}) collective-permute-start(f32[5,40,128]{2,1,0:T(8,128)S(1)} %get-tuple-element.51.refs_7_), channel_id=1, source_target_pairs={{0,1},{1,0},{2,3},{3,2},{4,5},{5,4},{6,7},{7,6},{8,9},{9,8},{10,11... | collective-permute-start | bytes 307208 | tf_op jit(solution)/shard_map/ppermute | solution.py:62
  24.0 2.7 %sweep_inner.4 = (f32[5,256,128]{2,1,0:T(8,128)S(1)}, f32[5,256,128]{2,1,0:T(8,128)S(1)}) custom-call(s32[6,8,128]{2,1,0:T(8,128)S(1)} %broadcast_in_dim.4.info, f32[75,8,128]{2,1,0:T(8,128)S(1)} %get-tuple-element.40.flux, f32[5,256,128]{2,1,0:T(8,128)S(1)} %get-tuple-element.49.bg.refs_0_, f32[3,256,128]{2,1,0:T(8,128)S(1)} %bitcast.31, ...), custom_call_target="tpu_custom_call" | custom-call | flops 15073280 | bytes 4849664 | tf_op jit(solution)/shard_map/sweep_inner/pallas_call | solution.py:323
  26.7 1.9 %collective-permute-done.8.messages_0_ = f32[5,40,128]{2,1,0:T(8,128)S(1)} collective-permute-done((f32[5,40,128]{2,1,0:T(8,128)S(1)}, f32[5,40,128]{2,1,0:T(8,128)S(1)}, u32[]{:S(2)}, u32[]{:S(2)}) %collective-permute-start.8) | collective-permute-done | bytes 102432 | tf_op jit(solution)/shard_map/ppermute | solution.py:62
  28.6 0.4 next_faces.5
  29.0 2.5 %collective-permute-start.12 = (f32[5,40,128]{2,1,0:T(8,128)S(1)}, f32[5,40,128]{2,1,0:T(8,128)S(1)}, u32[]{:S(2)}, u32[]{:S(2)}) collective-permute-start(f32[5,40,128]{2,1,0:T(8,128)S(1)} %get-tuple-element.57.refs_7_), channel_id=1, source_target_pairs={{0,1},{1,0},{2,3},{3,2},{4,5},{5,4},{6,7},{7,6},{8,9},{9,8},{10,11... | collective-permute-start | bytes 307208 | tf_op jit(solution)/shard_map/ppermute | solution.py:62
  31.5 1.2 %collective-permute-start.14 = (f32[5,40,128]{2,1,0:T(8,128)S(1)}, f32[5,40,128]{2,1,0:T(8,128)S(1)}, u32[]{:S(2)}, u32[]{:S(2)}) collective-permute-start(f32[5,40,128]{2,1,0:T(8,128)S(1)} %get-tuple-element.59.refs_9_), channel_id=1, source_target_pairs={{0,24},{1,25},{2,26},{3,27},{4,28},{5,29},{6,30},{7,31},{8,16},{9,... | collective-permute-start | bytes 307208 | tf_op jit(solution)/shard_map/ppermute | solution.py:62
  32.7 2.9 %sweep_inner.5 = (f32[5,256,128]{2,1,0:T(8,128)S(1)}, f32[5,256,128]{2,1,0:T(8,128)S(1)}) custom-call(s32[6,8,128]{2,1,0:T(8,128)S(1)} %broadcast_in_dim.4.info, f32[75,8,128]{2,1,0:T(8,128)S(1)} %get-tuple-element.40.flux, f32[5,256,128]{2,1,0:T(8,128)S(1)} %get-tuple-element.55.bg.refs_0_, f32[3,256,128]{2,1,0:T(8,128)S(1)} %bitcast.33, ...), custom_call_target="tpu_custom_call" | custom-call | flops 15073280 | bytes 4849664 | tf_op jit(solution)/shard_map/sweep_inner/pallas_call | solution.py:323
  35.6 0.4 collective-permute-done.14.refs_2_
  36.1 2.7 %pick.1 = (f32[5,256,128]{2,1,0:T(8,128)}, f32[32,1,1664]{2,1,0:T(1,128)S(1)}) custom-call(s32[6,8,128]{2,1,0:T(8,128)S(1)} %broadcast_in_dim.4.info, f32[75,8,128]{2,1,0:T(8,128)S(1)} %get-tuple-element.40.flux, f32[5,256,128]{2,1,0:T(8,128)S(1)} %get-tuple-element.62.inner, f32[3,256,128]{2,1,0:T(8,128)S(1)} %bitcast.26, ...), custom_call_target="tpu_custom_call" | custom-call | tf_op jit(solution)/shard_map/pick/pallas_call | solution.py:440
  38.8 12.9 %all_to_all.5.refs_4_ = f32[32,1,1664]{2,1,0:T(1,128)S(1)} all-to-all(f32[32,1,1664]{2,1,0:T(1,128)S(1)} %get-tuple-element.64), channel_id=1, replica_groups=mesh['bulk'=4,'valve'=8] {'bulk','valve'}, dimensions={0} | all-to-all | bytes 425984 | tf_op jit(solution)/shard_map/all_to_all | solution.py:622
  51.7 9.6 %scatter.1 = f32[5,256,128]{2,1,0:T(8,128)} custom-call(s32[6,8,128]{2,1,0:T(8,128)S(1)} %broadcast_in_dim.4.info, f32[75,8,128]{2,1,0:T(8,128)S(1)} %get-tuple-element.40.flux, f32[5,256,128]{2,1,0:T(8,128)S(1)} %get-tuple-element.61.inner, f32[3,256,128]{2,1,0:T(8,128)S(1)} %bitcast.34, s32[1,256,128]{2,1,0:T(8,128)S(1)} %bitcast.42, ...), custom_call_target="tpu_custom_call" | custom-call | tf_op jit(solution)/shard_map/scatter/pallas_call | solution.py:565
  (37 shorter events, 0.1 us)
Async XLA Ops:
  0.8 6.2 %copy-start.6 = (f32[3,5,5]{2,0,1:T(4,128)S(1)}, f32[3,5,5]{2,0,1:T(4,128)}, u32[]{:S(2)}) copy-start(f32[3,5,5]{2,0,1:T(4,128)} %param.19) | copy-start | bytes 904
  0.8 6.2 %copy-start = (f32[3,8,32,128]{3,2,1,0:T(8,128)S(1)}, f32[3,8,32,128]{3,2,1,0:T(8,128)}, u32[]{:S(2)}) copy-start(f32[3,8,32,128]{3,2,1,0:T(8,128)} %param.17) | copy-start | bytes 1179652
  0.8 6.2 %copy-start.1 = (f32[3,8,32,128]{3,2,1,0:T(8,128)S(1)}, f32[3,8,32,128]{3,2,1,0:T(8,128)}, u32[]{:S(2)}) copy-start(f32[3,8,32,128]{3,2,1,0:T(8,128)} %param.13) | copy-start | bytes 1179652
  0.8 6.3 %copy-start.2 = (s32[8,32,128]{2,1,0:T(8,128)S(1)}, s32[8,32,128]{2,1,0:T(8,128)}, u32[]{:S(2)}) copy-start(s32[8,32,128]{2,1,0:T(8,128)} %param.15) | copy-start | bytes 393220
  2.4 8.7 %collective-permute-start = (f32[5,40,128]{2,1,0:T(8,128)S(1)}, f32[5,40,128]{2,1,0:T(8,128)S(1)}, u32[]{:S(2)}, u32[]{:S(2)}) collective-permute-start(f32[5,40,128]{2,1,0:T(8,128)S(1)} %get-tuple-element.36.refs_6_), channel_id=1, source_target_pairs={{0,1},{1,0},{2,3},{3,2},{4,5},{5,4},{6,7},{7,6},{8,9},{9,8},{10,11... | collective-permute-start | bytes 307208 | tf_op jit(solution)/shard_map/ppermute | solution.py:62
  5.5 5.7 %collective-permute-start.1 = (f32[5,40,128]{2,1,0:T(8,128)S(1)}, f32[5,40,128]{2,1,0:T(8,128)S(1)}, u32[]{:S(2)}, u32[]{:S(2)}) collective-permute-start(f32[5,40,128]{2,1,0:T(8,128)S(1)} %get-tuple-element.37.refs_7_), channel_id=1, source_target_pairs={{0,8},{1,2},{2,1},{3,4},{4,3},{5,6},{6,5},{7,15},{8,0},{9,10},{10,... | collective-permute-start | bytes 307208 | tf_op jit(solution)/shard_map/ppermute | solution.py:62
  5.5 5.7 %collective-permute-start.2 = (f32[5,40,128]{2,1,0:T(8,128)S(1)}, f32[5,40,128]{2,1,0:T(8,128)S(1)}, u32[]{:S(2)}, u32[]{:S(2)}) collective-permute-start(f32[5,40,128]{2,1,0:T(8,128)S(1)} %get-tuple-element.38.refs_8_), channel_id=1, source_target_pairs={{0,24},{1,25},{2,26},{3,27},{4,28},{5,29},{6,30},{7,31},{8,16},{9,... | collective-permute-start | bytes 307208 | tf_op jit(solution)/shard_map/ppermute | solution.py:62
  7.1 4.1 %collective-permute-start.3 = (f32[5,40,128]{2,1,0:T(8,128)S(1)}, f32[5,40,128]{2,1,0:T(8,128)S(1)}, u32[]{:S(2)}, u32[]{:S(2)}) collective-permute-start(f32[5,40,128]{2,1,0:T(8,128)S(1)} %get-tuple-element.39.refs_9_), channel_id=1, source_target_pairs={{0,8},{1,9},{2,10},{3,11},{4,12},{5,13},{6,14},{7,15},{8,0},{9,1},... | collective-permute-start | bytes 307208 | tf_op jit(solution)/shard_map/ppermute | solution.py:62
  11.6 7.6 %collective-permute-start.4 = (f32[5,40,128]{2,1,0:T(8,128)S(1)}, f32[5,40,128]{2,1,0:T(8,128)S(1)}, u32[]{:S(2)}, u32[]{:S(2)}) collective-permute-start(f32[5,40,128]{2,1,0:T(8,128)S(1)} %get-tuple-element.45.refs_7_), channel_id=1, source_target_pairs={{0,1},{1,0},{2,3},{3,2},{4,5},{5,4},{6,7},{7,6},{8,9},{9,8},{10,11... | collective-permute-start | bytes 307208 | tf_op jit(solution)/shard_map/ppermute | solution.py:62
  14.7 4.5 %collective-permute-start.5 = (f32[5,40,128]{2,1,0:T(8,128)S(1)}, f32[5,40,128]{2,1,0:T(8,128)S(1)}, u32[]{:S(2)}, u32[]{:S(2)}) collective-permute-start(f32[5,40,128]{2,1,0:T(8,128)S(1)} %get-tuple-element.46.refs_8_), channel_id=1, source_target_pairs={{0,8},{1,2},{2,1},{3,4},{4,3},{5,6},{6,5},{7,15},{8,0},{9,10},{10,... | collective-permute-start | bytes 307208 | tf_op jit(solution)/shard_map/ppermute | solution.py:62
  14.7 4.5 %collective-permute-start.6 = (f32[5,40,128]{2,1,0:T(8,128)S(1)}, f32[5,40,128]{2,1,0:T(8,128)S(1)}, u32[]{:S(2)}, u32[]{:S(2)}) collective-permute-start(f32[5,40,128]{2,1,0:T(8,128)S(1)} %get-tuple-element.47.refs_9_), channel_id=1, source_target_pairs={{0,24},{1,25},{2,26},{3,27},{4,28},{5,29},{6,30},{7,31},{8,16},{9,... | collective-permute-start | bytes 307208 | tf_op jit(solution)/shard_map/ppermute | solution.py:62
  15.3 3.9 %collective-permute-start.7 = (f32[5,40,128]{2,1,0:T(8,128)S(1)}, f32[5,40,128]{2,1,0:T(8,128)S(1)}, u32[]{:S(2)}, u32[]{:S(2)}) collective-permute-start(f32[5,40,128]{2,1,0:T(8,128)S(1)} %get-tuple-element.48.refs_10_), channel_id=1, source_target_pairs={{0,8},{1,9},{2,10},{3,11},{4,12},{5,13},{6,14},{7,15},{8,0},{9,1},... | collective-permute-start | bytes 307208 | tf_op jit(solution)/shard_map/ppermute | solution.py:62
  19.6 7.1 %collective-permute-start.10 = (f32[5,40,128]{2,1,0:T(8,128)S(1)}, f32[5,40,128]{2,1,0:T(8,128)S(1)}, u32[]{:S(2)}, u32[]{:S(2)}) collective-permute-start(f32[5,40,128]{2,1,0:T(8,128)S(1)} %get-tuple-element.53.refs_9_), channel_id=1, source_target_pairs={{0,24},{1,25},{2,26},{3,27},{4,28},{5,29},{6,30},{7,31},{8,16},{9,... | collective-permute-start | bytes 307208 | tf_op jit(solution)/shard_map/ppermute | solution.py:62
  20.3 6.4 %collective-permute-start.11 = (f32[5,40,128]{2,1,0:T(8,128)S(1)}, f32[5,40,128]{2,1,0:T(8,128)S(1)}, u32[]{:S(2)}, u32[]{:S(2)}) collective-permute-start(f32[5,40,128]{2,1,0:T(8,128)S(1)} %get-tuple-element.54.refs_10_), channel_id=1, source_target_pairs={{0,8},{1,9},{2,10},{3,11},{4,12},{5,13},{6,14},{7,15},{8,0},{9,1},... | collective-permute-start | bytes 307208 | tf_op jit(solution)/shard_map/ppermute | solution.py:62
  20.3 8.3 %collective-permute-start.8 = (f32[5,40,128]{2,1,0:T(8,128)S(1)}, f32[5,40,128]{2,1,0:T(8,128)S(1)}, u32[]{:S(2)}, u32[]{:S(2)}) collective-permute-start(f32[5,40,128]{2,1,0:T(8,128)S(1)} %get-tuple-element.51.refs_7_), channel_id=1, source_target_pairs={{0,1},{1,0},{2,3},{3,2},{4,5},{5,4},{6,7},{7,6},{8,9},{9,8},{10,11... | collective-permute-start | bytes 307208 | tf_op jit(solution)/shard_map/ppermute | solution.py:62
  24.0 4.6 %collective-permute-start.9 = (f32[5,40,128]{2,1,0:T(8,128)S(1)}, f32[5,40,128]{2,1,0:T(8,128)S(1)}, u32[]{:S(2)}, u32[]{:S(2)}) collective-permute-start(f32[5,40,128]{2,1,0:T(8,128)S(1)} %get-tuple-element.52.refs_8_), channel_id=1, source_target_pairs={{0,8},{1,2},{2,1},{3,4},{4,3},{5,6},{6,5},{7,15},{8,0},{9,10},{10,... | collective-permute-start | bytes 307208 | tf_op jit(solution)/shard_map/ppermute | solution.py:62
  29.0 6.6 %collective-permute-start.12 = (f32[5,40,128]{2,1,0:T(8,128)S(1)}, f32[5,40,128]{2,1,0:T(8,128)S(1)}, u32[]{:S(2)}, u32[]{:S(2)}) collective-permute-start(f32[5,40,128]{2,1,0:T(8,128)S(1)} %get-tuple-element.57.refs_7_), channel_id=1, source_target_pairs={{0,1},{1,0},{2,3},{3,2},{4,5},{5,4},{6,7},{7,6},{8,9},{9,8},{10,11... | collective-permute-start | bytes 307208 | tf_op jit(solution)/shard_map/ppermute | solution.py:62
  31.5 4.1 %collective-permute-start.13 = (f32[5,40,128]{2,1,0:T(8,128)S(1)}, f32[5,40,128]{2,1,0:T(8,128)S(1)}, u32[]{:S(2)}, u32[]{:S(2)}) collective-permute-start(f32[5,40,128]{2,1,0:T(8,128)S(1)} %get-tuple-element.58.refs_8_), channel_id=1, source_target_pairs={{0,8},{1,2},{2,1},{3,4},{4,3},{5,6},{6,5},{7,15},{8,0},{9,10},{10,... | collective-permute-start | bytes 307208 | tf_op jit(solution)/shard_map/ppermute | solution.py:62
  31.5 4.5 %collective-permute-start.14 = (f32[5,40,128]{2,1,0:T(8,128)S(1)}, f32[5,40,128]{2,1,0:T(8,128)S(1)}, u32[]{:S(2)}, u32[]{:S(2)}) collective-permute-start(f32[5,40,128]{2,1,0:T(8,128)S(1)} %get-tuple-element.59.refs_9_), channel_id=1, source_target_pairs={{0,24},{1,25},{2,26},{3,27},{4,28},{5,29},{6,30},{7,31},{8,16},{9,... | collective-permute-start | bytes 307208 | tf_op jit(solution)/shard_map/ppermute | solution.py:62
  32.7 3.4 %copy-start.3 = (f32[8,1,32,128]{3,2,1,0:T(8,128)S(1)}, f32[8,1,32,128]{3,2,1,0:T(8,128)}, u32[]{:S(2)}) copy-start(f32[8,1,32,128]{3,2,1,0:T(8,128)} %param.22) | copy-start | bytes 393220
  32.7 3.4 %collective-permute-start.15 = (f32[5,40,128]{2,1,0:T(8,128)S(1)}, f32[5,40,128]{2,1,0:T(8,128)S(1)}, u32[]{:S(2)}, u32[]{:S(2)}) collective-permute-start(f32[5,40,128]{2,1,0:T(8,128)S(1)} %get-tuple-element.60.refs_10_), channel_id=1, source_target_pairs={{0,8},{1,9},{2,10},{3,11},{4,12},{5,13},{6,14},{7,15},{8,0},{9,1},... | collective-permute-start | bytes 307208 | tf_op jit(solution)/shard_map/ppermute | solution.py:62
  32.7 3.4 %copy-start.4 = (s32[1,32,128]{2,1,0:T(8,128)S(1)}, s32[1,32,128]{2,1,0:T(8,128)}, u32[]{:S(2)}) copy-start(s32[1,32,128]{2,1,0:T(8,128)} %param.20) | copy-start | bytes 49156
  32.7 3.4 %copy-start.5 = (s32[1,32,128]{2,1,0:T(8,128)S(1)}, s32[1,32,128]{2,1,0:T(8,128)}, u32[]{:S(2)}) copy-start(s32[1,32,128]{2,1,0:T(8,128)} %param.21) | copy-start | bytes 49156
